TPU v7x, 256 devices: a whole 4x4x8 slice. The times are simulated.
256 devices in a mesh: lon: 32 (over y_lo, z, core), lat: 8 (over x, y_hi).
Axes of the slice: x: 4, y: 4 (y_hi: 2, y_lo: 2; y = y_hi * 2 + y_lo), z: 8, core: 2. Of those that a mesh axis runs over, the one named last changes fastest.
Arguments:
- tokens: bfloat16 [2, 192, 73728], P(None, 'lat', 'lon'), may hold values from -8 to 8
- fine_attend: bfloat16 [192, 576], replicated, may hold values from -0.4375 to 0.4375
- fine_project: bfloat16 [192, 192], replicated, may hold values from -0.4375 to 0.4375
- fine_gain_one: float32 [192], replicated, may hold values from 0.25 to 1.75
- fine_expand: bfloat16 [192, 768], replicated, may hold values from -0.4375 to 0.4375
- fine_reduce: bfloat16 [768, 192], replicated, may hold values from -0.21875 to 0.21875
- fine_gain_two: float32 [192], replicated, may hold values from 0.25 to 1.75
- fine_bias: float32 [32, 6, 23, 144], P('lat'), may hold values from -4 to 260
- merge_gain: float32 [768], replicated, may hold values from 0.25 to 1.75
- merge_weight: bfloat16 [768, 384], replicated, may hold values from -0.21875 to 0.21875
- coarse_attend: bfloat16 [384, 1152], replicated, may hold values from -0.3125 to 0.3125
- coarse_project: bfloat16 [384, 384], replicated, may hold values from -0.3125 to 0.3125
- coarse_gain_one: float32 [384], replicated, may hold values from 0.25 to 1.75
- coarse_expand: bfloat16 [384, 1536], replicated, may hold values from -0.3125 to 0.3125
- coarse_reduce: bfloat16 [1536, 384], replicated, may hold values from -0.15625 to 0.15625
- coarse_gain_two: float32 [384], replicated, may hold values from 0.25 to 1.75
- coarse_bias: float32 [16, 12, 23, 144], P('lat'), may hold values from -4 to 260
- cotangent: bfloat16 [2, 96, 73728], P(None, 'lat', 'lon'), may hold values from -6 to 6
Outputs:
- coarse_out: bfloat16 [2, 96, 73728], P(None, 'lat', 'lon')
- grad_tokens: bfloat16 [2, 192, 73728], P(None, 'lat', 'lon')
- grad_fine_bias: float32 [32, 6, 23, 144], P('lat')
- grad_coarse_bias: float32 [16, 12, 23, 144], P('lat')
All inputs are finite; a program needn't handle non-finite values.
Results may differ from a plain program's by a relative error of at most 0.034.
Values may be sent and summed in bfloat16 or wider, within the bound.
No kernel may reach another device: no remote copies, remote signals or barrier semaphores. Data moves between devices by JAX's collectives and lax.ppermute only.
A program may use at most 256 MiB of HBM per device.

v0:
```python
import math

import jax
import jax.numpy as jnp
from jax import lax
from jax.sharding import PartitionSpec as P

C1 = 192
C2 = 384
HD = 32
NZ = 2
WZ = 2
WLAT = 6
WLON = 12


EPSILON = 1e-05
MASKED = -1000000000.0


def shifted_2(value, axis, steps):
    count = lax.axis_size(axis)
    pairs = [(source, (source + steps) % count) for source in range(count)]
    return lax.ppermute(value, axis, pairs)


def swapped_2(value, axis, distance):
    mask = 2**distance
    pairs = [(source, source ^ mask) for source in range(lax.axis_size(axis))]
    return lax.ppermute(value, axis, pairs)


def layer_norm(values):
    average = jnp.mean(values, axis=-1, keepdims=True)
    centred = values - average
    variance = jnp.mean(centred * centred, axis=-1, keepdims=True)
    return centred * lax.rsqrt(variance + EPSILON)


def offset_onehot():
    position = jnp.arange(WLON, dtype=jnp.int32)
    offset_index = position[:, None] - position[None, :] + (WLON - 1)
    offsets = jnp.arange(2 * WLON - 1, dtype=jnp.int32)
    return (offset_index[None, :, :] == offsets[:, None, None]).astype(jnp.float32)


def build_bias(bias_table):
    groups, head_count = (bias_table.shape[0], bias_table.shape[1])
    plane_cells = WZ * WLAT
    shaped = bias_table.reshape(groups, head_count, 2 * WLON - 1, plane_cells, plane_cells)
    spread = jnp.einsum(
        "ghdab,dpq->ghapbq", shaped, offset_onehot(), precision=lax.Precision.HIGHEST
    )
    return spread.reshape(groups, head_count, plane_cells * WLON, plane_cells * WLON)


def region(position, extent, window):
    return (position >= extent - window).astype(jnp.int32) + (
        position >= extent - window // 2
    ).astype(jnp.int32)


def pair_allowed(lat_windows, level_windows, row_start, lat_total):
    token_index = jnp.arange(WZ * WLAT * WLON, dtype=jnp.int32)
    level_in = token_index // (WLAT * WLON)
    row_in = token_index // WLON % WLAT
    level_pos = jnp.arange(level_windows, dtype=jnp.int32)[:, None] * WZ + level_in[None, :]
    row_pos = row_start + jnp.arange(lat_windows, dtype=jnp.int32)[:, None] * WLAT + row_in[None, :]
    region_code = (
        region(level_pos, NZ, WZ)[None, :, :] * 3 + region(row_pos, lat_total, WLAT)[:, None, :]
    )
    return region_code[..., :, None] == region_code[..., None, :]


def project(tokens_in, weight):
    return jnp.dot(tokens_in, weight, preferred_element_type=jnp.float32).astype(jnp.bfloat16)


def to_heads(block_data, head_count):
    shaped = lax.optimization_barrier(block_data).astype(jnp.float32)
    shaped = shaped.reshape(block_data.shape[:-1] + (head_count, HD))
    return jnp.swapaxes(shaped, -2, -3)


def split_qkv(packed, head_count):
    block_width = packed.shape[-1] // 3
    return (
        to_heads(packed[..., :block_width], head_count),
        to_heads(packed[..., block_width : 2 * block_width], head_count),
        to_heads(packed[..., 2 * block_width :], head_count),
    )


def attend(query_heads, key_heads, value_heads, bias_full, allowed):
    scores = jnp.einsum(
        "gwhqd,gwhkd->gwhqk", query_heads, key_heads, precision=lax.Precision.HIGHEST
    )
    scores = scores / math.sqrt(HD) + bias_full[:, None]
    scores = jnp.where(allowed[:, None, None], scores, MASKED)
    softmaxed = jax.nn.softmax(scores, axis=-1).astype(jnp.bfloat16)
    mixture = jnp.einsum(
        "gwhqk,gwhkd->gwqhd",
        lax.optimization_barrier(softmaxed).astype(jnp.float32),
        value_heads,
        precision=lax.Precision.HIGHEST,
    )
    return mixture.reshape(mixture.shape[:3] + (-1,)).astype(jnp.bfloat16)


def block_tail(tokens_in, head_out, level_weights):
    w_project, gain_attend, w_expand, w_reduce, gain_mixer = level_weights[1:]
    attention = jnp.dot(head_out, w_project, preferred_element_type=jnp.float32)
    middle = (tokens_in.astype(jnp.float32) + gain_attend * layer_norm(attention)).astype(
        jnp.bfloat16
    )
    expanded = jnp.dot(middle, w_expand, preferred_element_type=jnp.float32)
    activated = jax.nn.gelu(expanded, approximate=False).astype(jnp.bfloat16)
    reduced = jnp.dot(activated, w_reduce, preferred_element_type=jnp.float32)
    middle_wide = lax.optimization_barrier(middle).astype(jnp.float32)
    return (middle_wide + gain_mixer * layer_norm(reduced)).astype(jnp.bfloat16)


def window_block(tokens_in, bias_table, allowed, level_weights):
    head_count = bias_table.shape[1]
    query_heads, key_heads, value_heads = split_qkv(
        project(tokens_in, level_weights[0]), head_count
    )
    head_out = attend(query_heads, key_heads, value_heads, build_bias(bias_table), allowed)
    return block_tail(tokens_in, head_out, level_weights)


def windows_of(cell_grid):
    levels, row_count, col_count, channels = cell_grid.shape
    shaped = cell_grid.reshape(
        levels // WZ, WZ, row_count // WLAT, WLAT, col_count // WLON, WLON, channels
    )
    shaped = shaped.transpose(2, 0, 4, 1, 3, 5, 6)
    return shaped.reshape(
        row_count // WLAT, levels // WZ, col_count // WLON, WZ * WLAT * WLON, channels
    )


def grid_of(windows, levels, row_count, col_count):
    channels = windows.shape[-1]
    shaped = windows.reshape(
        row_count // WLAT, levels // WZ, col_count // WLON, WZ, WLAT, WLON, channels
    )
    return shaped.transpose(1, 3, 0, 4, 2, 5, 6).reshape(levels, row_count, col_count, channels)


def merge_level(fine_grid, norm_gain, weight):
    levels, row_count, col_count, channels = fine_grid.shape
    quadrants = fine_grid.reshape(levels, row_count // 2, 2, col_count // 2, 2, channels)
    quadrants = quadrants.transpose(0, 1, 3, 2, 4, 5).reshape(
        levels, row_count // 2, col_count // 2, 4 * channels
    )
    normed = (norm_gain * layer_norm(quadrants.astype(jnp.float32))).astype(jnp.bfloat16)
    return jnp.dot(normed, weight, preferred_element_type=jnp.float32).astype(jnp.bfloat16)


def lon_step(strip_data, offset):
    return shifted_2(strip_data, "lon", offset)


def lat_step(strip_data, offset):
    return shifted_2(strip_data, "lat", offset)


def to_frame(tokens_in):
    levels, row_count, row_width = tokens_in.shape
    half_width = row_width // 2
    col_strip = lon_step(tokens_in[:, :, :half_width], -1)
    shifted = jnp.concatenate([tokens_in[:, :, half_width:], col_strip], axis=2)
    row_strip = lat_step(shifted[:, : WLAT // 2, :], -1)
    shifted = jnp.concatenate([shifted[:, WLAT // 2 :, :], row_strip], axis=1)
    return jnp.roll(shifted, -1, axis=0)


def from_frame(tokens_in):
    levels, row_count, row_width = tokens_in.shape
    half_width = row_width // 2
    rolled = jnp.roll(tokens_in, 1, axis=0)
    row_strip = lat_step(rolled[:, row_count - WLAT // 2 :, :], 1)
    rolled = jnp.concatenate([row_strip, rolled[:, : row_count - WLAT // 2, :]], axis=1)
    col_strip = lon_step(rolled[:, :, half_width:], 1)
    return jnp.concatenate([col_strip, rolled[:, :, :half_width]], axis=2)


def half_windows(cell_grid):
    levels, row_count, col_count, channels = cell_grid.shape
    shaped = cell_grid.reshape(levels // WZ, WZ, row_count // WLAT, WLAT, col_count, channels)
    shaped = shaped.transpose(2, 0, 1, 3, 4, 5)
    return shaped.reshape(row_count // WLAT * (levels // WZ), WZ * WLAT * col_count, channels)


def half_grid(windows, levels, row_count):
    groups, place_count, channels = windows.shape
    col_count = place_count // (WZ * WLAT)
    shaped = windows.reshape(row_count // WLAT, levels // WZ, WZ, WLAT, col_count, channels)
    return shaped.transpose(1, 2, 0, 3, 4, 5).reshape(levels, row_count, col_count, channels)


def join_halves(left_half, right_half):
    leading = left_half.shape[:-2]
    channels = left_half.shape[-1]
    first_half = left_half.reshape(leading + (WZ * WLAT, -1, channels))
    second_half = right_half.reshape(leading + (WZ * WLAT, -1, channels))
    return jnp.concatenate([first_half, second_half], axis=-2).reshape(leading + (-1, channels))


def split_halves(complete):
    leading = complete.shape[:-2]
    channels = complete.shape[-1]
    shaped = complete.reshape(leading + (WZ * WLAT, WLON, channels))
    half_width = WLON // 2
    return (
        shaped[..., :half_width, :].reshape(leading + (-1, channels)),
        shaped[..., half_width:, :].reshape(leading + (-1, channels)),
    )


def arrange(mine_part, other_part, on_left):
    return join_halves(
        jnp.where(on_left, mine_part, other_part), jnp.where(on_left, other_part, mine_part)
    )


def pick_mine(complete, on_left):
    left_half, right_half = split_halves(complete)
    return (jnp.where(on_left, left_half, right_half), jnp.where(on_left, right_half, left_half))


def heads_to_columns(heads_block):
    swapped = jnp.swapaxes(heads_block, -2, -3)
    return swapped.reshape(swapped.shape[:-2] + (-1,))


def columns_to_heads(columns, head_count):
    shaped = columns.reshape(columns.shape[:-1] + (head_count, HD))
    return jnp.swapaxes(shaped, -2, -3)


def shards(
    tokens,
    fine_attend,
    fine_project,
    fine_gain_one,
    fine_expand,
    fine_reduce,
    fine_gain_two,
    fine_bias,
    merge_gain,
    merge_weight,
    coarse_attend,
    coarse_project,
    coarse_gain_one,
    coarse_expand,
    coarse_reduce,
    coarse_gain_two,
    coarse_bias,
    cotangent,
):
    fine_weights = (
        fine_attend,
        fine_project,
        fine_gain_one,
        fine_expand,
        fine_reduce,
        fine_gain_two,
    )
    coarse_weights = (
        coarse_attend,
        coarse_project,
        coarse_gain_one,
        coarse_expand,
        coarse_reduce,
        coarse_gain_two,
    )
    levels, row_count, row_width = tokens.shape
    lat_total = row_count * lax.axis_size("lat")
    row_start = lax.axis_index("lat") * row_count
    on_left = lax.axis_index("lon") % 2 == 0
    lat_windows = row_count // WLAT
    level_windows = levels // WZ
    window_cells = WZ * WLAT * WLON
    fine_allowed = pair_allowed(lat_windows, level_windows, row_start, lat_total)
    fine_allowed = fine_allowed.reshape(lat_windows * level_windows, window_cells, window_cells)

    def fine_level(framed, bias_table):
        cell_grid = framed.reshape(levels, row_count, WLON, C1)
        windows = windows_of(cell_grid)
        grouped = windows.reshape((lat_windows * level_windows,) + windows.shape[2:])
        mixture = window_block(grouped, bias_table, fine_allowed, fine_weights)
        return grid_of(mixture.reshape(windows.shape), levels, row_count, WLON).reshape(
            levels, row_count, row_width
        )

    framed = to_frame(tokens)
    rolled_out, fine_pullback = jax.vjp(fine_level, framed, fine_bias)
    fine_out = from_frame(rolled_out)

    def merge_piece(tokens_in):
        return merge_level(tokens_in.reshape(levels, row_count, WLON, C1), merge_gain, merge_weight)

    coarse_in, merge_pullback = jax.vjp(merge_piece, fine_out)
    coarse_rows = row_count // 2
    own_cells = half_windows(coarse_in)
    groups = own_cells.shape[0]
    head_count = coarse_bias.shape[1]
    packed, project_pullback = jax.vjp(
        lambda tokens_in: project(tokens_in, coarse_attend), own_cells
    )
    own_heads, split_pullback = jax.vjp(
        lambda block_data: split_qkv(block_data, head_count), packed
    )
    bias_full, bias_pullback = jax.vjp(build_bias, coarse_bias)
    column_width = packed.shape[-1] // 3
    partner_packed = swapped_2(packed[..., column_width:], "lon", 0)
    partner_key = to_heads(partner_packed[..., :column_width], head_count)
    partner_value = to_heads(partner_packed[..., column_width:], head_count)
    key_all = arrange(own_heads[1], partner_key, on_left)
    value_all = arrange(own_heads[2], partner_value, on_left)
    bias_rows = pick_mine(bias_full, on_left)[0]
    allowed_rows = jnp.ones((groups, own_cells.shape[1], window_cells), jnp.bool_)

    def attend_rows(query_heads, key_heads, value_heads, bias_part):
        return attend(
            query_heads[:, None], key_heads[:, None], value_heads[:, None], bias_part, allowed_rows
        )[:, 0]

    head_out, attend_pullback = jax.vjp(attend_rows, own_heads[0], key_all, value_all, bias_rows)
    out_cells, tail_pullback = jax.vjp(
        lambda tokens_in, heads_in: block_tail(tokens_in, heads_in, coarse_weights),
        own_cells,
        head_out,
    )
    coarse_out = half_grid(out_cells, levels, coarse_rows).reshape(levels, coarse_rows, -1)
    seed_cells = half_windows(cotangent.reshape(levels, coarse_rows, WLON // 2, C2))
    tail_cells, tail_heads = tail_pullback(seed_cells)
    grad_query, grad_key, grad_value, bias_mine = attend_pullback(tail_heads)
    key_mine, key_other = pick_mine(grad_key, on_left)
    value_mine, value_other = pick_mine(grad_value, on_left)
    outgoing = jnp.concatenate(
        [heads_to_columns(key_other), heads_to_columns(value_other)], axis=-1
    )
    incoming = swapped_2(outgoing.astype(jnp.bfloat16), "lon", 0).astype(outgoing.dtype)
    column_width = incoming.shape[-1] // 2
    grad_own = (
        grad_query,
        key_mine + columns_to_heads(incoming[..., :column_width], head_count),
        value_mine + columns_to_heads(incoming[..., column_width:], head_count),
    )
    grad_rows = arrange(bias_mine, jnp.zeros_like(bias_mine), on_left)
    (grad_coarse_bias,) = bias_pullback(grad_rows)
    (grad_packed,) = split_pullback(grad_own)
    (attend_cells,) = project_pullback(grad_packed)
    grad_cells = attend_cells + tail_cells
    grad_coarse_in = half_grid(grad_cells, levels, coarse_rows)
    (grad_fine_out,) = merge_pullback(grad_coarse_in)
    grad_frame, grad_fine_bias = fine_pullback(to_frame(grad_fine_out))
    grad_tokens = from_frame(grad_frame)
    grad_fine_bias, grad_coarse_bias = (
        lax.psum(grad_fine_bias.astype(jnp.bfloat16), "lon").astype(jnp.float32),
        lax.psum(grad_coarse_bias.astype(jnp.bfloat16), "lon").astype(jnp.float32),
    )
    return (coarse_out, grad_tokens, grad_fine_bias, grad_coarse_bias)


def solution(mesh):
    in_specs = (
        P(None, "lat", "lon"),
        P(),
        P(),
        P(),
        P(),
        P(),
        P(),
        P("lat", None, None, None),
        P(),
        P(),
        P(),
        P(),
        P(),
        P(),
        P(),
        P(),
        P("lat", None, None, None),
        P(None, "lat", "lon"),
    )
    out_specs = (
        P(None, "lat", "lon"),
        P(None, "lat", "lon"),
        P("lat", None, None, None),
        P("lat", None, None, None),
    )
    return jax.shard_map(shards, mesh=mesh, in_specs=in_specs, out_specs=out_specs, check_vma=False)
```

profile of v0, /device:TPU:1, one launch (start us, length us, event | category | flops | bytes accessed | tf_op | source)
XLA Modules:
  0.0 695.2 jit_solution(463967865874696550)
XLA Ops:
  8.3 3.3 collective-permute-start
  13.4 3.4 copy.162
  16.8 45.9 %convolution_bitcast_fusion = f32[2,12,12,12,12,12]{4,5,2,1,0,3:T(8,128)} fusion(f32[2,12,23,12,12]{2,0,4,3,1:T(2,128)} %bitcast.416, s32[12,12]{1,0:T(8,128)S(1)} %subtract_add_fusion), kind=kOutput, calls=%fused_computation.8 | convolution fusion | flops 137358576 | bytes 2309184 | tf_op jit(solution)/shard_map/jvp(ghdab,dpq->ghapbq)/dot_general | solution.py:51
  62.7 14.9 %convolution_bitcast_fusion.1 = f32[4,6,12,12,12,12]{4,5,2,1,0,3:T(8,128)} fusion(f32[4,6,23,12,12]{2,0,4,3,1:T(4,128)S(1)} %bitcast.415, s32[12,12]{1,0:T(8,128)S(1)} %subtract_add_fusion), kind=kOutput, calls=%fused_computation.9 | convolution fusion | flops 137358576 | bytes 2309184 | tf_op jit(solution)/shard_map/jvp(ghdab,dpq->ghapbq)/dot_general | solution.py:51
  77.9 32.0 %copy.164 = f32[2,12,12,12,12,12]{5,4,0,3,2,1:T(8,128)} copy(f32[2,12,12,12,12,12]{4,5,2,1,0,3:T(8,128)} %convolution_bitcast_fusion) | data formatting | bytes 3981312 | tf_op jit(solution)/shard_map/jvp(ghdab,dpq->ghapbq)/transpose | solution.py:51
  109.9 20.8 %reshape.879 = f32[2,12,12,12,144]{4,0,3,2,1:T(2,128)} reshape(f32[2,12,12,12,12,12]{5,4,0,3,2,1:T(8,128)} %copy.164) | data formatting | bytes 3981312 | tf_op jit(solution)/shard_map/reshape;jvp()/reshape | solution.py:214
  130.7 40.5 %copy.223 = f32[4,6,12,12,12,12]{3,2,5,4,1,0:T(8,128)} copy(f32[4,6,12,12,12,12]{4,5,2,1,0,3:T(8,128)} %convolution_bitcast_fusion.1) | data formatting | bytes 3981312 | tf_op jit(solution)/shard_map/jvp()/broadcast_in_dim;jvp()/reshape | solution.py:98
  171.2 19.7 %reshape.923 = f32[4,6,144,144]{2,3,1,0:T(8,128)} reshape(f32[4,6,12,12,12,12]{3,2,5,4,1,0:T(8,128)} %copy.223) | data formatting | bytes 3981312 | tf_op jit(solution)/shard_map/jvp()/broadcast_in_dim;jvp()/reshape | solution.py:98
  190.9 3.4 collective-permute-start.1
  200.3 3.4 fusion.257
  209.1 3.9 fusion.36
  218.2 4.2 slice_select_fusion
  223.3 3.6 collective-permute-start.3
  227.5 4.7 collective-permute-done.3
  237.8 5.5 collective-permute-start.4
  252.2 3.7 copy.161
  258.1 4.9 fusion.260
  266.4 3.6 pad_maximum_fusion
  270.0 3.9 copy.166
  283.0 4.3 multiply_reduce_fusion.5
  300.8 3.4 copy.176
  310.2 3.4 copy.174
  347.6 10.2 %select_n.187 = f32[2,12,12,6,12,12]{5,4,3,2,1,0:T(8,128)} reshape(f32[2,1,12,72,144]{4,3,2,0,1:T(8,128)} %get-tuple-element.20) | data formatting | bytes 1990656 | tf_op jit(solution)/shard_map/jit(_where)/select_n | solution.py:224
  357.8 8.5 %select_n.189 = f32[2,12,12,6,12,12]{5,4,3,2,1,0:T(8,128)} reshape(f32[2,1,12,72,144]{4,3,2,0,1:T(8,128)S(1)} %copy-done.21) | data formatting | bytes 1990656 | tf_op jit(solution)/shard_map/jit(_where)/select_n | solution.py:224
  366.2 3.5 collective-permute-start.7
  374.4 4.2 fusion.148
  394.3 18.3 %fusion.62 = bf16[2,12,23,12,12]{2,4,3,1,0:T(8,128)(2,1)S(1)} fusion(f32[2,12,12,6,12,12]{5,4,3,2,1,0:T(8,128)} %select_n.189, f32[2,12,12,6,12,12]{5,4,3,2,1,0:T(8,128)} %select_n.187, s32[12,12]{1,0:T(8,128)S(1)} %subtract_add_fusion), kind=kOutput, calls=%fused_computation.95 | convolution fusion | flops 137935728 | bytes 2150208 | tf_op jit(solution)/shard_map/transpose(jvp(ghdab,dpq->ghapbq))/dot_general | solution.py:51
  415.8 5.6 copy.205
  421.3 18.4 %reshape.904 = f32[4,6,12,12,12,12]{5,4,3,2,1,0:T(8,128)} reshape(f32[4,1,6,144,144]{4,3,2,0,1:T(8,128)} %copy.205) | data formatting | bytes 3981312 | tf_op jit(solution)/shard_map/transpose(jvp())/reshape | solution.py:54
  439.8 3.3 collective-permute-start.9
  443.1 15.6 %fusion.59 = bf16[4,6,23,12,12]{2,4,3,1,0:T(8,128)(2,1)S(1)} fusion(f32[4,6,12,12,12,12]{5,4,3,2,1,0:T(8,128)} %reshape.904, s32[12,12]{1,0:T(8,128)S(1)} %subtract_add_fusion), kind=kOutput, calls=%fused_computation.94 | convolution fusion | flops 137438064 | bytes 2150208 | tf_op jit(solution)/shard_map/transpose(jvp(ghdab,dpq->ghapbq))/dot_general | solution.py:51
  461.6 221.9 %all-reduce.9.cloned.1.call-done = (bf16[4,6,23,144]{2,0,3,1:T(4,128)(2,1)}, bf16[2,12,23,144]{2,0,3,1:T(2,128)(2,1)}) async-done(((bf16[4,6,23,144]{2,0,3,1:T(4,128)(2,1)}, bf16[2,12,23,144]{2,0,3,1:T(2,128)(2,1)}), (bf16[4,6,23,144]{2,0,3,1:T(4,128)(2,1)}, bf16[2,12,23,144]{2,0,3,1:T(2,128)(2,1)})) %all-reduce.9.cloned.1.call-update) | async-done | bytes 317968 | tf_op jit(solution)/shard_map/psum | solution.py:363
  (360 shorter events, 133.7 us)
Async XLA Ops:
  7.2 270.6 %copy-start = (bf16[384,1536]{1,0:T(8,128)(2,1)S(1)}, bf16[384,1536]{1,0:T(8,128)(2,1)}, u32[]{:S(2)}) copy-start(bf16[384,1536]{1,0:T(8,128)(2,1)} %param.31) | copy-start | bytes 3538948
  7.2 676.3 %all-reduce.9.cloned.1.call-start = ((), (), s32[]{:S(2)}) async-start(), calls=%async_computation | async-start | bytes 3538944 | tf_op jit(solution)/shard_map/psum | solution.py:363
  8.3 182.6 %collective-permute-start = (bf16[2,24,1152]{2,1,0:T(8,128)(2,1)S(1)}, bf16[2,24,1152]{2,1,0:T(8,128)(2,1)S(1)}, u32[]{:S(2)}, u32[]{:S(2)}) collective-permute-start(bf16[2,24,1152]{2,1,0:T(8,128)(2,1)S(1)} %get-tuple-element.45), channel_id=1, source_target_pairs={{0,248},{8,0},{16,8},{24,16},{32,24},{40,32},{48,40},{56,48},{64,5... | collective-permute-start | bytes 331784 | tf_op jit(solution)/shard_map/ppermute | solution.py:24
  77.9 119.5 %copy-start.36 = (pred[4,144,144]{1,2,0:T(8,128)(4,1)}, pred[4,144,144]{1,2,0:T(8,128)(4,1)S(1)}, u32[]{:S(2)}) copy-start(pred[4,144,144]{1,2,0:T(8,128)(4,1)S(1)} %broadcast_compare_fusion) | copy-start | bytes 248836
  190.9 5.2 copy-start.57
  190.9 4.5 collective-permute-start.1
  196.9 3.4 copy-start.22
  197.3 8.2 %copy-start.27 = (bf16[4,1,144,192]{2,3,0,1:T(8,128)(2,1)}, bf16[4,1,144,192]{2,3,0,1:T(8,128)(2,1)S(1)}, u32[]{:S(2)}) copy-start(bf16[4,1,144,192]{2,3,0,1:T(8,128)(2,1)S(1)} %copy.135) | copy-start | bytes 663556
  209.0 3.9 copy-start.15
  209.0 3.9 copy-start.51
  216.2 6.2 copy-start.62
  216.2 10.7 %copy-start.48 = (f32[4,6,144]{2,1,0:T(8,128)S(1)}, f32[4,6,144]{2,1,0:T(8,128)}, u32[]{:S(2)}) copy-start(f32[4,6,144]{2,1,0:T(8,128)} %copy-done.47) | copy-start | bytes 41476
  216.2 7.0 %collective-permute-start.2 = (bf16[2,3,2304]{2,1,0:T(4,128)(2,1)S(1)}, bf16[2,3,2304]{2,1,0:T(4,128)(2,1)S(1)}, u32[]{:S(2)}, u32[]{:S(2)}) collective-permute-start(bf16[2,3,2304]{2,1,0:T(4,128)(2,1)S(1)} %slice.193), channel_id=1, source_target_pairs={{0,1},{1,2},{2,3},{3,4},{4,5},{5,6},{6,7},{7,0},{8,9},{9,10},{10,1... | collective-permute-start | bytes 82952 | tf_op jit(solution)/shard_map/ppermute | solution.py:24
  223.3 8.9 %collective-permute-start.3 = (bf16[2,24,1152]{2,1,0:T(8,128)(2,1)S(1)}, bf16[2,24,1152]{2,1,0:T(8,128)(2,1)S(1)}, u32[]{:S(2)}, u32[]{:S(2)}) collective-permute-start(bf16[2,24,1152]{2,1,0:T(8,128)(2,1)S(1)} %fusion.200), channel_id=1, source_target_pairs={{0,8},{8,16},{16,24},{24,32},{32,40},{40,48},{48,56},{56,64},{64,7... | collective-permute-start | bytes 331784 | tf_op jit(solution)/shard_map/ppermute | solution.py:24
  235.3 8.0 %copy-start.7 = (f32[2,12,6,768]{3,2,1,0:T(8,128)}, f32[2,12,6,768]{3,2,1,0:T(8,128)S(1)}, u32[]{:S(2)}) copy-start(f32[2,12,6,768]{3,2,1,0:T(8,128)S(1)} %reshape.924) | copy-start | bytes 1327108
  236.7 7.9 %copy-start.39 = (bf16[1,2,2,6,6,384]{5,2,4,3,1,0:T(2,128)(2,1)}, bf16[1,2,2,6,6,384]{5,2,4,3,1,0:T(2,128)(2,1)S(1)}, u32[]{:S(2)}) copy-start(bf16[1,2,2,6,6,384]{5,2,4,3,1,0:T(2,128)(2,1)S(1)} %copy.149) | copy-start | bytes 331780
  237.8 6.8 collective-permute-start.4
  252.2 3.7 copy-start.18
  287.3 5.2 copy-start.14
  294.6 4.2 copy-start.11
  319.1 3.3 collective-permute-start.5
  327.8 3.4 copy-start.26
  333.6 3.4 copy-start.8
  338.1 6.7 copy-start.12
  344.7 21.5 %collective-permute-start.6 = (bf16[2,24,1152]{2,1,0:T(8,128)(2,1)}, bf16[2,24,1152]{2,1,0:T(8,128)(2,1)S(1)}, u32[]{:S(2)}, u32[]{:S(2)}) collective-permute-start(bf16[2,24,1152]{2,1,0:T(8,128)(2,1)} %get-tuple-element.37), channel_id=1, source_target_pairs={{0,248},{8,0},{16,8},{24,16},{32,24},{40,32},{48,40},{56,48},{64,5... | collective-permute-start | bytes 331784 | tf_op jit(solution)/shard_map/ppermute | solution.py:24
  347.6 10.2 %copy-start.21 = (f32[2,1,12,72,144]{4,3,2,0,1:T(8,128)S(1)}, f32[2,1,12,72,144]{4,3,2,0,1:T(8,128)}, u32[]{:S(2)}) copy-start(f32[2,1,12,72,144]{4,3,2,0,1:T(8,128)} %get-tuple-element.21) | copy-start | bytes 2985988
  366.2 4.6 collective-permute-start.7
  378.6 4.0 copy-start.6
  392.9 19.8 %copy-start.50 = (bf16[2,72,384]{2,1,0:T(8,128)(2,1)S(1)}, bf16[2,72,384]{2,1,0:T(8,128)(2,1)}, u32[]{:S(2)}) copy-start(bf16[2,72,384]{2,1,0:T(8,128)(2,1)} %get-tuple-element.35) | copy-start | bytes 331780
  392.9 46.9 %collective-permute-start.8 = (bf16[2,3,2304]{2,1,0:T(4,128)(2,1)S(1)}, bf16[2,3,2304]{2,1,0:T(4,128)(2,1)S(1)}, u32[]{:S(2)}, u32[]{:S(2)}) collective-permute-start(bf16[2,3,2304]{2,1,0:T(4,128)(2,1)S(1)} %slice.219), channel_id=1, source_target_pairs={{0,1},{1,2},{2,3},{3,4},{4,5},{5,6},{6,7},{7,0},{8,9},{9,10},{10,1... | collective-permute-start | bytes 82952 | tf_op jit(solution)/shard_map/ppermute | solution.py:24
  439.8 21.0 %collective-permute-start.9 = (bf16[2,24,1152]{2,1,0:T(8,128)(2,1)S(1)}, bf16[2,24,1152]{2,1,0:T(8,128)(2,1)S(1)}, u32[]{:S(2)}, u32[]{:S(2)}) collective-permute-start(bf16[2,24,1152]{2,1,0:T(8,128)(2,1)S(1)} %fusion.198), channel_id=1, source_target_pairs={{0,8},{8,16},{16,24},{24,32},{32,40},{40,48},{48,56},{56,64},{64,7... | collective-permute-start | bytes 331784 | tf_op jit(solution)/shard_map/ppermute | solution.py:24
  460.8 227.4 %copy-start.1 = (bf16[384,1536]{1,0:T(8,128)(2,1)S(1)}, bf16[384,1536]{1,0:T(8,128)(2,1)}, u32[]{:S(2)}) copy-start(bf16[384,1536]{1,0:T(8,128)(2,1)} %param.31) | copy-start | bytes 3538948
  (65 other events, 101.4 us)
Sparse Core Ops, SparseCore 0:
  461.0 222.4 all-reduce.8
where the time goes:
time: 709 us; the launch traced here: 695 us
  local copies, waits for them, and re-layouts  231 us (33%)
  waiting for transfers between devices  229 us (32%)
  matrix products  133 us (19%)
  other arithmetic  60 us (8%)
  starting transfers between devices  26.7 us (4%)
  between operations  15.8 us (2%)
    psum x1, waiting for transfers between devices, shards(): lax.psum(grad_fine_bias.astype(jnp.bfloat16), 'lon').astype(jnp.float32)  222 us
    dot_general x4, matrix products, build_bias(): jnp.einsum('ghdab,dpq->ghapbq', shaped, offset_onehot(), precision=lax.Pr...  94.7 us
    reshape x2, local copies, waits for them, and re-layouts, attend(): scores = scores / math.sqrt(HD) + bias_full[:, None]  60.2 us
    transpose x1, local copies, waits for them, and re-layouts, build_bias(): jnp.einsum('ghdab,dpq->ghapbq', shaped, offset_onehot(), precision=lax.Pr...  32 us
    reshape x1, local copies, waits for them, and re-layouts, split_halves(): shaped = complete.reshape(leading + (WZ * WLAT, WLON, channels))  20.8 us
    ppermute x8, starting transfers between devices, shifted_2(): return lax.ppermute(value, axis, pairs)  20.8 us
    unnamed x178, local copies, waits for them, and re-layouts  19.1 us
    reshape x1, local copies, waits for them, and re-layouts, build_bias(): spread.reshape(groups, head_count, plane_cells * WLON, plane_cells * WLON)  18.4 us
  transfers between devices with their start and end apart: 11, of which 5 were waited for; matrix products, arithmetic and copies ran while one was open for 39% of the time, Pallas kernels for 0%

commit v1 on v0

v1 whole, which is shorter than its diff:
```python
import functools
import math

import jax
import jax.numpy as jnp
import numpy as np
from jax import lax
from jax.experimental import pallas as pl
from jax.experimental.pallas import tpu as pltpu
from jax.sharding import PartitionSpec as P

C1 = 192
C2 = 384
HD = 32
H1 = 6
H2 = 12
WLON = 12
HALF = 72
EPSILON = 1e-05
MASKED = -1000000000.0
SCALE = 1.0 / math.sqrt(HD)
F32 = jnp.float32
BF16 = jnp.bfloat16


def pair_lane(pair):
    return pair // 5 * 128 + pair % 5 * 24


def spread_onehot(pairs, lanes):
    onehot = np.zeros((WLON, (pairs + 4) // 5 * 128, lanes), np.float32)
    for p in range(WLON):
        for b in range(pairs):
            for q in range(WLON):
                onehot[p, pair_lane(b) + p - q + WLON - 1, b * WLON + q] = 1.0
    return onehot.astype(jnp.bfloat16)


def merge_onehot():
    onehot = np.zeros((4, 2, 2, 48, 648), np.float32)
    for rr in range(2):
        for cc in range(2):
            for bh in range(2):
                for lam in range(2):
                    for z in range(2):
                        for a in range(6):
                            for b in range(3):
                                row = 2 * (lam * 6 + a) + rr
                                col = 2 * (bh * 3 + b) + cc
                                if row < 3:
                                    cell = 576 + z * 36 + row * 12 + col
                                else:
                                    cell = z * 288 + (row - 3) * 12 + col
                                onehot[rr * 2 + cc, bh, lam, z * 18 + a * 3 + b, cell] = 1.0
    return onehot.reshape(768, 648).astype(jnp.bfloat16)


def strip_onehot():
    onehot = np.zeros((576, 72), np.float32)
    for z in range(2):
        for k in range(36):
            onehot[z * 288 + 252 + k, z * 36 + k] = 1.0
    return onehot.astype(jnp.bfloat16)


def window_onehot():
    onehot = np.zeros((2, 144, 192), np.float32)
    for parity in range(2):
        for z in range(2):
            for a in range(6):
                for c in range(12):
                    kept = (c < 6) == (parity == 0)
                    local = c % 6
                    place = (0 if kept else 96) + local // 3 * 48 + z * 18 + a * 3 + local % 3
                    onehot[parity, z * 72 + a * 12 + c, place] = 1.0
    return onehot.astype(jnp.bfloat16)


def halves_onehot():
    onehot = np.zeros((2, 144, 144), np.float32)
    for parity in range(2):
        for z in range(2):
            for a in range(6):
                for c in range(12):
                    kept = (c < 6) == (parity == 0)
                    place = (0 if kept else 72) + z * 36 + a * 6 + c % 6
                    onehot[parity, z * 72 + a * 12 + c, place] = 1.0
    return onehot.astype(jnp.bfloat16)


def nn(left, right):
    return lax.dot_general(left, right, (((1,), (0,)), ((), ())), preferred_element_type=F32)


def nt(left, right):
    return lax.dot_general(left, right, (((1,), (1,)), ((), ())), preferred_element_type=F32)


def tn(left, right):
    return lax.dot_general(left, right, (((0,), (0,)), ((), ())), preferred_element_type=F32)


def norm_parts(values):
    average = jnp.mean(values, axis=-1, keepdims=True)
    centred = values - average
    scale = lax.rsqrt(jnp.mean(centred * centred, axis=-1, keepdims=True) + EPSILON)
    return centred * scale, scale


def norm_back(grad, normed, scale):
    first = jnp.mean(grad, axis=-1, keepdims=True)
    second = jnp.mean(grad * normed, axis=-1, keepdims=True)
    return scale * (grad - first - normed * second)


def split3(values):
    high = values.astype(BF16)
    rest = values - high.astype(F32)
    mid = rest.astype(BF16)
    low = (rest - mid.astype(F32)).astype(BF16)
    return high, mid, low


def head_mask(rows, heads, width):
    row = lax.broadcasted_iota(jnp.int32, (heads * rows, width), 0) // rows
    lane = lax.broadcasted_iota(jnp.int32, (heads * rows, width), 1) // HD
    return (row == lane).astype(F32)


def heads_stack(values, heads, mask):
    return (jnp.concatenate([values] * heads, axis=0) * mask).astype(BF16)


def heads_fold(stacked, heads, mask):
    rows = stacked.shape[0] // heads
    kept = stacked * mask
    total = kept[:rows]
    for h in range(1, heads):
        total = total + kept[h * rows : (h + 1) * rows]
    return total


def gelu_parts(values):
    phi = 0.5 * (1.0 + lax.erf(values * (1.0 / math.sqrt(2.0))))
    density = jnp.exp(-0.5 * values * values) * (1.0 / math.sqrt(2.0 * math.pi))
    return values * phi, phi + values * density


def softmax(scores):
    top = jnp.max(scores, axis=-1, keepdims=True)
    powers = jnp.exp(scores - top)
    return powers / jnp.sum(powers, axis=-1, keepdims=True)


def bias_kernel(par_ref, fine_ref, coarse_ref, ef_ref, ec_ref, bf_ref, bc_ref, cols_f, cols_c):
    cols_f[...] = jnp.zeros_like(cols_f)
    cols_c[...] = jnp.zeros_like(cols_c)
    for th in range(24):
        cols_f[th * 144 : (th + 1) * 144, 0:23] = jnp.swapaxes(fine_ref[th], 0, 1)
    par = par_ref[0]
    for h in range(12):
        cols_c[h * 144 : (h + 1) * 144, 0:23] = jnp.swapaxes(coarse_ref[par, h], 0, 1)
    low_level = lax.broadcasted_iota(jnp.int32, (288, 128), 0) % 12 < 6
    tiles = []
    for t in range(2):
        tile = None
        for jm in range(t * 5, min(t * 5 + 5, 6)):
            piece = jnp.where(
                low_level,
                cols_f[pl.ds(jm, 288, stride=12), :],
                cols_f[pl.ds(6 + jm, 288, stride=12), :],
            )
            if jm % 5:
                piece = pltpu.roll(piece, jm % 5 * 24, 1)
            tile = piece if tile is None else tile + piece
        tiles.append(tile)
    table = jnp.concatenate(tiles, axis=1)
    parts = jnp.concatenate(split3(table), axis=0)
    for p in range(WLON):
        spread = nn(parts, ef_ref[p])
        bf_ref[pl.ds(p, 288, stride=12), :] = spread[:288] + spread[288:576] + spread[576:]
    tiles = []
    for t in range(3):
        tile = None
        for b in range(t * 5, min(t * 5 + 5, 12)):
            piece = cols_c[pl.ds(b, 144, stride=12), :]
            if b % 5:
                piece = pltpu.roll(piece, b % 5 * 24, 1)
            tile = piece if tile is None else tile + piece
        tiles.append(tile)
    table = jnp.concatenate(tiles, axis=1)
    parts = jnp.concatenate(split3(table), axis=0)
    for p in range(WLON):
        spread = nn(parts, ec_ref[p])
        total = spread[:144] + spread[144:288] + spread[288:]
        bc_ref[0, pl.ds(p, 144, stride=12), :] = total[:, :128]
        bc_ref[1, pl.ds(p, 144, stride=12), :] = total[:, 128:]


def bias_call(par, fine_table, coarse_tables):
    return pl.pallas_call(
        bias_kernel,
        out_shape=(
            jax.ShapeDtypeStruct((3456, 128), F32),
            jax.ShapeDtypeStruct((2, 1728, 128), F32),
        ),
        in_specs=[pl.BlockSpec(memory_space=pltpu.SMEM)]
        + [pl.BlockSpec(memory_space=pltpu.VMEM)] * 4,
        scratch_shapes=[pltpu.VMEM((3456, 128), F32), pltpu.VMEM((1728, 128), F32)],
        compiler_params=pltpu.CompilerParams(vmem_limit_bytes=24 << 20),
        name="bias_spread",
    )(par, fine_table, coarse_tables, spread_onehot(6, 128), spread_onehot(12, 256))


def fine_kernel(
    last_ref, x_ref, wa_ref, wp_ref, g1_ref, we_ref, wr_ref, g2_ref, bias_ref,
    y_ref, q_ref, k_ref, v_ref, a_ref, att_ref, slope_ref, red_ref, o_ref,
):
    x = x_ref[...]
    q_ref[...] = nn(x, wa_ref[:, :C1]).astype(BF16).astype(F32)
    k_ref[...] = nn(x, wa_ref[:, C1 : 2 * C1]).astype(BF16).astype(F32)
    v_ref[...] = nn(x, wa_ref[:, 2 * C1 :]).astype(BF16).astype(F32)
    mask = head_mask(HALF, H1, C1)
    last = last_ref[0]
    for z in range(2):
        for w in range(4):
            rows = slice(z * 288 + w * 72, z * 288 + w * 72 + 72)
            qs = heads_stack(q_ref[rows, :], H1, mask)
            places = [((w * 6 + h) * 2 + 1 - z) * 72 for h in range(H1)]
            bias = jnp.concatenate([bias_ref[s : s + 72, :] for s in places], axis=0)[:, :72]
            scores = nt(qs, k_ref[rows, :].astype(BF16)) * SCALE + bias
            if w == 3:
                row = lax.broadcasted_iota(jnp.int32, scores.shape, 0) % 72 < 36
                col = lax.broadcasted_iota(jnp.int32, scores.shape, 1) < 36
                scores = jnp.where(jnp.logical_and(row != col, last == 1), MASKED, scores)
            weights = softmax(scores).astype(BF16)
            block = z * 4 + w
            a_ref[block * 432 : (block + 1) * 432, :] = weights
            o_ref[rows, :] = heads_fold(nn(weights, v_ref[rows, :].astype(BF16)), H1, mask)
    for c in range(4):
        rows = slice(c * 144, (c + 1) * 144)
        att = nn(o_ref[rows, :].astype(BF16), wp_ref[...])
        att_ref[rows, :] = att
        normed, _ = norm_parts(att)
        middle = (x_ref[rows, :].astype(F32) + g1_ref[...] * normed).astype(BF16)
        act, slope = gelu_parts(nn(middle, we_ref[...]))
        slope_ref[rows, :] = slope.astype(BF16)
        red = nn(act.astype(BF16), wr_ref[...])
        red_ref[rows, :] = red
        normed, _ = norm_parts(red)
        y_ref[rows, :] = (middle.astype(F32) + g2_ref[...] * normed).astype(BF16)


def fine_call(last, x, weights, bias):
    wa, wp, g1, we, wr, g2 = weights
    shape = jax.ShapeDtypeStruct
    return pl.pallas_call(
        fine_kernel,
        out_shape=(
            shape((576, C1), BF16),
            shape((576, C1), F32),
            shape((576, C1), F32),
            shape((576, C1), F32),
            shape((3456, 72), BF16),
            shape((576, C1), F32),
            shape((576, 4 * C1), BF16),
            shape((576, C1), F32),
        ),
        in_specs=[pl.BlockSpec(memory_space=pltpu.SMEM)]
        + [pl.BlockSpec(memory_space=pltpu.VMEM)] * 8,
        scratch_shapes=[pltpu.VMEM((576, C1), F32)],
        compiler_params=pltpu.CompilerParams(vmem_limit_bytes=32 << 20),
        name="fine_forward",
    )(last, x, wa, wp, g1.reshape(1, C1), we, wr, g2.reshape(1, C1), bias)


def merge_kernel(y_ref, strip_ref, pick_ref, gain_ref, w_ref, out_ref, f_ref):
    cells = jnp.concatenate([y_ref[...], strip_ref[...]], axis=0)
    f = nn(pick_ref[...], cells)
    f_ref[...] = f.astype(BF16)
    total = sum(jnp.sum(f[k * 192 : (k + 1) * 192], axis=-1, keepdims=True) for k in range(4))
    average = total * (1.0 / 768)
    centred = [f[k * 192 : (k + 1) * 192] - average for k in range(4)]
    square = sum(jnp.sum(c * c, axis=-1, keepdims=True) for c in centred)
    scale = lax.rsqrt(square * (1.0 / 768) + EPSILON)
    result = None
    for k in range(4):
        normed = (gain_ref[k : k + 1, :] * (centred[k] * scale)).astype(BF16)
        part = nn(normed, w_ref[k * 192 : (k + 1) * 192, :])
        result = part if result is None else result + part
    out_ref[...] = result.astype(BF16)


def merge_call(y, strip, pick, gain, weight):
    shape = jax.ShapeDtypeStruct
    return pl.pallas_call(
        merge_kernel,
        out_shape=(shape((192, C2), BF16), shape((768, C1), BF16)),
        in_specs=[pl.BlockSpec(memory_space=pltpu.VMEM)] * 5,
        compiler_params=pltpu.CompilerParams(vmem_limit_bytes=24 << 20),
        name="merge_forward",
    )(y, strip, pick, gain.reshape(4, C1), weight)


def coarse_kernel(
    par_ref, keep_ref, got_ref, ckeep_ref, cgot_ref, pick_ref, half_ref,
    wa_ref, wp_ref, g1_ref, we_ref, wr_ref, g2_ref, bias_ref, ec_ref,
    okeep_ref, osend_ref, gkeep_ref, gsend_ref, dt_ref,
    a_ref, qs_ref, o_ref, ds_ref, slope_ref,
):
    par = par_ref[0]
    pick = pick_ref[par]
    half = half_ref[par]
    x = nn(pick, jnp.concatenate([keep_ref[...], got_ref[...]], axis=0)).astype(BF16)
    seed = nn(half, jnp.concatenate([ckeep_ref[...], cgot_ref[...]], axis=0))
    packed = nn(x, wa_ref[...]).astype(BF16)
    mask = head_mask(144, 4, 128)
    for g in range(3):
        lanes = slice(g * 128, (g + 1) * 128)
        rows = slice(g * 576, (g + 1) * 576)
        qs = heads_stack(packed[:, lanes].astype(F32), 4, mask)
        qs_ref[rows, :] = qs
        key = packed[:, C2 + g * 128 : C2 + (g + 1) * 128]
        value = packed[:, 2 * C2 + g * 128 : 2 * C2 + (g + 1) * 128]
        bias = jnp.concatenate([bias_ref[0, rows, :], bias_ref[1, rows, :]], axis=1)[:, :144]
        weights = softmax(nt(qs, key) * SCALE + bias).astype(BF16)
        a_ref[rows, :] = weights
        o_ref[:, lanes] = heads_fold(nn(weights, value), 4, mask)
    att = nn(o_ref[...].astype(BF16), wp_ref[...])
    normed1, scale1 = norm_parts(att)
    middle = (x.astype(F32) + g1_ref[...] * normed1).astype(BF16)
    act, slope = gelu_parts(nn(middle, we_ref[...]))
    slope_ref[...] = slope
    red = nn(act.astype(BF16), wr_ref[...])
    normed2, scale2 = norm_parts(red)
    out = (middle.astype(F32) + g2_ref[...] * normed2).astype(BF16)
    parted = tn(half, out)
    okeep_ref[...] = parted[:72].astype(BF16)
    osend_ref[...] = parted[72:].astype(BF16)
    grad_red = norm_back(seed * g2_ref[...], normed2, scale2).astype(BF16)
    grad_act = nt(grad_red, wr_ref[...]).astype(BF16).astype(F32)
    grad_exp = (grad_act * slope_ref[...]).astype(BF16)
    grad_middle = (seed + nt(grad_exp, we_ref[...]).astype(BF16).astype(F32)).astype(BF16)
    grad_middle = grad_middle.astype(F32)
    grad_att = norm_back(grad_middle * g1_ref[...], normed1, scale1).astype(BF16)
    grad_o = nt(grad_att, wp_ref[...]).astype(BF16)
    grad_x = grad_middle
    for g in range(3):
        lanes = slice(g * 128, (g + 1) * 128)
        rows = slice(g * 576, (g + 1) * 576)
        os = heads_stack(grad_o[:, lanes].astype(F32), 4, mask)
        key = packed[:, C2 + g * 128 : C2 + (g + 1) * 128]
        value = packed[:, 2 * C2 + g * 128 : 2 * C2 + (g + 1) * 128]
        weights = a_ref[rows, :]
        grad_a = nt(os, value)
        wide = weights.astype(F32)
        grad_s = wide * (grad_a - jnp.sum(wide * grad_a, axis=-1, keepdims=True))
        ds_ref[0, rows, :] = grad_s[:, :128]
        ds_ref[1, rows, 0:16] = grad_s[:, 128:]
        short = grad_s.astype(BF16)
        grad_v = tn(weights, os).astype(BF16)
        grad_q = (heads_fold(nn(short, key), 4, mask) * SCALE).astype(BF16)
        grad_k = (tn(short, qs_ref[rows, :]) * SCALE).astype(BF16)
        grad_x = grad_x + nt(grad_q, wa_ref[:, g * 128 : (g + 1) * 128])
        grad_x = grad_x + nt(grad_k, wa_ref[:, C2 + g * 128 : C2 + (g + 1) * 128])
        grad_x = grad_x + nt(grad_v, wa_ref[:, 2 * C2 + g * 128 : 2 * C2 + (g + 1) * 128])
    parted = tn(pick, grad_x.astype(BF16))
    gkeep_ref[...] = parted[:96].astype(BF16)
    gsend_ref[...] = parted[96:].astype(BF16)
    table = None
    for p in range(WLON):
        piece = jnp.concatenate(
            [
                ds_ref[0, pl.ds(p, 144, stride=12), :],
                ds_ref[1, pl.ds(p, 144, stride=12), :][:, :16],
            ],
            axis=1,
        ).astype(BF16)
        part = nt(piece, ec_ref[p])
        table = part if table is None else table + part
    dt_ref[...] = table.astype(BF16)


def coarse_call(par, keep, got, ckeep, cgot, weights, bias):
    wa, wp, g1, we, wr, g2 = weights
    shape = jax.ShapeDtypeStruct
    return pl.pallas_call(
        coarse_kernel,
        out_shape=(
            shape((72, C2), BF16),
            shape((72, C2), BF16),
            shape((96, C2), BF16),
            shape((96, C2), BF16),
            shape((144, 384), BF16),
        ),
        in_specs=[pl.BlockSpec(memory_space=pltpu.SMEM)]
        + [pl.BlockSpec(memory_space=pltpu.VMEM)] * 14,
        scratch_shapes=[
            pltpu.VMEM((1728, 144), BF16),
            pltpu.VMEM((1728, 128), BF16),
            pltpu.VMEM((144, C2), F32),
            pltpu.VMEM((2, 1728, 128), F32),
            pltpu.VMEM((144, 4 * C2), F32),
        ],
        compiler_params=pltpu.CompilerParams(vmem_limit_bytes=36 << 20),
        name="coarse_both",
    )(
        par, keep, got, ckeep, cgot, window_onehot(), halves_onehot(),
        wa, wp, g1.reshape(1, C2), we, wr, g2.reshape(1, C2), bias,
        spread_onehot(12, 144),
    )


def merge_back_kernel(g_ref, f_ref, place_ref, gain_ref, w_ref, gy_ref, gstrip_ref):
    f = f_ref[...].astype(F32)
    total = sum(jnp.sum(f[k * 192 : (k + 1) * 192], axis=-1, keepdims=True) for k in range(4))
    average = total * (1.0 / 768)
    centred = [f[k * 192 : (k + 1) * 192] - average for k in range(4)]
    square = sum(jnp.sum(c * c, axis=-1, keepdims=True) for c in centred)
    scale = lax.rsqrt(square * (1.0 / 768) + EPSILON)
    g = g_ref[...]
    normed = [c * scale for c in centred]
    grads = []
    for k in range(4):
        part = nt(g, w_ref[k * 192 : (k + 1) * 192, :]).astype(BF16).astype(F32)
        grads.append(part * gain_ref[k : k + 1, :])
    first = sum(jnp.sum(p, axis=-1, keepdims=True) for p in grads) * (1.0 / 768)
    second = sum(jnp.sum(p * n, axis=-1, keepdims=True) for p, n in zip(grads, normed))
    second = second * (1.0 / 768)
    back = [(scale * (p - first - n * second)).astype(BF16) for p, n in zip(grads, normed)]
    placed = nn(place_ref[...], jnp.concatenate(back, axis=0)).astype(BF16)
    gy_ref[...] = placed[:576]
    gstrip_ref[...] = placed[576:]


def merge_back_call(g, f, place, gain, weight):
    shape = jax.ShapeDtypeStruct
    return pl.pallas_call(
        merge_back_kernel,
        out_shape=(shape((576, C1), BF16), shape((72, C1), BF16)),
        in_specs=[pl.BlockSpec(memory_space=pltpu.VMEM)] * 5,
        compiler_params=pltpu.CompilerParams(vmem_limit_bytes=24 << 20),
        name="merge_backward",
    )(g, f, place, gain.reshape(4, C1), weight)


def fine_back_kernel(
    gy_ref, strip_ref, place_ref, q_ref, k_ref, v_ref, a_ref, att_ref, slope_ref, red_ref,
    wa_ref, wp_ref, g1_ref, we_ref, wr_ref, g2_ref, ef_ref,
    gx_ref, dt_ref, gm_ref, go_ref, dq_ref, dk_ref, dv_ref, ds_ref,
):
    strip = strip_ref[...]
    for c in range(4):
        rows = slice(c * 144, (c + 1) * 144)
        seed = gy_ref[rows, :].astype(F32) + nn(place_ref[rows, :], strip)
        normed, scale = norm_parts(red_ref[rows, :])
        grad_red = norm_back(seed * g2_ref[...], normed, scale).astype(BF16)
        grad_act = nt(grad_red, wr_ref[...]).astype(BF16).astype(F32)
        grad_exp = (grad_act * slope_ref[rows, :].astype(F32)).astype(BF16)
        grad_middle = seed + nt(grad_exp, we_ref[...]).astype(BF16).astype(F32)
        grad_middle = grad_middle.astype(BF16).astype(F32)
        gm_ref[rows, :] = grad_middle
        normed, scale = norm_parts(att_ref[rows, :])
        grad_att = norm_back(grad_middle * g1_ref[...], normed, scale).astype(BF16)
        go_ref[rows, :] = nt(grad_att, wp_ref[...]).astype(BF16).astype(F32)
    mask = head_mask(HALF, H1, C1)
    for z in range(2):
        for w in range(4):
            rows = slice(z * 288 + w * 72, z * 288 + w * 72 + 72)
            block = z * 4 + w
            os = heads_stack(go_ref[rows, :], H1, mask)
            qs = heads_stack(q_ref[rows, :], H1, mask)
            weights = a_ref[block * 432 : (block + 1) * 432, :]
            grad_a = nt(os, v_ref[rows, :].astype(BF16))
            wide = weights.astype(F32)
            grad_s = wide * (grad_a - jnp.sum(wide * grad_a, axis=-1, keepdims=True))
            for h in range(H1):
                place = ((w * 6 + h) * 2 + 1 - z) * 72
                ds_ref[place : place + 72, 0:72] = grad_s[h * 72 : (h + 1) * 72]
            short = grad_s.astype(BF16)
            dv_ref[rows, :] = tn(weights, os)
            dq_ref[rows, :] = heads_fold(nn(short, k_ref[rows, :].astype(BF16)), H1, mask) * SCALE
            dk_ref[rows, :] = tn(short, qs) * SCALE
    table = None
    for p in range(WLON):
        piece = ds_ref[pl.ds(p, 288, stride=12), :][:, :72].astype(BF16)
        part = nt(piece, ef_ref[p][:, :72])
        table = part if table is None else table + part
    dt_ref[...] = table.astype(BF16)
    total = gm_ref[...]
    total = total + nt(dq_ref[...].astype(BF16), wa_ref[:, :C1])
    total = total + nt(dk_ref[...].astype(BF16), wa_ref[:, C1 : 2 * C1])
    total = total + nt(dv_ref[...].astype(BF16), wa_ref[:, 2 * C1 :])
    gx_ref[...] = total.astype(BF16)


def fine_back_call(gy, strip, saved, weights):
    wa, wp, g1, we, wr, g2 = weights
    shape = jax.ShapeDtypeStruct
    return pl.pallas_call(
        fine_back_kernel,
        out_shape=(shape((576, C1), BF16), shape((288, 256), BF16)),
        in_specs=[pl.BlockSpec(memory_space=pltpu.VMEM)] * 17,
        scratch_shapes=[pltpu.VMEM((576, C1), F32)] * 5 + [pltpu.VMEM((3456, 128), F32)],
        compiler_params=pltpu.CompilerParams(vmem_limit_bytes=36 << 20),
        name="fine_backward",
    )(
        gy, strip, strip_onehot(), *saved, wa, wp, g1.reshape(1, C1), we, wr,
        g2.reshape(1, C1), spread_onehot(6, 128),
    )


def table_kernel(par_ref, mine_ref, got_ref, fine_ref, coarse_ref, cols_f, cols_c):
    par = par_ref[0]
    cols_f[...] = jnp.zeros_like(cols_f)
    level = lax.broadcasted_iota(jnp.int32, (144, 128), 0) % 12 < 6
    for s in range(2):
        source = jnp.where(par == s, mine_ref[...].astype(F32), got_ref[...].astype(F32))
        for jm in range(6):
            tile = source[jm // 5 * 144 : jm // 5 * 144 + 144]
            if jm % 5:
                tile = pltpu.roll(tile, 128 - jm % 5 * 24, 1)
            base = s * 1728
            cols_f[pl.ds(base + jm, 144, stride=12), :] = jnp.where(level, tile, 0.0)
            cols_f[pl.ds(base + 6 + jm, 144, stride=12), :] = jnp.where(level, 0.0, tile)
        for b in range(12):
            tile = source[288 + b // 5 * 144 : 288 + b // 5 * 144 + 144]
            if b % 5:
                tile = pltpu.roll(tile, 128 - b % 5 * 24, 1)
            cols_c[pl.ds(s * 1728 + b, 144, stride=12), :] = tile
    for th in range(24):
        rows = slice(th * 144, (th + 1) * 144)
        fine_ref[th] = jnp.swapaxes(cols_f[rows, 0:24], 0, 1)[:23]
        coarse_ref[th] = jnp.swapaxes(cols_c[rows, 0:24], 0, 1)[:23]


def table_call(par, mine, got):
    shape = jax.ShapeDtypeStruct
    return pl.pallas_call(
        table_kernel,
        out_shape=(shape((24, 23, 144), F32), shape((24, 23, 144), F32)),
        in_specs=[pl.BlockSpec(memory_space=pltpu.SMEM)]
        + [pl.BlockSpec(memory_space=pltpu.VMEM)] * 2,
        scratch_shapes=[pltpu.VMEM((3456, 128), F32)] * 2,
        compiler_params=pltpu.CompilerParams(vmem_limit_bytes=24 << 20),
        name="table_gradients",
    )(par, mine, got)


def shifted(value, axis, steps):
    count = lax.axis_size(axis)
    return lax.ppermute(value, axis, [(s, (s + steps) % count) for s in range(count)])


def swapped(value):
    return lax.ppermute(value, "lon", [(s, s ^ 1) for s in range(lax.axis_size("lon"))])


def to_frame(value):
    half = value.shape[2] // 2
    strip = shifted(value[:, :, :half], "lon", -1)
    value = jnp.concatenate([value[:, :, half:], strip], axis=2)
    strip = shifted(value[:, :3], "lat", -1)
    return jnp.concatenate([value[:, 3:], strip], axis=1)


def from_frame(value):
    rows = value.shape[1]
    half = value.shape[2] // 2
    strip = shifted(value[:, rows - 3 :], "lat", 1)
    value = jnp.concatenate([strip, value[:, : rows - 3]], axis=1)
    strip = shifted(value[:, :, half:], "lon", 1)
    return jnp.concatenate([strip, value[:, :, :half]], axis=2)


def shards(
    tokens, fine_attend, fine_project, fine_gain_one, fine_expand, fine_reduce, fine_gain_two,
    fine_bias, merge_gain, merge_weight, coarse_attend, coarse_project, coarse_gain_one,
    coarse_expand, coarse_reduce, coarse_gain_two, coarse_bias, cotangent,
):
    fine_weights = (
        fine_attend, fine_project, fine_gain_one, fine_expand, fine_reduce, fine_gain_two,
    )
    coarse_weights = (
        coarse_attend, coarse_project, coarse_gain_one, coarse_expand, coarse_reduce,
        coarse_gain_two,
    )
    lon = lax.axis_index("lon")
    odd = lon % 2 == 1
    par = (lon % 2).astype(jnp.int32).reshape(1)
    last = (lax.axis_index("lat") == lax.axis_size("lat") - 1).astype(jnp.int32).reshape(1)

    def mine_of(first, second):
        return jnp.where(odd, second, first)

    bias_fine, bias_coarse = bias_call(par, fine_bias.reshape(24, 23, 144), coarse_bias)
    frame = to_frame(tokens).reshape(576, C1)
    cot = cotangent.reshape(2, 2, 36, C2)
    cot_keep = mine_of(cot[:, 0], cot[:, 1]).reshape(72, C2)
    cot_got = swapped(mine_of(cot[:, 1], cot[:, 0]).reshape(72, C2))

    y, *saved = fine_call(last, frame, fine_weights, bias_fine)
    strip = shifted(y.reshape(2, 288, C1)[:, 252:], "lat", 1).reshape(72, C1)
    pick = merge_onehot()
    coarse_in, quads = merge_call(y, strip, pick, merge_gain, merge_weight)
    cells = coarse_in.reshape(2, 2, 48, C2)
    from_left = shifted(cells[1], "lon", 1)
    both = jnp.stack([from_left, cells[0]])
    keep = mine_of(both[:, 0], both[:, 1]).reshape(96, C2)
    got = swapped(mine_of(both[:, 1], both[:, 0]).reshape(96, C2))
    out_keep, out_send, grad_keep, grad_send, table_coarse = coarse_call(
        par, keep, got, cot_keep, cot_got, coarse_weights, bias_coarse
    )
    grad_got = swapped(grad_send)
    first = mine_of(grad_keep, grad_got).reshape(2, 48, C2)
    second = mine_of(grad_got, grad_keep).reshape(2, 48, C2)
    both = jnp.stack([first, second], axis=1)
    from_right = shifted(both[0], "lon", -1)
    grad_in = jnp.stack([both[1], from_right]).reshape(192, C2)
    grad_y, grad_strip = merge_back_call(
        grad_in, quads, np.ascontiguousarray(pick.T), merge_gain, merge_weight
    )
    grad_strip = shifted(grad_strip, "lat", -1)
    grad_frame, table_fine = fine_back_call(grad_y, grad_strip, saved, fine_weights)

    out_got = swapped(out_send)
    top = mine_of(out_keep, out_got).reshape(2, 6, 2304)
    bottom = mine_of(out_got, out_keep).reshape(2, 6, 2304)
    coarse_out = jnp.concatenate([top, bottom], axis=1)

    half_got = swapped(mine_of(table_fine[144:], table_fine[:144]))
    half_sum = mine_of(table_fine[:144], table_fine[144:]).astype(F32) + half_got.astype(F32)
    half_sum = half_sum.astype(BF16)
    pieces = [half_sum[:, :128], half_sum[:, 128:]]
    pieces += [table_coarse[:, k * 128 : (k + 1) * 128] for k in range(3)]
    pieces += [jnp.zeros((48, 128), BF16)]
    partial = jnp.concatenate(pieces, axis=0).reshape(16, 48, 128)
    chips = [[2 * k + c for k in range(16)] for c in range(2)]
    partial = lax.all_to_all(partial, "lon", 0, 0, tiled=True, axis_index_groups=chips)
    total = jnp.sum(partial.astype(F32), axis=0).astype(BF16)
    spread = jnp.broadcast_to(total[None], (16, 48, 128))
    sums = lax.all_to_all(spread, "lon", 0, 0, tiled=True, axis_index_groups=chips)
    sums = sums.reshape(768, 128)
    grad_fine, grad_coarse = table_call(par, sums, swapped(sums))
    grad_tokens = from_frame(grad_frame.reshape(2, 24, 2304))
    return (
        coarse_out,
        grad_tokens,
        grad_fine.reshape(4, 6, 23, 144),
        grad_coarse.reshape(2, 12, 23, 144),
    )


def solution(mesh):
    rows = P(None, "lat", "lon")
    table = P("lat", None, None, None)
    in_specs = (rows,) + (P(),) * 6 + (table,) + (P(),) * 8 + (table, rows)
    return jax.shard_map(
        shards, mesh=mesh, in_specs=in_specs, out_specs=(rows, rows, table, table), check_vma=False
    )
```

time: 709 us -> 143 us (0.20); the launches traced: 695 us -> 142 us
  waiting for transfers between devices: 229 us -> 25 us
  local copies, waits for them, and re-layouts: 231 us -> 46 us
  matrix products: 133 us -> 0 us
  other arithmetic: 60 us -> 4.18 us
  Pallas kernels: 0 us -> 26.3 us
  between operations: 15.8 us -> 1.25 us
  starting transfers between devices: 26.7 us -> 39.1 us
    psum x1 -> x0, waiting for transfers between devices: 222 us -> none  [shards(): lax.psum(grad_fine_bias.astype(jnp.bfloat16), 'lon').astype(jnp.float32)]
    dot_general x32 -> x0, matrix products: 133 us -> none  [the longest x4 94.7 us: build_bias(): jnp.einsum('ghdab,dpq->ghapbq', shaped, offset_onehot(), precision=lax.Pr...]
    reshape x11 -> x9, local copies, waits for them, and re-layouts: 108 us -> 3.91 us  [the longest x1 1.68 us: shards(): cot = cotangent.reshape(2, 2, 36, C2)]
    transpose x10 -> x0, local copies, waits for them, and re-layouts: 41.6 us -> none  [the longest x1 32 us: build_bias(): jnp.einsum('ghdab,dpq->ghapbq', shaped, offset_onehot(), precision=lax.Pr...]
    select_n x11 -> x2, local copies, waits for them, and re-layouts: 31.6 us -> 2.92 us  [mine_of(): return jnp.where(odd, second, first)]
    pallas_call x0 -> x7, Pallas kernels: none -> 26.3 us  [the longest x1 8.2 us: coarse_call(): pl.pallas_call(coarse_kernel, out_shape=(shape((72, C2), BF16), shape((72...]
    unnamed x178 -> x122, local copies, waits for them, and re-layouts: 19.1 us -> 36 us
    convert_element_type x13 -> x0, local copies, waits for them, and re-layouts: 11.1 us -> none  [the longest x2 2.61 us: to_heads(): shaped = lax.optimization_barrier(block_data).astype(jnp.float32)]
  transfers between devices with their start and end apart: 11 -> 16, of which waited for: 5 -> 10; matrix products, arithmetic and copies ran while one was open for 39% -> 9% of each run, Pallas kernels for 0% -> 3%
where the time goes in v1:
time: 143 us; the launch traced here: 142 us
  local copies, waits for them, and re-layouts  46 us (32%)
  starting transfers between devices  39.1 us (27%)
  Pallas kernels  26.3 us (18%)
  waiting for transfers between devices  25 us (17%)
  other arithmetic  4.18 us (3%)
    unnamed x122, local copies, waits for them, and re-layouts  36 us
    ppermute x8, starting transfers between devices, shifted(): lax.ppermute(value, axis, [(s, (s + steps) % count) for s in range(count)])  19.8 us
    ppermute x8, waiting for transfers between devices, shifted(): lax.ppermute(value, axis, [(s, (s + steps) % count) for s in range(count)])  13.1 us
    ppermute x6, starting transfers between devices, swapped(): lax.ppermute(value, 'lon', [(s, s ^ 1) for s in range(lax.axis_size('lon'...  10.1 us
    pallas_call x1, Pallas kernels, coarse_call(): pl.pallas_call(coarse_kernel, out_shape=(shape((72, C2), BF16), shape((72...  8.2 us
    pallas_call x1, Pallas kernels, fine_back_call(): pl.pallas_call(fine_back_kernel, out_shape=(shape((576, C1), BF16), shape...  6.82 us
    all_to_all x1, waiting for transfers between devices, shards(): lax.all_to_all(partial, 'lon', 0, 0, tiled=True, axis_index_groups=chips)  5.71 us
    all_to_all x1, starting transfers between devices, shards(): lax.all_to_all(spread, 'lon', 0, 0, tiled=True, axis_index_groups=chips)  5.5 us
  transfers between devices with their start and end apart: 16, of which 10 were waited for; matrix products, arithmetic and copies ran while one was open for 9% of the time, Pallas kernels for 3%

profile of v1, /device:TPU:1, one launch (start us, length us, event | category | flops | bytes accessed | tf_op | source)
XLA Modules:
  0.0 141.9 jit_solution(16161370286759765506)
XLA Ops:
  1.8 3.3 %collective-permute-start = (bf16[2,24,1152]{2,1,0:T(8,128)(2,1)S(1)}, bf16[2,24,1152]{2,1,0:T(8,128)(2,1)S(1)}, u32[]{:S(2)}, u32[]{:S(2)}) collective-permute-start(bf16[2,24,1152]{2,1,0:T(8,128)(2,1)S(1)} %get-tuple-element.59), channel_id=1, source_target_pairs={{0,248},{8,0},{16,8},{24,16},{32,24},{40,32},{48,40},{56,48},{64,5... | collective-permute-start | bytes 331784 | tf_op jit(solution)/shard_map/ppermute | solution.py:552
  6.5 1.7 %copy-done.1 = bf16[12,384,256]{2,1,0:T(8,128)(2,1)S(1)} copy-done((bf16[12,384,256]{2,1,0:T(8,128)(2,1)S(1)}, bf16[12,384,256]{2,1,0:T(8,128)(2,1)}, u32[]{:S(2)}) %copy-start.1) | copy-done | bytes 2359320
  8.2 3.6 %bias_spread.1 = (f32[3456,128]{1,0:T(8,128)S(1)}, f32[2,1728,128]{2,1,0:T(8,128)S(1)}) custom-call(s32[1]{0:T(128)} %bitcast.par_ref, f32[24,23,144]{2,1,0:T(8,128)S(1)} %bitcast.28, f32[2,12,23,144]{3,2,1,0:T(8,128)S(1)} %copy.43.coarse_ref, bf16[12,256,128]{2,1,0:T(8,128)(2,1)S(1)} %copy-done, bf16[12,384,256]{2,1,0:T(8,128)(2,1)S(1)} %copy-done.1), custom_call_target="tpu_custom_call" | custom-call | tf_op jit(solution)/shard_map/bias_spread/pallas_call | solution.py:201
  14.3 3.5 %collective-permute-start.1 = (bf16[2,3,2304]{2,1,0:T(4,128)(2,1)S(1)}, bf16[2,3,2304]{2,1,0:T(4,128)(2,1)S(1)}, u32[]{:S(2)}, u32[]{:S(2)}) collective-permute-start(bf16[2,3,2304]{2,1,0:T(4,128)(2,1)S(1)} %pad_maximum_fusion.6), channel_id=1, source_target_pairs={{0,7},{1,0},{2,1},{3,2},{4,3},{5,4},{6,5},{7,6},{8,15},{9,8},{10,9... | collective-permute-start | bytes 82952 | tf_op jit(solution)/shard_map/ppermute | solution.py:552
  19.3 1.5 %copy-done.6 = f32[3456,128]{1,0:T(8,128)S(1)} copy-done((f32[3456,128]{1,0:T(8,128)S(1)}, f32[3456,128]{1,0:T(8,128)}, u32[]{:S(2)}) %copy-start.6) | copy-done | bytes 1769496
  20.8 4.3 %fine_forward.1 = (bf16[576,192]{1,0:T(8,128)(2,1)S(1)}, f32[576,192]{1,0:T(8,128)S(1)}, f32[576,192]{1,0:T(8,128)S(1)}, f32[576,192]{1,0:T(8,128)S(1)}, bf16[34...) custom-call(s32[1]{0:T(128)} %bitcast.1.last_ref, ...), custom_call_target="tpu_custom_call" | custom-call | tf_op jit(solution)/shard_map/fine_forward/pallas_call | solution.py:257
  31.8 2.0 %collective-permute-start.2 = (bf16[2,36,192]{2,1,0:T(8,128)(2,1)S(1)}, bf16[2,36,192]{2,1,0:T(8,128)(2,1)S(1)}, u32[]{:S(2)}, u32[]{:S(2)}) collective-permute-start(bf16[2,36,192]{2,1,0:T(8,128)(2,1)S(1)} %slice.109), channel_id=1, source_target_pairs={{0,1},{1,2},{2,3},{3,4},{4,5},{5,6},{6,7},{7,0},{8,9},{9,10},{10,1... | collective-permute-start | bytes 82952 | tf_op jit(solution)/shard_map/ppermute | solution.py:552
  33.8 4.7 %collective-permute-done.2 = bf16[2,36,192]{2,1,0:T(8,128)(2,1)S(1)} collective-permute-done((bf16[2,36,192]{2,1,0:T(8,128)(2,1)S(1)}, bf16[2,36,192]{2,1,0:T(8,128)(2,1)S(1)}, u32[]{:S(2)}, u32[]{:S(2)}) %collective-permute-start.2) | collective-permute-done | bytes 27680 | tf_op jit(solution)/shard_map/ppermute | solution.py:552
  40.2 1.3 copy-done.11
  43.2 1.4 merge_forward.1
  46.0 3.6 %collective-permute-start.3 = (bf16[2,48,384]{2,1,0:T(8,128)(2,1)}, bf16[2,48,384]{2,1,0:T(8,128)(2,1)}, u32[]{:S(2)}, u32[]{:S(2)}) collective-permute-start(bf16[2,48,384]{2,1,0:T(8,128)(2,1)} %bitcast.6), channel_id=1, source_target_pairs={{0,8},{8,16},{16,24},{24,32},{32,40},{40,48},{48,56},{56,64},{64,7... | collective-permute-start | bytes 221192 | tf_op jit(solution)/shard_map/ppermute | solution.py:552
  49.6 1.6 %copy.46 = bf16[2,12,2304]{2,1,0:T(8,128)(2,1)} copy(bf16[2,12,2304]{2,0,1:T(2,128)(2,1)} %param.44) | data formatting | bytes 221184 | tf_op args[17]
  51.2 1.7 %reshape.108 = bf16[2,2,36,384]{3,2,1,0:T(8,128)(2,1)} reshape(bf16[2,12,2304]{2,1,0:T(8,128)(2,1)} %copy.46) | data formatting | bytes 221184 | tf_op jit(solution)/shard_map/reshape | solution.py:598
  52.8 2.3 %collective-permute-done.3 = bf16[2,48,384]{2,1,0:T(8,128)(2,1)} collective-permute-done((bf16[2,48,384]{2,1,0:T(8,128)(2,1)}, bf16[2,48,384]{2,1,0:T(8,128)(2,1)}, u32[]{:S(2)}, u32[]{:S(2)}) %collective-permute-start.3) | collective-permute-done | bytes 73760 | tf_op jit(solution)/shard_map/ppermute | solution.py:552
  55.2 1.6 %broadcast_select_fusion.3 = (bf16[2,1,48,384]{3,2,0,1:T(8,128)(2,1)}, bf16[2,1,48,384]{3,2,0,1:T(8,128)(2,1)}) fusion(pred[]{:T(512)S(6)} %eq.9, bf16[1,2,48,384]{3,2,0,1:T(8,128)(2,1)} %bitcast.42, bf16[1,2,48,384]{3,2,0,1:T(8,128)(2,1)} %bitcast.7), kind=kLoop, calls=%fused_computation.22 | loop fusion | flops 184320 | bytes 294913 | tf_op jit(solution)/shard_map/jit(_where)/select_n | solution.py:594
  56.7 5.1 %collective-permute-start.4 = (bf16[96,384]{1,0:T(8,128)(2,1)}, bf16[96,384]{1,0:T(8,128)(2,1)}, u32[]{:S(2)}, u32[]{:S(2)}) collective-permute-start(bf16[96,384]{1,0:T(8,128)(2,1)} %bitcast.11), channel_id=1, source_target_pairs={{0,8},{8,0},{16,24},{24,16},{32,40},{40,32},{48,56},{56,48},{64,72... | collective-permute-start | bytes 221192 | tf_op jit(solution)/shard_map/ppermute | solution.py:556
  61.8 1.5 %broadcast_select_fusion.5 = (bf16[2,1,36,384]{3,2,1,0:T(8,128)(2,1)}, bf16[2,1,36,384]{3,2,1,0:T(8,128)(2,1)}) fusion(pred[]{:T(512)S(6)} %eq.9, bf16[2,2,36,384]{3,2,1,0:T(8,128)(2,1)} %reshape.108), kind=kLoop, calls=%fused_computation.24 | loop fusion | flops 55296 | bytes 221185 | tf_op jit(solution)/shard_map/jit(_where)/select_n | solution.py:594
  63.3 1.5 %select_n.96 = bf16[72,384]{1,0:T(8,128)(2,1)} reshape(bf16[2,1,36,384]{3,2,1,0:T(8,128)(2,1)} %get-tuple-element.68) | data formatting | bytes 110592 | tf_op jit(solution)/shard_map/jit(_where)/select_n | solution.py:594
  64.8 1.5 %select_n.94.ckeep_ref = bf16[72,384]{1,0:T(8,128)(2,1)} reshape(bf16[2,1,36,384]{3,2,1,0:T(8,128)(2,1)} %get-tuple-element.69) | data formatting | bytes 110592 | tf_op jit(solution)/shard_map/jit(_where)/select_n | solution.py:594
  67.0 1.5 %copy-done.8 = f32[2,1728,128]{2,1,0:T(8,128)S(1)} copy-done((f32[2,1728,128]{2,1,0:T(8,128)S(1)}, f32[2,1728,128]{2,1,0:T(8,128)}, u32[]{:S(2)}) %copy-start.8) | copy-done | bytes 1769496
  68.5 1.3 copy-done.12
  76.7 8.2 %coarse_both.1 = (bf16[72,384]{1,0:T(8,128)(2,1)S(1)}, bf16[72,384]{1,0:T(8,128)(2,1)S(1)}, bf16[96,384]{1,0:T(8,128)(2,1)S(1)}, bf16[96,384]{1,0:T(8,128)(2,1)S(1)}, bf16[144,384]{1,0:T(8,128)(2,1)S(1)}) custom-call(s32[1]{0:T(128)} %bitcast.par_ref, bf16[96,384]{1,0:T(8,128)(2,1)S(1)} %bitcast.35, bf16[96,384]{1,0:T(8,128)(2,1)} %collective-permute-done.4.got_ref, ...), custom_call_target="tpu_custom_call" | custom-call | tf_op jit(solution)/shard_map/coarse_both/pallas_call | solution.py:387
  87.0 3.4 %collective-permute-done.8 = bf16[2,48,384]{2,1,0:T(8,128)(2,1)S(1)} collective-permute-done((bf16[2,48,384]{2,1,0:T(8,128)(2,1)S(1)}, bf16[2,48,384]{2,1,0:T(8,128)(2,1)S(1)}, u32[]{:S(2)}, u32[]{:S(2)}) %collective-permute-start.8) | collective-permute-done | bytes 73760 | tf_op jit(solution)/shard_map/ppermute | solution.py:552
  91.5 3.5 %collective-permute-start.9 = (bf16[72,192]{1,0:T(8,128)(2,1)S(1)}, bf16[72,192]{1,0:T(8,128)(2,1)S(1)}, u32[]{:S(2)}, u32[]{:S(2)}) collective-permute-start(bf16[72,192]{1,0:T(8,128)(2,1)S(1)} %get-tuple-element.37), channel_id=1, source_target_pairs={{0,7},{1,0},{2,1},{3,2},{4,3},{5,4},{6,5},{7,6},{8,15},{9,8},{10,9... | collective-permute-start | bytes 82952 | tf_op jit(solution)/shard_map/ppermute | solution.py:552
  95.1 1.6 %collective-permute-done.9.strip_ref = bf16[72,192]{1,0:T(8,128)(2,1)S(1)} collective-permute-done((bf16[72,192]{1,0:T(8,128)(2,1)S(1)}, bf16[72,192]{1,0:T(8,128)(2,1)S(1)}, u32[]{:S(2)}, u32[]{:S(2)}) %collective-permute-start.9) | collective-permute-done | bytes 27680 | tf_op jit(solution)/shard_map/ppermute | solution.py:552
  96.8 6.8 %fine_backward.1 = (bf16[576,192]{1,0:T(8,128)(2,1)S(1)}, bf16[288,256]{1,0:T(8,128)(2,1)S(1)}) custom-call(bf16[576,192]{1,0:T(8,128)(2,1)S(1)} %get-tuple-element.36.gy_ref, bf16[72,192]{1,0:T(8,128)(2,1)S(1)} %collective-permute-done.9.strip_ref, bf16[576,72]{1,0:T(8,128)(2,1)S(1)} %copy-done.41, f32[576,192]{1,0:T(8,128)S(1)} %copy-done.23, ...), custom_call_target="tpu_custom_call" | custom-call | tf_op jit(solution)/shard_map/fine_backward/pallas_call | solution.py:500
  108.8 3.8 %all-to-all-start = ((bf16[16,48,128]{2,1,0:T(8,128)(2,1)}), bf16[16,48,128]{2,1,0:T(8,128)(2,1)S(1)}, u32[]{:S(2)}, u32[]{:S(2)}) async-start(bf16[16,48,128]{2,1,0:T(8,128)(2,1)} %bitcast.19), calls=%async_computation | async-start | bytes 393216 | tf_op jit(solution)/shard_map/all_to_all | solution.py:639
  114.4 5.7 %all-to-all-done = bf16[16,48,128]{2,1,0:T(8,128)(2,1)S(1)} async-done(((bf16[16,48,128]{2,1,0:T(8,128)(2,1)}), bf16[16,48,128]{2,1,0:T(8,128)(2,1)S(1)}, u32[]{:S(2)}, u32[]{:S(2)}) %all-to-all-start) | async-done | bytes 196640 | tf_op jit(solution)/shard_map/all_to_all | solution.py:639
  120.9 5.5 %all-to-all-start.1 = ((bf16[16,48,128]{2,1,0:T(8,128)(2,1)}), bf16[16,48,128]{2,1,0:T(8,128)(2,1)S(1)}, u32[]{:S(2)}, u32[]{:S(2)}) async-start(bf16[16,48,128]{2,1,0:T(8,128)(2,1)} %broadcast_in_dim.10), calls=%async_computation.1 | async-start | bytes 393216 | tf_op jit(solution)/shard_map/all_to_all | solution.py:642
  126.5 2.7 %collective-permute-start.11 = (bf16[2,24,1152]{2,1,0:T(8,128)(2,1)S(1)}, bf16[2,24,1152]{2,1,0:T(8,128)(2,1)S(1)}, u32[]{:S(2)}, u32[]{:S(2)}) collective-permute-start(bf16[2,24,1152]{2,1,0:T(8,128)(2,1)S(1)} %fusion.1), channel_id=1, source_target_pairs={{0,8},{8,16},{16,24},{24,32},{32,40},{40,48},{48,56},{56,64},{64,7... | collective-permute-start | bytes 331784 | tf_op jit(solution)/shard_map/ppermute | solution.py:552
  129.9 4.0 %all-to-all-done.1 = bf16[16,48,128]{2,1,0:T(8,128)(2,1)S(1)} async-done(((bf16[16,48,128]{2,1,0:T(8,128)(2,1)}), bf16[16,48,128]{2,1,0:T(8,128)(2,1)S(1)}, u32[]{:S(2)}, u32[]{:S(2)}) %all-to-all-start.1) | async-done | bytes 196640 | tf_op jit(solution)/shard_map/all_to_all | solution.py:642
  134.0 3.4 %collective-permute-start.13 = (bf16[768,128]{1,0:T(8,128)(2,1)S(1)}, bf16[768,128]{1,0:T(8,128)(2,1)S(1)}, u32[]{:S(2)}, u32[]{:S(2)}) collective-permute-start(bf16[768,128]{1,0:T(8,128)(2,1)S(1)} %bitcast.29), channel_id=1, source_target_pairs={{0,8},{8,0},{16,24},{24,16},{32,40},{40,32},{48,56},{56,48},{64,72... | collective-permute-start | bytes 589832 | tf_op jit(solution)/shard_map/ppermute | solution.py:556
  (161 shorter events, 41.8 us)
Async XLA Ops:
  1.8 12.5 %collective-permute-start = (bf16[2,24,1152]{2,1,0:T(8,128)(2,1)S(1)}, bf16[2,24,1152]{2,1,0:T(8,128)(2,1)S(1)}, u32[]{:S(2)}, u32[]{:S(2)}) collective-permute-start(bf16[2,24,1152]{2,1,0:T(8,128)(2,1)S(1)} %get-tuple-element.59), channel_id=1, source_target_pairs={{0,248},{8,0},{16,8},{24,16},{32,24},{40,32},{48,40},{56,48},{64,5... | collective-permute-start | bytes 331784 | tf_op jit(solution)/shard_map/ppermute | solution.py:552
  14.3 4.5 %collective-permute-start.1 = (bf16[2,3,2304]{2,1,0:T(4,128)(2,1)S(1)}, bf16[2,3,2304]{2,1,0:T(4,128)(2,1)S(1)}, u32[]{:S(2)}, u32[]{:S(2)}) collective-permute-start(bf16[2,3,2304]{2,1,0:T(4,128)(2,1)S(1)} %pad_maximum_fusion.6), channel_id=1, source_target_pairs={{0,7},{1,0},{2,1},{3,2},{4,3},{5,4},{6,5},{7,6},{8,15},{9,8},{10,9... | collective-permute-start | bytes 82952 | tf_op jit(solution)/shard_map/ppermute | solution.py:552
  18.9 14.9 %copy-start.53 = (f32[768]{0:T(1024)S(1)}, f32[768]{0:T(1024)}, u32[]{:S(2)}) copy-start(f32[768]{0:T(1024)} %param.35) | copy-start | bytes 9220
  31.8 6.8 %collective-permute-start.2 = (bf16[2,36,192]{2,1,0:T(8,128)(2,1)S(1)}, bf16[2,36,192]{2,1,0:T(8,128)(2,1)S(1)}, u32[]{:S(2)}, u32[]{:S(2)}) collective-permute-start(bf16[2,36,192]{2,1,0:T(8,128)(2,1)S(1)} %slice.109), channel_id=1, source_target_pairs={{0,1},{1,2},{2,3},{3,4},{4,5},{5,6},{6,7},{7,0},{8,9},{9,10},{10,1... | collective-permute-start | bytes 82952 | tf_op jit(solution)/shard_map/ppermute | solution.py:552
  43.2 23.0 %copy-start.54 = (f32[384]{0:T(512)S(1)}, f32[384]{0:T(512)}, u32[]{:S(2)}) copy-start(f32[384]{0:T(512)} %param.39) | copy-start | bytes 4612
  43.2 23.7 %copy-start.2 = (bf16[12,384,144]{2,1,0:T(8,128)(2,1)S(1)}, bf16[12,384,144]{2,1,0:T(8,128)(2,1)}, u32[]{:S(2)}) copy-start(bf16[12,384,144]{2,1,0:T(8,128)(2,1)} %constant.52.clone.ec_ref) | copy-start | bytes 3981316
  46.0 9.1 %collective-permute-start.3 = (bf16[2,48,384]{2,1,0:T(8,128)(2,1)}, bf16[2,48,384]{2,1,0:T(8,128)(2,1)}, u32[]{:S(2)}, u32[]{:S(2)}) collective-permute-start(bf16[2,48,384]{2,1,0:T(8,128)(2,1)} %bitcast.6), channel_id=1, source_target_pairs={{0,8},{8,16},{16,24},{24,32},{32,40},{40,48},{48,56},{56,64},{64,7... | collective-permute-start | bytes 221192 | tf_op jit(solution)/shard_map/ppermute | solution.py:552
  56.7 10.3 %collective-permute-start.4 = (bf16[96,384]{1,0:T(8,128)(2,1)}, bf16[96,384]{1,0:T(8,128)(2,1)}, u32[]{:S(2)}, u32[]{:S(2)}) collective-permute-start(bf16[96,384]{1,0:T(8,128)(2,1)} %bitcast.11), channel_id=1, source_target_pairs={{0,8},{8,0},{16,24},{24,16},{32,40},{40,32},{48,56},{56,48},{64,72... | collective-permute-start | bytes 221192 | tf_op jit(solution)/shard_map/ppermute | solution.py:556
  64.8 2.2 %collective-permute-start.5 = (bf16[72,384]{1,0:T(8,128)(2,1)}, bf16[72,384]{1,0:T(8,128)(2,1)}, u32[]{:S(2)}, u32[]{:S(2)}) collective-permute-start(bf16[72,384]{1,0:T(8,128)(2,1)} %select_n.96), channel_id=1, source_target_pairs={{0,8},{8,0},{16,24},{24,16},{32,40},{40,32},{48,56},{56,48},{64,72... | collective-permute-start | bytes 165896 | tf_op jit(solution)/shard_map/ppermute | solution.py:556
  76.6 13.8 %copy-start.4 = (bf16[768,384]{1,0:T(8,128)(2,1)S(1)}, bf16[768,384]{1,0:T(8,128)(2,1)}, u32[]{:S(2)}) copy-start(bf16[768,384]{1,0:T(8,128)(2,1)} %w_ref.3) | copy-start | bytes 1769476
  76.6 13.8 %copy-start.14 = (bf16[648,768]{1,0:T(8,128)(2,1)S(1)}, bf16[648,768]{1,0:T(8,128)(2,1)}, u32[]{:S(2)}) copy-start(bf16[648,768]{1,0:T(8,128)(2,1)} %constant.53.clone.place_ref) | copy-start | bytes 2985988
  76.6 13.8 %copy-start.33 = (bf16[768,192]{1,0:T(8,128)(2,1)S(1)}, bf16[768,192]{1,0:T(8,128)(2,1)}, u32[]{:S(2)}) copy-start(bf16[768,192]{1,0:T(8,128)(2,1)} %copy-done.32) | copy-start | bytes 884740
  76.7 20.0 %copy-start.25 = (f32[576,192]{1,0:T(8,128)S(1)}, f32[576,192]{1,0:T(8,128)}, u32[]{:S(2)}) copy-start(f32[576,192]{1,0:T(8,128)} %copy-done.24) | copy-start | bytes 1327108
  76.7 20.0 %copy-start.27 = (f32[576,192]{1,0:T(8,128)S(1)}, f32[576,192]{1,0:T(8,128)}, u32[]{:S(2)}) copy-start(f32[576,192]{1,0:T(8,128)} %copy-done.26) | copy-start | bytes 1327108
  76.7 20.0 %copy-start.29 = (f32[576,192]{1,0:T(8,128)S(1)}, f32[576,192]{1,0:T(8,128)}, u32[]{:S(2)}) copy-start(f32[576,192]{1,0:T(8,128)} %copy-done.28) | copy-start | bytes 1327108
  76.7 20.0 %copy-start.31 = (f32[576,192]{1,0:T(8,128)S(1)}, f32[576,192]{1,0:T(8,128)}, u32[]{:S(2)}) copy-start(f32[576,192]{1,0:T(8,128)} %copy-done.30) | copy-start | bytes 1327108
  76.7 20.0 %copy-start.41 = (bf16[576,72]{1,0:T(8,128)(2,1)S(1)}, bf16[576,72]{1,0:T(8,128)(2,1)}, u32[]{:S(2)}) copy-start(bf16[576,72]{1,0:T(8,128)(2,1)} %constant.54.clone.place_ref) | copy-start | bytes 248836
  84.9 11.8 %copy-start.10 = (bf16[192,768]{1,0:T(8,128)(2,1)S(1)}, bf16[192,768]{1,0:T(8,128)(2,1)}, u32[]{:S(2)}) copy-start(bf16[192,768]{1,0:T(8,128)(2,1)} %we_ref.5) | copy-start | bytes 884740
  84.9 11.8 %copy-start.16 = (bf16[192,576]{1,0:T(8,128)(2,1)S(1)}, bf16[192,576]{1,0:T(8,128)(2,1)}, u32[]{:S(2)}) copy-start(bf16[192,576]{1,0:T(8,128)(2,1)} %wa_ref.5) | copy-start | bytes 663556
  85.0 11.8 %copy-start.19 = (bf16[3456,72]{1,0:T(8,128)(2,1)S(1)}, bf16[3456,72]{1,0:T(8,128)(2,1)}, u32[]{:S(2)}) copy-start(bf16[3456,72]{1,0:T(8,128)(2,1)} %copy-done.18) | copy-start | bytes 1492996
  85.0 11.8 %copy-start.21 = (bf16[576,768]{1,0:T(8,128)(2,1)S(1)}, bf16[576,768]{1,0:T(8,128)(2,1)}, u32[]{:S(2)}) copy-start(bf16[576,768]{1,0:T(8,128)(2,1)} %copy-done.20) | copy-start | bytes 2654212
  85.0 1.5 %collective-permute-start.7 = (bf16[96,384]{1,0:T(8,128)(2,1)S(1)}, bf16[96,384]{1,0:T(8,128)(2,1)S(1)}, u32[]{:S(2)}, u32[]{:S(2)}) collective-permute-start(bf16[96,384]{1,0:T(8,128)(2,1)S(1)} %get-tuple-element.33), channel_id=1, source_target_pairs={{0,8},{8,0},{16,24},{24,16},{32,40},{40,32},{48,56},{56,48},{64,72... | collective-permute-start | bytes 221192 | tf_op jit(solution)/shard_map/ppermute | solution.py:556
  86.6 3.9 %collective-permute-start.8 = (bf16[2,48,384]{2,1,0:T(8,128)(2,1)S(1)}, bf16[2,48,384]{2,1,0:T(8,128)(2,1)S(1)}, u32[]{:S(2)}, u32[]{:S(2)}) collective-permute-start(bf16[2,48,384]{2,1,0:T(8,128)(2,1)S(1)} %get-tuple-element.61), channel_id=1, source_target_pairs={{0,248},{8,0},{16,8},{24,16},{32,24},{40,32},{48,40},{56,48},{64,5... | collective-permute-start | bytes 221192 | tf_op jit(solution)/shard_map/ppermute | solution.py:552
  91.5 5.2 %collective-permute-start.9 = (bf16[72,192]{1,0:T(8,128)(2,1)S(1)}, bf16[72,192]{1,0:T(8,128)(2,1)S(1)}, u32[]{:S(2)}, u32[]{:S(2)}) collective-permute-start(bf16[72,192]{1,0:T(8,128)(2,1)S(1)} %get-tuple-element.37), channel_id=1, source_target_pairs={{0,7},{1,0},{2,1},{3,2},{4,3},{5,4},{6,5},{7,6},{8,15},{9,8},{10,9... | collective-permute-start | bytes 82952 | tf_op jit(solution)/shard_map/ppermute | solution.py:552
  96.8 15.8 %copy-start.50 = (bf16[72,384]{1,0:T(8,128)(2,1)S(1)}, bf16[72,384]{1,0:T(8,128)(2,1)}, u32[]{:S(2)}) copy-start(bf16[72,384]{1,0:T(8,128)(2,1)} %copy-done.49) | copy-start | bytes 165892
  103.6 1.4 collective-permute-start.12
  108.8 11.4 %all-to-all-start = ((bf16[16,48,128]{2,1,0:T(8,128)(2,1)}), bf16[16,48,128]{2,1,0:T(8,128)(2,1)S(1)}, u32[]{:S(2)}, u32[]{:S(2)}) async-start(bf16[16,48,128]{2,1,0:T(8,128)(2,1)} %bitcast.19), calls=%async_computation | async-start | bytes 393216 | tf_op jit(solution)/shard_map/all_to_all | solution.py:639
  112.6 1.7 %collective-permute-start.6 = (bf16[72,384]{1,0:T(8,128)(2,1)S(1)}, bf16[72,384]{1,0:T(8,128)(2,1)S(1)}, u32[]{:S(2)}, u32[]{:S(2)}) collective-permute-start(bf16[72,384]{1,0:T(8,128)(2,1)S(1)} %copy-done.50), channel_id=1, source_target_pairs={{0,8},{8,0},{16,24},{24,16},{32,40},{40,32},{48,56},{56,48},{64,72... | collective-permute-start | bytes 165896 | tf_op jit(solution)/shard_map/ppermute | solution.py:556
  113.4 13.0 %collective-permute-start.10 = (bf16[2,3,2304]{2,1,0:T(4,128)(2,1)S(1)}, bf16[2,3,2304]{2,1,0:T(4,128)(2,1)S(1)}, u32[]{:S(2)}, u32[]{:S(2)}) collective-permute-start(bf16[2,3,2304]{2,1,0:T(4,128)(2,1)S(1)} %slice.116), channel_id=1, source_target_pairs={{0,1},{1,2},{2,3},{3,4},{4,5},{5,6},{6,7},{7,0},{8,9},{9,10},{10,1... | collective-permute-start | bytes 82952 | tf_op jit(solution)/shard_map/ppermute | solution.py:552
  120.9 13.1 %all-to-all-start.1 = ((bf16[16,48,128]{2,1,0:T(8,128)(2,1)}), bf16[16,48,128]{2,1,0:T(8,128)(2,1)S(1)}, u32[]{:S(2)}, u32[]{:S(2)}) async-start(bf16[16,48,128]{2,1,0:T(8,128)(2,1)} %broadcast_in_dim.10), calls=%async_computation.1 | async-start | bytes 393216 | tf_op jit(solution)/shard_map/all_to_all | solution.py:642
  126.5 10.9 %collective-permute-start.11 = (bf16[2,24,1152]{2,1,0:T(8,128)(2,1)S(1)}, bf16[2,24,1152]{2,1,0:T(8,128)(2,1)S(1)}, u32[]{:S(2)}, u32[]{:S(2)}) collective-permute-start(bf16[2,24,1152]{2,1,0:T(8,128)(2,1)S(1)} %fusion.1), channel_id=1, source_target_pairs={{0,8},{8,16},{16,24},{24,32},{32,40},{40,48},{48,56},{56,64},{64,7... | collective-permute-start | bytes 331784 | tf_op jit(solution)/shard_map/ppermute | solution.py:552
  134.0 4.5 %collective-permute-start.13 = (bf16[768,128]{1,0:T(8,128)(2,1)S(1)}, bf16[768,128]{1,0:T(8,128)(2,1)S(1)}, u32[]{:S(2)}, u32[]{:S(2)}) collective-permute-start(bf16[768,128]{1,0:T(8,128)(2,1)S(1)} %bitcast.29), channel_id=1, source_target_pairs={{0,8},{8,0},{16,24},{24,16},{32,40},{40,32},{48,56},{56,48},{64,72... | collective-permute-start | bytes 589832 | tf_op jit(solution)/shard_map/ppermute | solution.py:556
  (39 other events, 126.4 us)

commit v2 on v1

v2 whole, which is shorter than its diff:
```python
import functools
import math

import jax
import jax.numpy as jnp
import numpy as np
from jax import lax
from jax.experimental import pallas as pl
from jax.experimental.pallas import tpu as pltpu
from jax.sharding import PartitionSpec as P

C1 = 192
C2 = 384
HD = 32
H1 = 6
H2 = 12
WLON = 12
HALF = 72
EPSILON = 1e-05
MASKED = -1000000000.0
SCALE = 1.0 / math.sqrt(HD)
F32 = jnp.float32
BF16 = jnp.bfloat16


def pair_lane(pair):
    return pair // 5 * 128 + pair % 5 * 24


def spread_onehot(pairs, lanes):
    onehot = np.zeros((WLON, (pairs + 4) // 5 * 128, lanes), np.float32)
    for p in range(WLON):
        for b in range(pairs):
            for q in range(WLON):
                onehot[p, pair_lane(b) + p - q + WLON - 1, b * WLON + q] = 1.0
    return onehot.astype(jnp.bfloat16)


def merge_onehot():
    onehot = np.zeros((4, 2, 2, 48, 648), np.float32)
    for rr in range(2):
        for cc in range(2):
            for bh in range(2):
                for lam in range(2):
                    for z in range(2):
                        for a in range(6):
                            for b in range(3):
                                row = 2 * (lam * 6 + a) + rr
                                col = 2 * (bh * 3 + b) + cc
                                if row < 3:
                                    cell = 576 + z * 36 + row * 12 + col
                                elif row < 21:
                                    cell = z * 216 + (row - 3) * 12 + col
                                else:
                                    cell = 432 + z * 72 + (row - 21) * 12 + col
                                onehot[rr * 2 + cc, bh, lam, z * 18 + a * 3 + b, cell] = 1.0
    return onehot.reshape(768, 648).astype(jnp.bfloat16)


def strip_onehot():
    onehot = np.zeros((144, 72), np.float32)
    for z in range(2):
        for k in range(36):
            onehot[z * 72 + 36 + k, z * 36 + k] = 1.0
    return onehot.astype(jnp.bfloat16)


def nn(left, right):
    return lax.dot_general(left, right, (((1,), (0,)), ((), ())), preferred_element_type=F32)


def nt(left, right):
    return lax.dot_general(left, right, (((1,), (1,)), ((), ())), preferred_element_type=F32)


def tn(left, right):
    return lax.dot_general(left, right, (((0,), (0,)), ((), ())), preferred_element_type=F32)


def norm_parts(values):
    average = jnp.mean(values, axis=-1, keepdims=True)
    centred = values - average
    scale = lax.rsqrt(jnp.mean(centred * centred, axis=-1, keepdims=True) + EPSILON)
    return centred * scale, scale


def norm_back(grad, normed, scale):
    first = jnp.mean(grad, axis=-1, keepdims=True)
    second = jnp.mean(grad * normed, axis=-1, keepdims=True)
    return scale * (grad - first - normed * second)


def split3(values):
    high = values.astype(BF16)
    rest = values - high.astype(F32)
    mid = rest.astype(BF16)
    low = (rest - mid.astype(F32)).astype(BF16)
    return high, mid, low


def head_mask(rows, heads, width):
    row = lax.broadcasted_iota(jnp.int32, (heads * rows, width), 0) // rows
    lane = lax.broadcasted_iota(jnp.int32, (heads * rows, width), 1) // HD
    return (row == lane).astype(F32)


def heads_stack(values, heads, mask):
    return (jnp.concatenate([values] * heads, axis=0) * mask).astype(BF16)


def heads_fold(stacked, heads, mask):
    rows = stacked.shape[0] // heads
    kept = stacked * mask
    total = kept[:rows]
    for h in range(1, heads):
        total = total + kept[h * rows : (h + 1) * rows]
    return total


def gelu_parts(values):
    phi = 0.5 * (1.0 + lax.erf(values * (1.0 / math.sqrt(2.0))))
    density = jnp.exp(-0.5 * values * values) * (1.0 / math.sqrt(2.0 * math.pi))
    return values * phi, phi + values * density


def softmax(scores):
    top = jnp.max(scores, axis=-1, keepdims=True)
    powers = jnp.exp(scores - top)
    return powers / jnp.sum(powers, axis=-1, keepdims=True)


def vmem(count):
    return [pl.BlockSpec(memory_space=pltpu.VMEM)] * count


def cost(microseconds):
    return pl.CostEstimate(
        flops=int(microseconds * 1e9), bytes_accessed=int(microseconds * 1e6), transcendentals=0
    )


def parity():
    return lax.rem(lax.axis_index("lon"), 2)


def fine_bias_kernel(table_ref, out_ref, cols_ref):
    key = lax.broadcasted_iota(jnp.int32, (256, 128), 0)
    lane = lax.broadcasted_iota(jnp.int32, (256, 128), 1)
    place = key % 128
    pair = key // 128 * 5 + place // 24
    meets = jnp.logical_and(pair == lane // 12, place < 120)
    column = jnp.where(meets, place % 24 + lane % 12 - (WLON - 1), -1)
    cols_ref[...] = jnp.zeros_like(cols_ref)
    for th in range(24):
        cols_ref[th * 144 : (th + 1) * 144, 0:23] = jnp.swapaxes(
            table_ref[th % 6, :, th // 6, :], 0, 1
        )
    low_level = lax.broadcasted_iota(jnp.int32, (288, 128), 0) % 12 < 6
    tiles = []
    for t in range(2):
        tile = None
        for jm in range(t * 5, min(t * 5 + 5, 6)):
            piece = jnp.where(
                low_level,
                cols_ref[pl.ds(jm, 288, stride=12), :],
                cols_ref[pl.ds(6 + jm, 288, stride=12), :],
            )
            if jm % 5:
                piece = pltpu.roll(piece, jm % 5 * 24, 1)
            tile = piece if tile is None else tile + piece
        tiles.append(tile)
    parts = jnp.concatenate(split3(jnp.concatenate(tiles, axis=1)), axis=0)
    for p in range(WLON):
        spread = nn(parts, (column == p).astype(F32).astype(BF16))
        out_ref[pl.ds(p, 288, stride=12), :] = spread[:288] + spread[288:576] + spread[576:]


def fine_bias_call(table):
    return pl.pallas_call(
        fine_bias_kernel,
        out_shape=jax.ShapeDtypeStruct((3456, 128), F32),
        in_specs=vmem(1),
        scratch_shapes=[pltpu.VMEM((3456, 128), F32)],
        compiler_params=pltpu.CompilerParams(vmem_limit_bytes=10 << 20),
        cost_estimate=cost(2),
        name="fine_bias_spread",
    )(table)


def coarse_bias_kernel(table_ref, onehot_ref, out_ref, cols_ref):
    cols_ref[...] = jnp.zeros_like(cols_ref)
    par = parity()
    for h in range(12):
        cols_ref[h * 144 : (h + 1) * 144, 0:23] = jnp.swapaxes(
            jnp.where(par == 0, table_ref[h, :, 0, :], table_ref[h, :, 1, :]), 0, 1
        )
    tiles = []
    for t in range(3):
        tile = None
        for b in range(t * 5, min(t * 5 + 5, 12)):
            piece = cols_ref[pl.ds(b, 144, stride=12), :]
            if b % 5:
                piece = pltpu.roll(piece, b % 5 * 24, 1)
            tile = piece if tile is None else tile + piece
        tiles.append(tile)
    parts = jnp.concatenate(split3(jnp.concatenate(tiles, axis=1)), axis=0)
    for p in range(WLON):
        spread = nn(parts, onehot_ref[p])
        total = spread[:144] + spread[144:288] + spread[288:]
        out_ref[0, pl.ds(p, 144, stride=12), :] = total[:, :128]
        out_ref[1, pl.ds(p, 144, stride=12), :] = total[:, 128:]


def coarse_bias_call(table, onehot):
    return pl.pallas_call(
        coarse_bias_kernel,
        out_shape=jax.ShapeDtypeStruct((2, 1728, 128), F32),
        in_specs=vmem(2),
        scratch_shapes=[pltpu.VMEM((1728, 128), F32)],
        compiler_params=pltpu.CompilerParams(vmem_limit_bytes=10 << 20),
        cost_estimate=cost(2),
        name="coarse_bias_spread",
    )(table, onehot)


def split_kernel(
    far_tok_ref, table_ref, left_ref, top_ref, corner_ref, near_ref, tok_ref, tok_sem, table_sem
):
    half = left_ref.shape[2]
    tok_copy = pltpu.make_async_copy(far_tok_ref, tok_ref, tok_sem)
    table_copy = pltpu.make_async_copy(table_ref, near_ref, table_sem)
    tok_copy.start()
    table_copy.start()
    tok_copy.wait()
    left_ref[...] = tok_ref[:, :, :half]
    for z in range(2):
        rows = tok_ref[z].astype(F32)[:3]
        top_ref[z] = rows[:, half:].astype(BF16)
        corner_ref[z] = rows[:, :half].astype(BF16)
    table_copy.wait()


def split_call(tokens, table):
    levels, rows, width = tokens.shape
    shape = jax.ShapeDtypeStruct
    return pl.pallas_call(
        split_kernel,
        out_shape=(
            shape((levels, rows, width // 2), BF16),
            shape((levels, 3, width // 2), BF16),
            shape((levels, 3, width // 2), BF16),
            shape(table.shape, F32),
        ),
        in_specs=[pl.BlockSpec(memory_space=pl.ANY)] * 2,
        scratch_shapes=[
            pltpu.VMEM(tokens.shape, BF16),
            pltpu.SemaphoreType.DMA,
            pltpu.SemaphoreType.DMA,
        ],
        compiler_params=pltpu.CompilerParams(vmem_limit_bytes=4 << 20),
        cost_estimate=cost(1),
        name="left_half",
    )(tokens, table)


def fine_kernel(windows, *refs):
    edge = windows[-1] == 3
    refs = list(refs)
    tok_ref, col_ref = refs[:2]
    top_ref, corner_ref = refs[2:4] if edge else (None, None)
    refs = refs[4:] if edge else refs[2:]
    wa_ref, wp_ref, g1_ref, we_ref, wr_ref, g2_ref, bias_ref, y_ref = refs[:8]
    strip_ref = refs[8] if edge else None
    refs = refs[9:] if edge else refs[8:]
    qkv_ref, a_ref, att_ref, slope_ref, red_ref = refs[:5]
    q_ref, k_ref, v_ref, o_ref, grid_ref, low_ref, high_ref, x_ref, edge_ref = refs[5:]
    rows = 6 * len(windows)
    own = rows - 3 if edge else rows
    start = 3 + 6 * windows[0]
    half = grid_ref.shape[1] // 2
    for z in range(2):
        base = z * rows
        grid_ref[base : base + own, :half] = tok_ref[z].astype(F32)[start : start + own, half:]
        grid_ref[base : base + own, half:] = col_ref[z].astype(F32)[start : start + own]
        if edge:
            grid_ref[base + own : base + rows, :half] = top_ref[z].astype(F32)
            grid_ref[base + own : base + rows, half:] = corner_ref[z].astype(F32)
    for col in range(WLON):
        piece = grid_ref[:, col * C1 : (col + 1) * C1]
        places = pl.ds(col, 2 * rows, stride=WLON)
        low_ref[places, :] = piece[:, :128]
        high_ref[places, :] = jnp.concatenate([piece[:, 128:]] * 2, axis=1)
    x_ref[...] = jnp.concatenate([low_ref[...], high_ref[:, :64]], axis=1)
    x = x_ref[...].astype(BF16)
    for part, wide_ref in enumerate((q_ref, k_ref, v_ref)):
        short = nn(x, wa_ref[:, part * C1 : (part + 1) * C1]).astype(BF16)
        qkv_ref[part] = short
        wide_ref[...] = short.astype(F32)
    mask = head_mask(HALF, H1, C1)
    last = lax.axis_index("lat") == lax.axis_size("lat") - 1
    for z in range(2):
        for n, w in enumerate(windows):
            block = z * len(windows) + n
            cells = slice(block * 72, block * 72 + 72)
            qs = heads_stack(q_ref[cells, :], H1, mask)
            places = [((w * 6 + h) * 2 + 1 - z) * 72 for h in range(H1)]
            bias = jnp.concatenate([bias_ref[s : s + 72, :] for s in places], axis=0)[:, :72]
            scores = nt(qs, k_ref[cells, :].astype(BF16)) * SCALE + bias
            if w == 3:
                row = lax.broadcasted_iota(jnp.int32, scores.shape, 0) % 72 < 36
                col = lax.broadcasted_iota(jnp.int32, scores.shape, 1) < 36
                scores = jnp.where(jnp.logical_and(row != col, last), MASKED, scores)
            weights = softmax(scores).astype(BF16)
            a_ref[block * 432 : (block + 1) * 432, :] = weights
            o_ref[cells, :] = heads_fold(nn(weights, v_ref[cells, :].astype(BF16)), H1, mask)
    for c in range(len(windows)):
        cells = slice(c * 144, (c + 1) * 144)
        att = nn(o_ref[cells, :].astype(BF16), wp_ref[...])
        att_ref[cells, :] = att
        normed, _ = norm_parts(att)
        middle = (x_ref[cells, :] + g1_ref[...][None, :] * normed).astype(BF16)
        act, slope = gelu_parts(nn(middle, we_ref[...]))
        slope_ref[cells, :] = slope.astype(BF16)
        red = nt(act.astype(BF16), wr_ref[...])
        red_ref[cells, :] = red
        normed, _ = norm_parts(red)
        out = middle.astype(F32) + g2_ref[...][None, :] * normed
        y_ref[cells, :] = out.astype(BF16)
        if edge:
            edge_ref[0:36, :] = out[36:72]
            edge_ref[36:72, :] = out[108:]
    if edge:
        strip_ref[...] = edge_ref[...].astype(BF16)


def fine_call(windows, cells, weights, bias):
    wa, wp, g1, we, wr, g2 = weights
    shape = jax.ShapeDtypeStruct
    count = len(windows)
    edge = windows[-1] == 3
    total = 144 * count
    return pl.pallas_call(
        functools.partial(fine_kernel, windows),
        out_shape=(shape((total, C1), BF16),)
        + ((shape((72, C1), BF16),) if edge else ())
        + (
            shape((3, total, C1), BF16),
            shape((count * 864, 72), BF16),
            shape((total, C1), F32),
            shape((total, 4 * C1), BF16),
            shape((total, C1), F32),
        ),
        in_specs=vmem(len(cells) + 7),
        scratch_shapes=[pltpu.VMEM((total, C1), F32)] * 4
        + [
            pltpu.VMEM((12 * count, WLON * C1), F32),
            pltpu.VMEM((total, 128), F32),
            pltpu.VMEM((total, 128), F32),
            pltpu.VMEM((total, C1), F32),
            pltpu.VMEM((72, C1), F32),
        ],
        compiler_params=pltpu.CompilerParams(vmem_limit_bytes=14 << 20),
        cost_estimate=cost(count + 0.5),
        name=f"fine_forward_{count}",
    )(*cells, wa, wp, g1, we, wr, g2, bias)


def merge_kernel(y_ref, last_ref, strip_ref, pick_ref, gain_ref, w_ref, both_ref, right_ref, f_ref):
    gain = gain_ref[...][None, :]
    cells = jnp.concatenate([y_ref[...], last_ref[...], strip_ref[...]], axis=0)
    f = nn(pick_ref[...], cells)
    f_ref[...] = f.astype(BF16)
    total = sum(jnp.sum(f[k * 192 : (k + 1) * 192], axis=-1, keepdims=True) for k in range(4))
    average = total * (1.0 / 768)
    centred = [f[k * 192 : (k + 1) * 192] - average for k in range(4)]
    square = sum(jnp.sum(c * c, axis=-1, keepdims=True) for c in centred)
    scale = lax.rsqrt(square * (1.0 / 768) + EPSILON)
    result = None
    for k in range(4):
        normed = (gain[:, k * C1 : (k + 1) * C1] * (centred[k] * scale)).astype(BF16)
        part = nn(normed, w_ref[k * 192 : (k + 1) * 192, :])
        result = part if result is None else result + part
    both_ref[...] = result.astype(BF16)
    right_ref[...] = result[96:].astype(BF16)


def merge_call(y, last, strip, pick, gain, weight):
    shape = jax.ShapeDtypeStruct
    return pl.pallas_call(
        merge_kernel,
        out_shape=(shape((192, C2), BF16), shape((96, C2), BF16), shape((768, C1), BF16)),
        in_specs=vmem(6),
        compiler_params=pltpu.CompilerParams(vmem_limit_bytes=8 << 20),
        cost_estimate=cost(1.5),
        name="merge_forward",
    )(y, last, strip, pick, gain, weight)


def window_places(par):
    row = lax.broadcasted_iota(jnp.int32, (144, 576), 0)
    z, a, c = row // 72, row // 12 % 6, row % 12
    group = c // 3
    even = jnp.where(group == 0, 4, jnp.where(group == 1, 0, jnp.where(group == 2, 1, 2)))
    odd = jnp.where(group == 0, 5, jnp.where(group == 1, 2, jnp.where(group == 2, 3, 0)))
    source = jnp.where(par == 0, even, odd)
    place = source * 96 + par * 48 + z * 18 + a * 3 + c % 3
    return (place == lax.broadcasted_iota(jnp.int32, (144, 576), 1)).astype(F32).astype(BF16)


def half_places(par):
    row = lax.broadcasted_iota(jnp.int32, (144, 24), 0)
    z, a, c = row // 72, row // 12 % 6, row % 12
    match = (z * 12 + par * 6 + a == lax.broadcasted_iota(jnp.int32, (144, 24), 1)).astype(F32)
    places = []
    for side in (par, 1 - par):
        places.append(
            [jnp.where(c == side * 6 + col, match, 0.0).astype(BF16) for col in range(6)]
        )
    return places


def coarse_kernel(
    both_ref, pboth_ref, even_ref, odd_ref, seed_ref, pseed_ref,
    wa_ref, wp_ref, g1_ref, we_ref, wr_ref, g2_ref, bias_ref,
    gboth_ref, gpboth_ref, geven_ref, godd_ref, out_ref, ds_ref,
    a_ref, qs_ref, o_ref, slope_ref, band_ref,
):
    par = parity()
    pick = window_places(par)
    half = half_places(par)
    cells = [both_ref[...], pboth_ref[...], even_ref[...], odd_ref[...]]
    x = nn(pick, jnp.concatenate(cells, axis=0)).astype(BF16)
    for side, source_ref in enumerate((seed_ref, pseed_ref)):
        wide = source_ref[...].astype(F32)
        for z in range(2):
            band_ref[side, z * 12 : (z + 1) * 12, :] = wide[:, z, :]
    seed = None
    for side in range(2):
        for col in range(6):
            part = nn(half[side][col], band_ref[side, :, col * C2 : (col + 1) * C2].astype(BF16))
            seed = part if seed is None else seed + part
    ds_ref[1] = jnp.zeros_like(ds_ref[1])
    packed = nn(x, wa_ref[...]).astype(BF16)
    mask = head_mask(144, 4, 128)
    for g in range(3):
        lanes = slice(g * 128, (g + 1) * 128)
        rows = slice(g * 576, (g + 1) * 576)
        qs = heads_stack(packed[:, lanes].astype(F32), 4, mask)
        qs_ref[rows, :] = qs
        key = packed[:, C2 + g * 128 : C2 + (g + 1) * 128]
        value = packed[:, 2 * C2 + g * 128 : 2 * C2 + (g + 1) * 128]
        bias = jnp.concatenate([bias_ref[0, rows, :], bias_ref[1, rows, :]], axis=1)[:, :144]
        weights = softmax(nt(qs, key) * SCALE + bias).astype(BF16)
        a_ref[rows, :] = weights
        o_ref[:, lanes] = heads_fold(nn(weights, value), 4, mask)
    att = nn(o_ref[...].astype(BF16), wp_ref[...])
    normed1, scale1 = norm_parts(att)
    middle = (x.astype(F32) + g1_ref[...][None, :] * normed1).astype(BF16)
    act, slope = gelu_parts(nn(middle, we_ref[...]))
    slope_ref[...] = slope
    red = nn(act.astype(BF16), wr_ref[...])
    normed2, scale2 = norm_parts(red)
    out_ref[...] = (middle.astype(F32) + g2_ref[...][None, :] * normed2).astype(BF16)
    grad_red = norm_back(seed * g2_ref[...][None, :], normed2, scale2).astype(BF16)
    grad_act = nt(grad_red, wr_ref[...]).astype(BF16).astype(F32)
    grad_exp = (grad_act * slope_ref[...]).astype(BF16)
    grad_middle = (seed + nt(grad_exp, we_ref[...]).astype(BF16).astype(F32)).astype(BF16)
    grad_middle = grad_middle.astype(F32)
    grad_att = norm_back(grad_middle * g1_ref[...][None, :], normed1, scale1).astype(BF16)
    grad_o = nt(grad_att, wp_ref[...]).astype(BF16)
    grad_x = grad_middle
    for g in range(3):
        lanes = slice(g * 128, (g + 1) * 128)
        rows = slice(g * 576, (g + 1) * 576)
        os = heads_stack(grad_o[:, lanes].astype(F32), 4, mask)
        key = packed[:, C2 + g * 128 : C2 + (g + 1) * 128]
        value = packed[:, 2 * C2 + g * 128 : 2 * C2 + (g + 1) * 128]
        weights = a_ref[rows, :]
        grad_a = nt(os, value)
        wide = weights.astype(F32)
        grad_s = wide * (grad_a - jnp.sum(wide * grad_a, axis=-1, keepdims=True))
        ds_ref[0, rows, :] = grad_s[:, :128]
        ds_ref[1, rows, 0:16] = grad_s[:, 128:]
        short = grad_s.astype(BF16)
        grad_v = tn(weights, os).astype(BF16)
        grad_q = (heads_fold(nn(short, key), 4, mask) * SCALE).astype(BF16)
        grad_k = (tn(short, qs_ref[rows, :]) * SCALE).astype(BF16)
        grad_x = grad_x + nt(grad_q, wa_ref[:, g * 128 : (g + 1) * 128])
        grad_x = grad_x + nt(grad_k, wa_ref[:, C2 + g * 128 : C2 + (g + 1) * 128])
        grad_x = grad_x + nt(grad_v, wa_ref[:, 2 * C2 + g * 128 : 2 * C2 + (g + 1) * 128])
    parted = tn(pick, grad_x.astype(BF16)).astype(BF16)
    gboth_ref[...] = parted[:192]
    gpboth_ref[...] = parted[192:384]
    geven_ref[...] = parted[384:480]
    godd_ref[...] = parted[480:]


def coarse_rest_kernel(out_ref, ds_ref, ec_ref, okeep_ref, osend_ref, dt_ref, cells_ref):
    half = half_places(parity())
    out = out_ref[...]
    for col in range(6):
        lanes = slice(col * C2, (col + 1) * C2)
        for side in range(2):
            part = tn(half[side][col], out)
            for z in range(2):
                cells_ref[side, :, z, lanes] = part[z * 12 : (z + 1) * 12]
    okeep_ref[...] = cells_ref[0].astype(BF16)
    osend_ref[...] = cells_ref[1].astype(BF16)
    table = None
    for p in range(WLON):
        places = pl.ds(p, 144, stride=12)
        piece = jnp.concatenate([ds_ref[0, places, :], ds_ref[1, places, :]], axis=1).astype(BF16)
        part = nt(piece, ec_ref[p])
        table = part if table is None else table + part
    for t in range(3):
        dt_ref[t * 144 : (t + 1) * 144, :] = table[:, t * 128 : (t + 1) * 128].astype(BF16)


def coarse_rest_call(out, ds, ec):
    shape = jax.ShapeDtypeStruct
    return pl.pallas_call(
        coarse_rest_kernel,
        out_shape=(
            shape((12, 2, 6 * C2), BF16),
            shape((12, 2, 6 * C2), BF16),
            shape((432, 128), BF16),
        ),
        in_specs=vmem(3),
        scratch_shapes=[pltpu.VMEM((2, 12, 2, 6 * C2), F32)],
        compiler_params=pltpu.CompilerParams(vmem_limit_bytes=10 << 20),
        cost_estimate=cost(1.5),
        name="coarse_rest",
    )(out, ds, ec)


def coarse_call(cells, seeds, weights, bias):
    wa, wp, g1, we, wr, g2 = weights
    shape = jax.ShapeDtypeStruct
    return pl.pallas_call(
        coarse_kernel,
        out_shape=(
            shape((192, C2), BF16),
            shape((192, C2), BF16),
            shape((96, C2), BF16),
            shape((96, C2), BF16),
            shape((144, C2), BF16),
            shape((2, 1728, 128), F32),
        ),
        in_specs=vmem(13),
        scratch_shapes=[
            pltpu.VMEM((1728, 144), BF16),
            pltpu.VMEM((1728, 128), BF16),
            pltpu.VMEM((144, C2), F32),
            pltpu.VMEM((144, 4 * C2), F32),
            pltpu.VMEM((2, 24, 6 * C2), F32),
        ],
        compiler_params=pltpu.CompilerParams(vmem_limit_bytes=20 << 20),
        cost_estimate=cost(7),
        name="coarse_both",
    )(*cells, *seeds, wa, wp, g1, we, wr, g2, bias)


def merge_back_kernel(_, g_ref, pg_ref, even_ref, odd_ref, f_ref, place_ref, gain_ref, w_ref, gy_ref, glast_ref, gstrip_ref):
    f = f_ref[...].astype(F32)
    total = sum(jnp.sum(f[k * 192 : (k + 1) * 192], axis=-1, keepdims=True) for k in range(4))
    average = total * (1.0 / 768)
    centred = [f[k * 192 : (k + 1) * 192] - average for k in range(4)]
    square = sum(jnp.sum(c * c, axis=-1, keepdims=True) for c in centred)
    scale = lax.rsqrt(square * (1.0 / 768) + EPSILON)
    gain = gain_ref[...][None, :]
    both = g_ref[...].astype(F32) + pg_ref[...].astype(F32)
    right = both[96:] + even_ref[...].astype(F32) + odd_ref[...].astype(F32)
    g = jnp.concatenate([both[:96], right], axis=0).astype(BF16)
    normed = [c * scale for c in centred]
    grads = []
    for k in range(4):
        part = nt(g, w_ref[k * 192 : (k + 1) * 192, :]).astype(BF16).astype(F32)
        grads.append(part * gain[:, k * C1 : (k + 1) * C1])
    first = sum(jnp.sum(p, axis=-1, keepdims=True) for p in grads) * (1.0 / 768)
    second = sum(jnp.sum(p * n, axis=-1, keepdims=True) for p, n in zip(grads, normed))
    second = second * (1.0 / 768)
    back = [(scale * (p - first - n * second)).astype(BF16) for p, n in zip(grads, normed)]
    placed = nn(place_ref[...], jnp.concatenate(back, axis=0)).astype(BF16)
    gy_ref[...] = placed[:432]
    glast_ref[...] = placed[432:576]
    gstrip_ref[...] = placed[576:]


def merge_back_call(after, grads, f, place, gain, weight):
    shape = jax.ShapeDtypeStruct
    return pl.pallas_call(
        merge_back_kernel,
        out_shape=(shape((432, C1), BF16), shape((144, C1), BF16), shape((72, C1), BF16)),
        in_specs=[pl.BlockSpec(memory_space=pl.ANY)] + vmem(8),
        compiler_params=pltpu.CompilerParams(vmem_limit_bytes=8 << 20),
        cost_estimate=cost(1),
        name="merge_backward",
    )(after, *grads, f, place, gain, weight)


def fine_back_kernel(windows, *refs):
    edge = windows[-1] == 3
    count = len(windows)
    refs = list(refs)
    gy_ref = refs.pop(0)
    if edge:
        strip_ref, place_ref, table_ref, body_ref = refs[:4]
        refs = refs[4:]
    qkv_ref, a_ref, att_ref, slope_ref, red_ref = refs[:5]
    wa_ref, wp_ref, g1_ref, we_ref, wr_ref, g2_ref, ef_ref = refs[5:12]
    refs = refs[12:]
    if edge:
        own_ref, last_ref, keep_ref, send_ref = refs[:4]
        refs = refs[4:]
    else:
        gx_ref, dt_ref = refs[:2]
        refs = refs[2:]
    low_ref, high_ref, grid_ref, q_ref, k_ref, v_ref = refs[:6]
    gm_ref, go_ref, dq_ref, dk_ref, dv_ref, ds_ref = refs[6:12]
    for part, wide_ref in enumerate((q_ref, k_ref, v_ref)):
        wide_ref[...] = qkv_ref[part].astype(F32)
    ds_ref[...] = jnp.zeros_like(ds_ref)
    for c in range(count):
        cells = slice(c * 144, (c + 1) * 144)
        seed = gy_ref[cells, :].astype(F32)
        if edge:
            seed = seed + nn(place_ref[...], strip_ref[...])
        normed, scale = norm_parts(red_ref[cells, :])
        grad_red = norm_back(seed * g2_ref[...][None, :], normed, scale).astype(BF16)
        grad_act = nn(grad_red, wr_ref[...]).astype(BF16).astype(F32)
        grad_exp = (grad_act * slope_ref[cells, :].astype(F32)).astype(BF16)
        grad_middle = seed + nt(grad_exp, we_ref[...]).astype(BF16).astype(F32)
        grad_middle = grad_middle.astype(BF16).astype(F32)
        gm_ref[cells, :] = grad_middle
        normed, scale = norm_parts(att_ref[cells, :])
        grad_att = norm_back(grad_middle * g1_ref[...][None, :], normed, scale).astype(BF16)
        go_ref[cells, :] = nt(grad_att, wp_ref[...]).astype(BF16).astype(F32)
    mask = head_mask(HALF, H1, C1)
    for z in range(2):
        for n in range(count):
            block = z * count + n
            cells = slice(block * 72, block * 72 + 72)
            os = heads_stack(go_ref[cells, :], H1, mask)
            qs = heads_stack(q_ref[cells, :], H1, mask)
            weights = a_ref[block * 432 : (block + 1) * 432, :]
            grad_a = nt(os, v_ref[cells, :].astype(BF16))
            wide = weights.astype(F32)
            grad_s = wide * (grad_a - jnp.sum(wide * grad_a, axis=-1, keepdims=True))
            for h in range(H1):
                place = ((n * 6 + h) * 2 + 1 - z) * 72
                ds_ref[place : place + 72, 0:72] = grad_s[h * 72 : (h + 1) * 72]
            short = grad_s.astype(BF16)
            dv_ref[cells, :] = tn(weights, os)
            dq_ref[cells, :] = heads_fold(nn(short, k_ref[cells, :].astype(BF16)), H1, mask) * SCALE
            dk_ref[cells, :] = tn(short, qs) * SCALE
    table = None
    for p in range(WLON):
        piece = ds_ref[pl.ds(p, 72 * count, stride=12), :].astype(BF16)
        part = nt(piece, ef_ref[p])
        table = part if table is None else table + part
    if edge:
        first = parity() == 0
        whole = jnp.concatenate([table_ref[...], table], axis=0)
        for half_ref, taken in ((keep_ref, first), (send_ref, jnp.logical_not(first))):
            half = jnp.where(taken, whole[:144], whole[144:]).astype(BF16)
            half_ref[:144, :] = half[:, :128]
            half_ref[144:, :] = half[:, 128:]
    else:
        dt_ref[...] = table
    total = gm_ref[...]
    total = total + nt(dq_ref[...].astype(BF16), wa_ref[:, :C1])
    total = total + nt(dk_ref[...].astype(BF16), wa_ref[:, C1 : 2 * C1])
    total = total + nt(dv_ref[...].astype(BF16), wa_ref[:, 2 * C1 :])
    low_ref[...] = total[:, :128]
    high_ref[:, 0:64] = total[:, 128:]
    rows = 6 * count
    for col in range(WLON):
        lanes = slice(col * C1, (col + 1) * C1)
        low = low_ref[pl.ds(col, 2 * rows, stride=WLON), :]
        high = high_ref[pl.ds(col, 2 * rows, stride=WLON), :]
        grid_ref[:, lanes] = jnp.concatenate([low, high[:, :64]], axis=1)
    for z in range(2):
        band = grid_ref[z * rows : (z + 1) * rows, :]
        if edge:
            own_ref[z] = jnp.concatenate([body_ref[z].astype(F32), band[:3]], axis=0).astype(BF16)
            last_ref[z] = band[3:].astype(BF16)
        else:
            gx_ref[z] = band.astype(BF16)


def fine_back_call(windows, grads, saved, weights, ef):
    wa, wp, g1, we, wr, g2 = weights
    shape = jax.ShapeDtypeStruct
    count = len(windows)
    total = 144 * count
    width = WLON * C1
    if windows[-1] == 3:
        outs = (shape((2, 21, width), BF16), shape((2, 3, width), BF16))
        outs = outs + (shape((288, 128), BF16),) * 2
    else:
        outs = (shape((2, 6 * count, width), BF16), shape((72 * count, 256), F32))
    return pl.pallas_call(
        functools.partial(fine_back_kernel, windows),
        out_shape=outs,
        in_specs=vmem(len(grads) + 12),
        scratch_shapes=[pltpu.VMEM((total, 128), F32)] * 2
        + [pltpu.VMEM((12 * count, width), F32)]
        + [pltpu.VMEM((total, C1), F32)] * 8
        + [pltpu.VMEM((864 * count, 128), F32)],
        compiler_params=pltpu.CompilerParams(vmem_limit_bytes=16 << 20),
        cost_estimate=cost(2 * count),
        name=f"fine_backward_{count}",
    )(*grads, *saved, wa, wp, g1, we, wr, g2, ef)


def partial_kernel(keep_ref, got_ref, coarse_ref, out_ref):
    out_ref[:288, :] = (keep_ref[...].astype(F32) + got_ref[...].astype(F32)).astype(BF16)
    out_ref[288:720, :] = coarse_ref[...]
    out_ref[720:, :] = jnp.zeros((48, 128), BF16)


def partial_call(keep, got, coarse):
    return pl.pallas_call(
        partial_kernel,
        out_shape=jax.ShapeDtypeStruct((768, 128), BF16),
        in_specs=vmem(3),
        compiler_params=pltpu.CompilerParams(vmem_limit_bytes=4 << 20),
        cost_estimate=cost(0.5),
        name="partial_sums",
    )(keep, got, coarse)


def sum_kernel(parts_ref, out_ref):
    total = jnp.sum(parts_ref[...].astype(F32), axis=0, keepdims=True).astype(BF16)
    out_ref[...] = jnp.broadcast_to(total, out_ref.shape)


def sum_call(parts):
    return pl.pallas_call(
        sum_kernel,
        out_shape=jax.ShapeDtypeStruct(parts.shape, BF16),
        in_specs=vmem(1),
        compiler_params=pltpu.CompilerParams(vmem_limit_bytes=4 << 20),
        cost_estimate=cost(0.7),
        name="chip_sums",
    )(parts)


def table_kernel(
    mine_ref, got_ref, okeep_ref, ogot_ref, out_ref, fine_ref, coarse_ref, cols_f, cols_c
):
    par = parity()
    out_ref[...] = (okeep_ref[...].astype(F32) + ogot_ref[...].astype(F32)).astype(BF16)
    level = lax.broadcasted_iota(jnp.int32, (144, 128), 0) % 12 < 6
    for s in range(2):
        source = jnp.where(par == s, mine_ref[...].astype(F32), got_ref[...].astype(F32))
        for jm in range(6):
            tile = source[jm // 5 * 144 : jm // 5 * 144 + 144]
            if jm % 5:
                tile = pltpu.roll(tile, 128 - jm % 5 * 24, 1)
            base = s * 1728
            cols_f[pl.ds(base + jm, 144, stride=12), :] = jnp.where(level, tile, 0.0)
            cols_f[pl.ds(base + 6 + jm, 144, stride=12), :] = jnp.where(level, 0.0, tile)
        for b in range(12):
            tile = source[288 + b // 5 * 144 : 288 + b // 5 * 144 + 144]
            if b % 5:
                tile = pltpu.roll(tile, 128 - b % 5 * 24, 1)
            cols_c[pl.ds(s * 1728 + b, 144, stride=12), :] = tile
    for th in range(24):
        rows = slice(th * 144, (th + 1) * 144)
        fine_ref[th % 6, :, th // 6, :] = jnp.swapaxes(cols_f[rows, 0:24], 0, 1)[:23]
        coarse_ref[th % 12, :, th // 12, :] = jnp.swapaxes(cols_c[rows, 0:24], 0, 1)[:23]


def table_call(mine, got, okeep, ogot):
    shape = jax.ShapeDtypeStruct
    return pl.pallas_call(
        table_kernel,
        out_shape=(
            shape((12, 2, 6 * C2), BF16),
            shape((6, 23, 4, 144), F32),
            shape((12, 23, 2, 144), F32),
        ),
        in_specs=vmem(4),
        scratch_shapes=[pltpu.VMEM((3456, 128), F32)] * 2,
        compiler_params=pltpu.CompilerParams(vmem_limit_bytes=10 << 20),
        cost_estimate=cost(2),
        name="results",
    )(mine, got, okeep, ogot)


def shifted(value, axis, steps):
    count = lax.axis_size(axis)
    return lax.ppermute(value, axis, [(s, (s + steps) % count) for s in range(count)])


def diagonal(value, steps):
    lon, lat = lax.axis_size("lon"), lax.axis_size("lat")
    pairs = [
        (a * lat + b, (a + steps) % lon * lat + (b + steps) % lat)
        for a in range(lon)
        for b in range(lat)
    ]
    return lax.ppermute(value, ("lon", "lat"), pairs)


def swapped(value):
    return lax.ppermute(value, "lon", [(s, s ^ 1) for s in range(lax.axis_size("lon"))])


def shards(
    tokens, fine_attend, fine_project, fine_gain_one, fine_expand, fine_reduce, fine_gain_two,
    fine_bias, merge_gain, merge_weight, coarse_attend, coarse_project, coarse_gain_one,
    coarse_expand, coarse_reduce, coarse_gain_two, coarse_bias, cotangent,
):
    fine_weights = (
        fine_attend, fine_project, fine_gain_one, fine_expand, fine_reduce.T, fine_gain_two,
    )
    coarse_weights = (
        coarse_attend, coarse_project, coarse_gain_one, coarse_expand, coarse_reduce,
        coarse_gain_two,
    )
    ef = spread_onehot(6, 128)
    ec = spread_onehot(12, 256)
    pick = merge_onehot()
    seed = jnp.transpose(cotangent, (1, 0, 2))
    seeds = (seed, swapped(seed))
    cols, top, corner, table = split_call(tokens, jnp.transpose(fine_bias, (1, 2, 0, 3)))
    cols = shifted(cols, "lon", -1)
    top = shifted(top, "lat", -1)
    corner = diagonal(corner, -1)
    bias_fine = fine_bias_call(table)
    bias_coarse = coarse_bias_call(jnp.transpose(coarse_bias, (1, 2, 0, 3)), ec)

    most, final = (0, 1, 2), (3,)
    y_last, strip, *saved_last = fine_call(
        final, (tokens, cols, top, corner), fine_weights, bias_fine
    )
    strip = shifted(strip, "lat", 1)
    y_most, *saved_most = fine_call(most, (tokens, cols), fine_weights, bias_fine)
    both, right, quads = merge_call(y_most, y_last, strip, pick, merge_gain, merge_weight)
    cells = (both, swapped(both), shifted(right, "lon", 1), shifted(right, "lon", 2))
    grad_both, grad_pboth, grad_even, grad_odd, out, grad_scores = coarse_call(
        cells, seeds, coarse_weights, bias_coarse
    )
    grads = (
        grad_both,
        swapped(grad_pboth),
        shifted(grad_even, "lon", -1),
        shifted(grad_odd, "lon", -2),
    )
    out_keep, out_send, table_coarse = coarse_rest_call(out, grad_scores, ec)
    grad_most, grad_last, grad_strip = merge_back_call(
        table_coarse, grads, quads, np.ascontiguousarray(pick.T), merge_gain, merge_weight
    )
    grad_strip = shifted(grad_strip, "lat", -1)
    body, table_most = fine_back_call(most, (grad_most,), saved_most, fine_weights, ef)
    grads = (grad_last, grad_strip, strip_onehot(), table_most, body)
    own, edge, table_keep, table_send = fine_back_call(
        final, grads, saved_last, fine_weights, ef
    )
    partial = partial_call(table_keep, swapped(table_send), table_coarse).reshape(16, 48, 128)
    chips = [[2 * k + c for k in range(16)] for c in range(2)]
    partial = lax.all_to_all(partial, "lon", 0, 0, tiled=True, axis_index_groups=chips)
    sums = lax.all_to_all(sum_call(partial), "lon", 0, 0, tiled=True, axis_index_groups=chips)
    sums = sums.reshape(768, 128)
    coarse_out, grad_fine, grad_coarse = table_call(
        sums, swapped(sums), out_keep, swapped(out_send)
    )
    band = jnp.concatenate([shifted(edge, "lat", 1), own], axis=1)
    half = band.shape[2] // 2
    grad_tokens = jnp.concatenate(
        [shifted(band[:, :, half:], "lon", 1), band[:, :, :half]], axis=2
    )
    return (
        jnp.transpose(coarse_out, (1, 0, 2)),
        grad_tokens,
        jnp.transpose(grad_fine, (2, 0, 1, 3)),
        jnp.transpose(grad_coarse, (2, 0, 1, 3)),
    )


def solution(mesh):
    rows = P(None, "lat", "lon")
    table = P("lat", None, None, None)
    in_specs = (rows,) + (P(),) * 6 + (table,) + (P(),) * 8 + (table, rows)
    return jax.shard_map(
        shards, mesh=mesh, in_specs=in_specs, out_specs=(rows, rows, table, table), check_vma=False
    )
```

time: 143 us -> 96.5 us (0.67)
  the two profiles are of different devices: /device:TPU:1 before, /device:TPU:8 now
where the time goes in v2:
time: 96.5 us; the launch traced here: 96.3 us
  Pallas kernels  31.1 us (32%)
  starting transfers between devices  26.5 us (27%)
  waiting for transfers between devices  20.1 us (21%)
  blocking collectives  14.5 us (15%)
  local copies, waits for them, and re-layouts  2.11 us (2%)
  between operations  1.09 us (1%)
    ppermute x10, waiting for transfers between devices, shifted(): lax.ppermute(value, axis, [(s, (s + steps) % count) for s in range(count)])  18.9 us
    ppermute x10, starting transfers between devices, shifted(): lax.ppermute(value, axis, [(s, (s + steps) % count) for s in range(count)])  14.7 us
    all_to_all x1, blocking collectives, shards(): lax.all_to_all(partial, 'lon', 0, 0, tiled=True, axis_index_groups=chips)  14.5 us
    pallas_call x2, Pallas kernels, fine_back_call(): pl.pallas_call(functools.partial(fine_back_kernel, windows), out_shape=ou...  7.23 us
    pallas_call x1, Pallas kernels, coarse_call(): pl.pallas_call(coarse_kernel, out_shape=(shape((192, C2), BF16), shape((1...  6.96 us
    pallas_call x2, Pallas kernels, fine_call(): pl.pallas_call(functools.partial(fine_kernel, windows), out_shape=(shape(...  5.45 us
    all_to_all x1, starting transfers between devices, shards(): lax.all_to_all(sum_call(partial), 'lon', 0, 0, tiled=True, axis_index_gro...  4.98 us
    ppermute x1, starting transfers between devices, diagonal(): return lax.ppermute(value, ('lon', 'lat'), pairs)  4.76 us
  transfers between devices with their start and end apart: 18, of which 7 were waited for; matrix products, arithmetic and copies ran while one was open for 1% of the time, Pallas kernels for 19%

profile of v2, /device:TPU:8, one launch (start us, length us, event | category | flops | bytes accessed | tf_op | source)
XLA Modules:
  0.0 96.3 jit_solution(1602838850502046275)
XLA Ops:
  0.7 1.0 %copy-done.4 = f32[4,6,23,144]{3,0,2,1:T(4,128)S(1)} copy-done((f32[4,6,23,144]{3,0,2,1:T(4,128)S(1)}, f32[4,6,23,144]{3,0,2,1:T(4,128)}, u32[]{:S(2)}) %copy-start.4) | copy-done | bytes 317976
  1.8 0.9 copy-done.10
  3.1 4.6 %collective-permute-start.1 = (bf16[2,3,1152]{2,1,0:T(4,128)(2,1)S(1)}, bf16[2,3,1152]{2,1,0:T(4,128)(2,1)S(1)}, u32[]{:S(2)}, u32[]{:S(2)}) collective-permute-start(bf16[2,3,1152]{2,1,0:T(4,128)(2,1)S(1)} %get-tuple-element.48), channel_id=1, source_target_pairs={{0,7},{1,0},{2,1},{3,2},{4,3},{5,4},{6,5},{7,6},{8,15},{9,8},{10,9... | collective-permute-start | bytes 41480 | tf_op jit(solution)/shard_map/ppermute | solution.py:794
  7.7 4.8 %collective-permute-start.2 = (bf16[2,3,1152]{2,1,0:T(4,128)(2,1)S(1)}, bf16[2,3,1152]{2,1,0:T(4,128)(2,1)S(1)}, u32[]{:S(2)}, u32[]{:S(2)}) collective-permute-start(bf16[2,3,1152]{2,1,0:T(4,128)(2,1)S(1)} %get-tuple-element.49), channel_id=1, source_target_pairs={{0,255},{1,248},{2,249},{3,250},{4,251},{5,252},{6,253},{7,254},{8... | collective-permute-start | bytes 41480 | tf_op jit(solution)/shard_map/ppermute | solution.py:804
  12.4 1.9 %collective-permute-start = (bf16[2,24,1152]{2,1,0:T(8,128)(2,1)S(1)}, bf16[2,24,1152]{2,1,0:T(8,128)(2,1)S(1)}, u32[]{:S(2)}, u32[]{:S(2)}) collective-permute-start(bf16[2,24,1152]{2,1,0:T(8,128)(2,1)S(1)} %get-tuple-element.45), channel_id=1, source_target_pairs={{0,248},{8,0},{16,8},{24,16},{32,24},{40,32},{48,40},{56,48},{64,5... | collective-permute-start | bytes 331784 | tf_op jit(solution)/shard_map/ppermute | solution.py:794
  14.4 2.3 %fine_bias_spread.1.refs_8_.refs_10_ = f32[3456,128]{1,0:T(8,128)S(1)} custom-call(f32[6,23,4,144]{3,2,1,0:T(4,128)S(1)} %get-tuple-element.46.table_ref), custom_call_target="tpu_custom_call" | custom-call | flops 2000000000 | bytes 2000000 | tf_op jit(solution)/shard_map/fine_bias_spread/pallas_call | solution.py:179
  16.8 2.0 %fine_forward_1.1 = (bf16[144,192]{1,0:T(8,128)(2,1)S(1)}, bf16[72,192]{1,0:T(8,128)(2,1)S(1)}, bf16[3,144,192]{2,1,0:T(8,128)(2,1)S(1)}, bf16[864,72]{1,0:T(8,1...) custom-call(bf16[2,24,2304]{2,1,0:T(8,128)(2,1)S(1)} %copy-done.11, ...), custom_call_target="tpu_custom_call" | custom-call | flops 1500000000 | bytes 1500000 | tf_op jit(solution)/shard_map/fine_forward_1/pallas_call | solution.py:342
  18.9 2.7 %collective-permute-start.3 = (bf16[72,192]{1,0:T(8,128)(2,1)S(1)}, bf16[72,192]{1,0:T(8,128)(2,1)S(1)}, u32[]{:S(2)}, u32[]{:S(2)}) collective-permute-start(bf16[72,192]{1,0:T(8,128)(2,1)S(1)} %get-tuple-element.51), channel_id=1, source_target_pairs={{0,1},{1,2},{2,3},{3,4},{4,5},{5,6},{6,7},{7,0},{8,9},{9,10},{10,1... | collective-permute-start | bytes 82952 | tf_op jit(solution)/shard_map/ppermute | solution.py:794
  21.5 3.5 %fine_forward_3.1 = (bf16[432,192]{1,0:T(8,128)(2,1)S(1)}, bf16[3,432,192]{2,1,0:T(8,128)(2,1)S(1)}, bf16[2592,72]{1,0:T(8,128)(2,1)S(1)}, f32[432,192]{1,0:T(8,...) custom-call(bf16[2,24,2304]{2,1,0:T(8,128)(2,1)S(1)} %copy-done.11, ...), custom_call_target="tpu_custom_call" | custom-call | flops 3500000000 | bytes 3500000 | tf_op jit(solution)/shard_map/fine_forward_3/pallas_call | solution.py:342
  25.0 1.5 %collective-permute-done.3.strip_ref = bf16[72,192]{1,0:T(8,128)(2,1)S(1)} collective-permute-done((bf16[72,192]{1,0:T(8,128)(2,1)S(1)}, bf16[72,192]{1,0:T(8,128)(2,1)S(1)}, u32[]{:S(2)}, u32[]{:S(2)}) %collective-permute-start.3) | collective-permute-done | bytes 27680 | tf_op jit(solution)/shard_map/ppermute | solution.py:794
  26.6 1.5 %merge_forward.1 = (bf16[192,384]{1,0:T(8,128)(2,1)S(1)}, bf16[96,384]{1,0:T(8,128)(2,1)S(1)}, bf16[768,192]{1,0:T(8,128)(2,1)S(1)}) custom-call(bf16[432,192]{1,0:T(8,128)(2,1)S(1)} %get-tuple-element.47.y_ref, bf16[144,192]{1,0:T(8,128)(2,1)S(1)} %get-tuple-element.50.last_ref, bf16[72,192]{1,0:T(8,128)(2,1)S(1)} %collective-permute-done.3.strip_ref, ...), custom_call_target="tpu_custom_call" | custom-call | flops 1500000000 | bytes 1500000 | tf_op jit(solution)/shard_map/merge_forward/pallas_call | solution.py:389
  28.7 2.0 %coarse_bias_spread.1.bias_ref = f32[2,1728,128]{2,1,0:T(8,128)S(1)} custom-call(f32[12,23,2,144]{3,2,1,0:T(2,128)S(1)} %bitcast.13, bf16[12,384,256]{2,1,0:T(8,128)(2,1)S(1)} %copy-done.19), custom_call_target="tpu_custom_call" | custom-call | flops 2000000000 | bytes 2000000 | tf_op jit(solution)/shard_map/coarse_bias_spread/pallas_call | solution.py:215
  30.7 4.4 %collective-permute-done.6.odd_ref = bf16[96,384]{1,0:T(8,128)(2,1)S(1)} collective-permute-done((bf16[96,384]{1,0:T(8,128)(2,1)S(1)}, bf16[96,384]{1,0:T(8,128)(2,1)S(1)}, u32[]{:S(2)}, u32[]{:S(2)}) %collective-permute-start.6) | collective-permute-done | bytes 73760 | tf_op jit(solution)/shard_map/ppermute | solution.py:794
  35.2 7.0 %coarse_both.1 = (bf16[192,384]{1,0:T(8,128)(2,1)S(1)}, bf16[192,384]{1,0:T(8,128)(2,1)S(1)}, bf16[96,384]{1,0:T(8,128)(2,1)S(1)}, bf16[96,384]{1,0:T(8,128)(2,1...) custom-call(bf16[192,384]{1,0:T(8,128)(2,1)S(1)} %get-tuple-element.52.both_ref, ...), custom_call_target="tpu_custom_call" | custom-call | flops 7000000000 | bytes 7000000 | tf_op jit(solution)/shard_map/coarse_both/pallas_call | solution.py:539
  42.3 1.2 %collective-permute-start.9 = (bf16[96,384]{1,0:T(8,128)(2,1)S(1)}, bf16[96,384]{1,0:T(8,128)(2,1)S(1)}, u32[]{:S(2)}, u32[]{:S(2)}) collective-permute-start(bf16[96,384]{1,0:T(8,128)(2,1)S(1)} %get-tuple-element.59), channel_id=1, source_target_pairs={{0,248},{8,0},{16,8},{24,16},{32,24},{40,32},{48,40},{56,48},{64,5... | collective-permute-start | bytes 221192 | tf_op jit(solution)/shard_map/ppermute | solution.py:794
  43.5 0.6 collective-permute-start.10
  44.0 1.3 %coarse_rest.1 = (bf16[12,2,2304]{2,1,0:T(2,128)(2,1)S(1)}, bf16[12,2,2304]{2,1,0:T(2,128)(2,1)S(1)}, bf16[432,128]{1,0:T(8,128)(2,1)S(1)}) custom-call(bf16[144,384]{1,0:T(8,128)(2,1)S(1)} %get-tuple-element.54.out_ref, f32[2,1728,128]{2,1,0:T(8,128)S(1)} %get-tuple-element.55.ds_ref, bf16[12,384,256]{2,1,0:T(8,128)(2,1)S(1)} %copy-done.19), custom_call_target="tpu_custom_call" | custom-call | flops 1500000000 | bytes 1500000 | tf_op jit(solution)/shard_map/coarse_rest/pallas_call | solution.py:521
  45.6 2.2 %collective-permute-done.10.odd_ref = bf16[96,384]{1,0:T(8,128)(2,1)S(1)} collective-permute-done((bf16[96,384]{1,0:T(8,128)(2,1)S(1)}, bf16[96,384]{1,0:T(8,128)(2,1)S(1)}, u32[]{:S(2)}, u32[]{:S(2)}) %collective-permute-start.10) | collective-permute-done | bytes 73760 | tf_op jit(solution)/shard_map/ppermute | solution.py:794
  47.8 1.1 %merge_backward.1 = (bf16[432,192]{1,0:T(8,128)(2,1)S(1)}, bf16[144,192]{1,0:T(8,128)(2,1)S(1)}, bf16[72,192]{1,0:T(8,128)(2,1)S(1)}) custom-call(bf16[432,128]{1,0:T(8,128)(2,1)S(1)} %get-tuple-element.56._.coarse_ref, bf16[192,384]{1,0:T(8,128)(2,1)S(1)} %get-tuple-element.57.g_ref, bf16[192,384]{1,0:T(8,128)(2,1)S(1)} %collective-permute-done.8.pg_ref, ...), custom_call_target="tpu_custom_call" | custom-call | flops 1000000000 | bytes 1000000 | tf_op jit(solution)/shard_map/merge_backward/pallas_call | solution.py:591
  49.0 1.6 %collective-permute-start.11 = (bf16[72,192]{1,0:T(8,128)(2,1)S(1)}, bf16[72,192]{1,0:T(8,128)(2,1)S(1)}, u32[]{:S(2)}, u32[]{:S(2)}) collective-permute-start(bf16[72,192]{1,0:T(8,128)(2,1)S(1)} %get-tuple-element.63), channel_id=1, source_target_pairs={{0,7},{1,0},{2,1},{3,2},{4,3},{5,4},{6,5},{7,6},{8,15},{9,8},{10,9... | collective-permute-start | bytes 82952 | tf_op jit(solution)/shard_map/ppermute | solution.py:794
  50.6 4.9 %fine_backward_3.1 = (bf16[2,18,2304]{2,1,0:T(8,128)(2,1)S(1)}, f32[216,256]{1,0:T(8,128)S(1)}) custom-call(bf16[432,192]{1,0:T(8,128)(2,1)S(1)} %get-tuple-element.64.refs_0_, bf16[3,432,192]{2,1,0:T(8,128)(2,1)S(1)} %get-tuple-element.65.refs_1_, bf16[2592,72]{1,0:T(8,128)(2,1)S(1)} %get-tuple-element.66.refs_2_, ...), custom_call_target="tpu_custom_call" | custom-call | flops 6000000000 | bytes 6000000 | tf_op jit(solution)/shard_map/fine_backward_3/pallas_call | solution.py:702
  55.5 2.3 %fine_backward_1.1 = (bf16[2,21,2304]{2,1,0:T(8,128)(2,1)S(1)}, bf16[2,3,2304]{2,1,0:T(4,128)(2,1)S(1)}, bf16[288,128]{1,0:T(8,128)(2,1)S(1)}, bf16[288,128]{1,0:T(8,128)(2,1)S(1)}) custom-call(bf16[144,192]{1,0:T(8,128)(2,1)S(1)} %get-tuple-element.62.refs_0_, bf16[72,192]{1,0:T(8,128)(2,1)S(1)} %collective-permute-done.11.refs_1_, ...), custom_call_target="tpu_custom_call" | custom-call | flops 2000000000 | bytes 2000000 | tf_op jit(solution)/shard_map/fine_backward_1/pallas_call | solution.py:702
  57.9 1.3 %collective-permute-done.12.got_ref = bf16[288,128]{1,0:T(8,128)(2,1)S(1)} collective-permute-done((bf16[288,128]{1,0:T(8,128)(2,1)S(1)}, bf16[288,128]{1,0:T(8,128)(2,1)S(1)}, u32[]{:S(2)}, u32[]{:S(2)}) %collective-permute-start.12) | collective-permute-done | bytes 73760 | tf_op jit(solution)/shard_map/ppermute | solution.py:808
  59.2 14.5 %all_to_all.10.parts_ref = bf16[16,48,128]{2,1,0:T(8,128)(2,1)S(1)} all-to-all(bf16[16,48,128]{2,1,0:T(8,128)(2,1)S(1)} %bitcast.11), channel_id=1, replica_groups={{0,16,32,48,64,80,96,112,128,144,160,176,192,208,224,240},{8,24,40,56,7..., dimensions={0} | all-to-all | bytes 393216 | tf_op jit(solution)/shard_map/all_to_all | solution.py:864
  73.8 0.7 chip_sums.1
  74.5 5.0 %all-to-all-start.1 = ((bf16[16,48,128]{2,1,0:T(8,128)(2,1)}), bf16[16,48,128]{2,1,0:T(8,128)(2,1)S(1)}, u32[]{:S(2)}, u32[]{:S(2)}) async-start(bf16[16,48,128]{2,1,0:T(8,128)(2,1)} %chip_sums.1), calls=%async_computation.1 | async-start | bytes 393216 | tf_op jit(solution)/shard_map/all_to_all | solution.py:865
  79.5 1.7 %collective-permute-start.15 = (bf16[2,3,2304]{2,1,0:T(4,128)(2,1)S(1)}, bf16[2,3,2304]{2,1,0:T(4,128)(2,1)S(1)}, u32[]{:S(2)}, u32[]{:S(2)}) collective-permute-start(bf16[2,3,2304]{2,1,0:T(4,128)(2,1)S(1)} %get-tuple-element.82), channel_id=1, source_target_pairs={{0,1},{1,2},{2,3},{3,4},{4,5},{5,6},{6,7},{7,0},{8,9},{9,10},{10,1... | collective-permute-start | bytes 82952 | tf_op jit(solution)/shard_map/ppermute | solution.py:794
  81.2 5.9 %collective-permute-done.15 = bf16[2,3,2304]{2,1,0:T(4,128)(2,1)S(1)} collective-permute-done((bf16[2,3,2304]{2,1,0:T(4,128)(2,1)S(1)}, bf16[2,3,2304]{2,1,0:T(4,128)(2,1)S(1)}, u32[]{:S(2)}, u32[]{:S(2)}) %collective-permute-start.15) | collective-permute-done | bytes 27680 | tf_op jit(solution)/shard_map/ppermute | solution.py:794
  87.2 1.7 %collective-permute-start.14 = (bf16[12,2,2304]{2,1,0:T(2,128)(2,1)S(1)}, bf16[12,2,2304]{2,1,0:T(2,128)(2,1)S(1)}, u32[]{:S(2)}, u32[]{:S(2)}) collective-permute-start(bf16[12,2,2304]{2,1,0:T(2,128)(2,1)S(1)} %get-tuple-element.80), channel_id=1, source_target_pairs={{0,8},{8,0},{16,24},{24,16},{32,40},{40,32},{48,56},{56,48},{64,72... | collective-permute-start | bytes 331784 | tf_op jit(solution)/shard_map/ppermute | solution.py:808
  88.9 4.6 %collective-permute-done.16 = bf16[2,24,1152]{2,1,0:T(8,128)(2,1)S(1)} collective-permute-done((bf16[2,24,1152]{2,1,0:T(8,128)(2,1)S(1)}, bf16[2,24,1152]{2,1,0:T(8,128)(2,1)S(1)}, u32[]{:S(2)}, u32[]{:S(2)}) %collective-permute-start.16) | collective-permute-done | bytes 110624 | tf_op jit(solution)/shard_map/ppermute | solution.py:794
  93.5 0.7 fusion
  94.2 2.0 %results.1 = (bf16[12,2,2304]{2,1,0:T(2,128)(2,1)}, f32[6,23,4,144]{3,2,1,0:T(4,128)}, f32[12,23,2,144]{3,2,1,0:T(2,128)}) custom-call(bf16[768,128]{1,0:T(8,128)(2,1)S(1)} %bitcast.10, bf16[768,128]{1,0:T(8,128)(2,1)S(1)} %collective-permute-done.13.got_ref, bf16[12,2,2304]{2,1,0:T(2,128)(2,1)S(1)} %get-tuple-element.79.okeep_ref, ...), custom_call_target="tpu_custom_call" | custom-call | flops 2000000000 | bytes 2000000 | tf_op jit(solution)/shard_map/results/pallas_call | solution.py:777
  (69 shorter events, 1.7 us)
Async XLA Ops:
  0.6 30.0 %collective-permute-start.7 = (bf16[12,2,2304]{2,1,0:T(2,128)(2,1)}, bf16[12,2,2304]{2,1,0:T(2,128)(2,1)S(1)}, u32[]{:S(2)}, u32[]{:S(2)}) collective-permute-start(bf16[12,2,2304]{2,1,0:T(2,128)(2,1)} %bitcast.18), channel_id=1, source_target_pairs={{0,8},{8,0},{16,24},{24,16},{32,40},{40,32},{48,56},{56,48},{64,72... | collective-permute-start | bytes 331784 | tf_op jit(solution)/shard_map/ppermute | solution.py:808
  3.1 13.6 %collective-permute-start.1 = (bf16[2,3,1152]{2,1,0:T(4,128)(2,1)S(1)}, bf16[2,3,1152]{2,1,0:T(4,128)(2,1)S(1)}, u32[]{:S(2)}, u32[]{:S(2)}) collective-permute-start(bf16[2,3,1152]{2,1,0:T(4,128)(2,1)S(1)} %get-tuple-element.48), channel_id=1, source_target_pairs={{0,7},{1,0},{2,1},{3,2},{4,3},{5,4},{6,5},{7,6},{8,15},{9,8},{10,9... | collective-permute-start | bytes 41480 | tf_op jit(solution)/shard_map/ppermute | solution.py:794
  7.7 9.1 %collective-permute-start.2 = (bf16[2,3,1152]{2,1,0:T(4,128)(2,1)S(1)}, bf16[2,3,1152]{2,1,0:T(4,128)(2,1)S(1)}, u32[]{:S(2)}, u32[]{:S(2)}) collective-permute-start(bf16[2,3,1152]{2,1,0:T(4,128)(2,1)S(1)} %get-tuple-element.49), channel_id=1, source_target_pairs={{0,255},{1,248},{2,249},{3,250},{4,251},{5,252},{6,253},{7,254},{8... | collective-permute-start | bytes 41480 | tf_op jit(solution)/shard_map/ppermute | solution.py:804
  12.4 4.3 %collective-permute-start = (bf16[2,24,1152]{2,1,0:T(8,128)(2,1)S(1)}, bf16[2,24,1152]{2,1,0:T(8,128)(2,1)S(1)}, u32[]{:S(2)}, u32[]{:S(2)}) collective-permute-start(bf16[2,24,1152]{2,1,0:T(8,128)(2,1)S(1)} %get-tuple-element.45), channel_id=1, source_target_pairs={{0,248},{8,0},{16,8},{24,16},{32,24},{40,32},{48,40},{56,48},{64,5... | collective-permute-start | bytes 331784 | tf_op jit(solution)/shard_map/ppermute | solution.py:794
  14.4 2.4 %copy-start.13 = (bf16[192,192]{1,0:T(8,128)(2,1)S(1)}, bf16[192,192]{1,0:T(8,128)(2,1)}, u32[]{:S(2)}) copy-start(bf16[192,192]{1,0:T(8,128)(2,1)} %refs_11_.3) | copy-start | bytes 221188
  18.8 7.7 %copy-start.3 = (bf16[768,384]{1,0:T(8,128)(2,1)S(1)}, bf16[768,384]{1,0:T(8,128)(2,1)}, u32[]{:S(2)}) copy-start(bf16[768,384]{1,0:T(8,128)(2,1)} %w_ref.3) | copy-start | bytes 1769476
  18.9 7.7 %copy-start.14 = (f32[768]{0:T(1024)S(1)}, f32[768]{0:T(1024)}, u32[]{:S(2)}) copy-start(f32[768]{0:T(1024)} %gain_ref.3) | copy-start | bytes 9220
  18.9 7.7 %copy-start.20 = (bf16[768,648]{1,0:T(8,128)(2,1)S(1)}, bf16[768,648]{1,0:T(8,128)(2,1)}, u32[]{:S(2)}) copy-start(bf16[768,648]{1,0:T(8,128)(2,1)} %constant.11.clone.pick_ref) | copy-start | bytes 2985988
  18.9 7.7 %collective-permute-start.3 = (bf16[72,192]{1,0:T(8,128)(2,1)S(1)}, bf16[72,192]{1,0:T(8,128)(2,1)S(1)}, u32[]{:S(2)}, u32[]{:S(2)}) collective-permute-start(bf16[72,192]{1,0:T(8,128)(2,1)S(1)} %get-tuple-element.51), channel_id=1, source_target_pairs={{0,1},{1,2},{2,3},{3,4},{4,5},{5,6},{6,7},{7,0},{8,9},{9,10},{10,1... | collective-permute-start | bytes 82952 | tf_op jit(solution)/shard_map/ppermute | solution.py:794
  28.1 7.0 %collective-permute-start.6 = (bf16[96,384]{1,0:T(8,128)(2,1)S(1)}, bf16[96,384]{1,0:T(8,128)(2,1)S(1)}, u32[]{:S(2)}, u32[]{:S(2)}) collective-permute-start(bf16[96,384]{1,0:T(8,128)(2,1)S(1)} %get-tuple-element.53), channel_id=1, source_target_pairs={{0,16},{8,24},{16,32},{24,40},{32,48},{40,56},{48,64},{56,72},{64,... | collective-permute-start | bytes 221192 | tf_op jit(solution)/shard_map/ppermute | solution.py:794
  28.2 6.9 %collective-permute-start.5 = (bf16[96,384]{1,0:T(8,128)(2,1)S(1)}, bf16[96,384]{1,0:T(8,128)(2,1)S(1)}, u32[]{:S(2)}, u32[]{:S(2)}) collective-permute-start(bf16[96,384]{1,0:T(8,128)(2,1)S(1)} %get-tuple-element.53), channel_id=1, source_target_pairs={{0,8},{8,16},{16,24},{24,32},{32,40},{40,48},{48,56},{56,64},{64,7... | collective-permute-start | bytes 221192 | tf_op jit(solution)/shard_map/ppermute | solution.py:794
  28.4 6.7 %collective-permute-start.4 = (bf16[192,384]{1,0:T(8,128)(2,1)S(1)}, bf16[192,384]{1,0:T(8,128)(2,1)S(1)}, u32[]{:S(2)}, u32[]{:S(2)}) collective-permute-start(bf16[192,384]{1,0:T(8,128)(2,1)S(1)} %get-tuple-element.52.both_ref), channel_id=1, source_target_pairs={{0,8},{8,0},{16,24},{24,16},{32,40},{40,32},{48,56},{56,48},{64,72... | collective-permute-start | bytes 442376 | tf_op jit(solution)/shard_map/ppermute | solution.py:808
  28.6 6.6 %copy-start = (bf16[384,1536]{1,0:T(8,128)(2,1)S(1)}, bf16[384,1536]{1,0:T(8,128)(2,1)}, u32[]{:S(2)}) copy-start(bf16[384,1536]{1,0:T(8,128)(2,1)} %we_ref.1) | copy-start | bytes 3538948
  28.6 6.5 %copy-start.1 = (bf16[1536,384]{1,0:T(8,128)(2,1)S(1)}, bf16[1536,384]{1,0:T(8,128)(2,1)}, u32[]{:S(2)}) copy-start(bf16[1536,384]{1,0:T(8,128)(2,1)} %wr_ref.1) | copy-start | bytes 3538948
  28.6 6.5 %copy-start.2 = (bf16[384,1152]{1,0:T(8,128)(2,1)S(1)}, bf16[384,1152]{1,0:T(8,128)(2,1)}, u32[]{:S(2)}) copy-start(bf16[384,1152]{1,0:T(8,128)(2,1)} %wa_ref.1) | copy-start | bytes 2654212
  28.6 6.5 %copy-start.6 = (bf16[384,384]{1,0:T(8,128)(2,1)S(1)}, bf16[384,384]{1,0:T(8,128)(2,1)}, u32[]{:S(2)}) copy-start(bf16[384,384]{1,0:T(8,128)(2,1)} %wp_ref.1) | copy-start | bytes 884740
  28.6 6.5 %copy-start.12 = (bf16[2,12,2304]{2,0,1:T(2,128)(2,1)S(1)}, bf16[2,12,2304]{2,0,1:T(2,128)(2,1)}, u32[]{:S(2)}) copy-start(bf16[2,12,2304]{2,0,1:T(2,128)(2,1)} %param.40) | copy-start | bytes 331780
  28.6 6.5 %copy-start.15 = (f32[384]{0:T(512)S(1)}, f32[384]{0:T(512)}, u32[]{:S(2)}) copy-start(f32[384]{0:T(512)} %g1_ref.1) | copy-start | bytes 4612
  28.6 6.5 %copy-start.16 = (f32[384]{0:T(512)S(1)}, f32[384]{0:T(512)}, u32[]{:S(2)}) copy-start(f32[384]{0:T(512)} %g2_ref.1) | copy-start | bytes 4612
  42.2 5.7 %collective-permute-start.8 = (bf16[192,384]{1,0:T(8,128)(2,1)S(1)}, bf16[192,384]{1,0:T(8,128)(2,1)S(1)}, u32[]{:S(2)}, u32[]{:S(2)}) collective-permute-start(bf16[192,384]{1,0:T(8,128)(2,1)S(1)} %get-tuple-element.58), channel_id=1, source_target_pairs={{0,8},{8,0},{16,24},{24,16},{32,40},{40,32},{48,56},{56,48},{64,72... | collective-permute-start | bytes 442376 | tf_op jit(solution)/shard_map/ppermute | solution.py:808
  42.3 3.4 %collective-permute-start.9 = (bf16[96,384]{1,0:T(8,128)(2,1)S(1)}, bf16[96,384]{1,0:T(8,128)(2,1)S(1)}, u32[]{:S(2)}, u32[]{:S(2)}) collective-permute-start(bf16[96,384]{1,0:T(8,128)(2,1)S(1)} %get-tuple-element.59), channel_id=1, source_target_pairs={{0,248},{8,0},{16,8},{24,16},{32,24},{40,32},{48,40},{56,48},{64,5... | collective-permute-start | bytes 221192 | tf_op jit(solution)/shard_map/ppermute | solution.py:794
  43.5 4.4 %collective-permute-start.10 = (bf16[96,384]{1,0:T(8,128)(2,1)S(1)}, bf16[96,384]{1,0:T(8,128)(2,1)S(1)}, u32[]{:S(2)}, u32[]{:S(2)}) collective-permute-start(bf16[96,384]{1,0:T(8,128)(2,1)S(1)} %get-tuple-element.60), channel_id=1, source_target_pairs={{0,240},{8,248},{16,0},{24,8},{32,16},{40,24},{48,32},{56,40},{64,... | collective-permute-start | bytes 221192 | tf_op jit(solution)/shard_map/ppermute | solution.py:794
  44.0 3.8 %copy-start.21 = (bf16[648,768]{1,0:T(8,128)(2,1)S(1)}, bf16[648,768]{1,0:T(8,128)(2,1)}, u32[]{:S(2)}) copy-start(bf16[648,768]{1,0:T(8,128)(2,1)} %constant.12.clone.place_ref) | copy-start | bytes 2985988
  47.8 2.8 %copy-start.22 = (bf16[12,256,128]{2,1,0:T(8,128)(2,1)S(1)}, bf16[12,256,128]{2,1,0:T(8,128)(2,1)}, u32[]{:S(2)}) copy-start(bf16[12,256,128]{2,1,0:T(8,128)(2,1)} %constant.13.clone.refs_12_.refs_16_) | copy-start | bytes 2359300
  49.0 6.5 %collective-permute-start.11 = (bf16[72,192]{1,0:T(8,128)(2,1)S(1)}, bf16[72,192]{1,0:T(8,128)(2,1)S(1)}, u32[]{:S(2)}, u32[]{:S(2)}) collective-permute-start(bf16[72,192]{1,0:T(8,128)(2,1)S(1)} %get-tuple-element.63), channel_id=1, source_target_pairs={{0,7},{1,0},{2,1},{3,2},{4,3},{5,4},{6,5},{7,6},{8,15},{9,8},{10,9... | collective-permute-start | bytes 82952 | tf_op jit(solution)/shard_map/ppermute | solution.py:794
  50.6 4.9 %copy-start.23 = (bf16[144,72]{1,0:T(8,128)(2,1)S(1)}, bf16[144,72]{1,0:T(8,128)(2,1)}, u32[]{:S(2)}) copy-start(bf16[144,72]{1,0:T(8,128)(2,1)} %constant.14.clone.refs_2_) | copy-start | bytes 62212
  57.8 1.4 %collective-permute-start.12 = (bf16[288,128]{1,0:T(8,128)(2,1)S(1)}, bf16[288,128]{1,0:T(8,128)(2,1)S(1)}, u32[]{:S(2)}, u32[]{:S(2)}) collective-permute-start(bf16[288,128]{1,0:T(8,128)(2,1)S(1)} %get-tuple-element.78), channel_id=1, source_target_pairs={{0,8},{8,0},{16,24},{24,16},{32,40},{40,32},{48,56},{56,48},{64,72... | collective-permute-start | bytes 221192 | tf_op jit(solution)/shard_map/ppermute | solution.py:808
  74.5 14.4 %all-to-all-start.1 = ((bf16[16,48,128]{2,1,0:T(8,128)(2,1)}), bf16[16,48,128]{2,1,0:T(8,128)(2,1)S(1)}, u32[]{:S(2)}, u32[]{:S(2)}) async-start(bf16[16,48,128]{2,1,0:T(8,128)(2,1)} %chip_sums.1), calls=%async_computation.1 | async-start | bytes 393216 | tf_op jit(solution)/shard_map/all_to_all | solution.py:865
  79.5 7.6 %collective-permute-start.15 = (bf16[2,3,2304]{2,1,0:T(4,128)(2,1)S(1)}, bf16[2,3,2304]{2,1,0:T(4,128)(2,1)S(1)}, u32[]{:S(2)}, u32[]{:S(2)}) collective-permute-start(bf16[2,3,2304]{2,1,0:T(4,128)(2,1)S(1)} %get-tuple-element.82), channel_id=1, source_target_pairs={{0,1},{1,2},{2,3},{3,4},{4,5},{5,6},{6,7},{7,0},{8,9},{9,10},{10,1... | collective-permute-start | bytes 82952 | tf_op jit(solution)/shard_map/ppermute | solution.py:794
  87.1 6.4 %collective-permute-start.16 = (bf16[2,24,1152]{2,1,0:T(8,128)(2,1)S(1)}, bf16[2,24,1152]{2,1,0:T(8,128)(2,1)S(1)}, u32[]{:S(2)}, u32[]{:S(2)}) collective-permute-start(bf16[2,24,1152]{2,1,0:T(8,128)(2,1)S(1)} %fusion.1), channel_id=1, source_target_pairs={{0,8},{8,16},{16,24},{24,32},{32,40},{40,48},{48,56},{56,64},{64,7... | collective-permute-start | bytes 331784 | tf_op jit(solution)/shard_map/ppermute | solution.py:794
  87.2 7.0 %collective-permute-start.14 = (bf16[12,2,2304]{2,1,0:T(2,128)(2,1)S(1)}, bf16[12,2,2304]{2,1,0:T(2,128)(2,1)S(1)}, u32[]{:S(2)}, u32[]{:S(2)}) collective-permute-start(bf16[12,2,2304]{2,1,0:T(2,128)(2,1)S(1)} %get-tuple-element.80), channel_id=1, source_target_pairs={{0,8},{8,0},{16,24},{24,16},{32,40},{40,32},{48,56},{56,48},{64,72... | collective-permute-start | bytes 331784 | tf_op jit(solution)/shard_map/ppermute | solution.py:808
  88.9 5.3 %collective-permute-start.13 = (bf16[768,128]{1,0:T(8,128)(2,1)S(1)}, bf16[768,128]{1,0:T(8,128)(2,1)S(1)}, u32[]{:S(2)}, u32[]{:S(2)}) collective-permute-start(bf16[768,128]{1,0:T(8,128)(2,1)S(1)} %bitcast.9), channel_id=1, source_target_pairs={{0,8},{8,0},{16,24},{24,16},{32,40},{40,32},{48,56},{56,48},{64,72... | collective-permute-start | bytes 589832 | tf_op jit(solution)/shard_map/ppermute | solution.py:808
  (10 other events, 20.5 us)

commit v3 on v2

--- a/solution.py
+++ b/solution.py
@@ -144,12 +144,13 @@
 
 
 def fine_bias_kernel(table_ref, out_ref, cols_ref):
-    key = lax.broadcasted_iota(jnp.int32, (256, 128), 0)
-    lane = lax.broadcasted_iota(jnp.int32, (256, 128), 1)
+    key = lax.broadcasted_iota(jnp.int32, (256, 256), 0)
+    lane = lax.broadcasted_iota(jnp.int32, (256, 256), 1) % 128
+    second = lax.broadcasted_iota(jnp.int32, (256, 256), 1) // 128
     place = key % 128
     pair = key // 128 * 5 + place // 24
     meets = jnp.logical_and(pair == lane // 12, place < 120)
-    column = jnp.where(meets, place % 24 + lane % 12 - (WLON - 1), -1)
+    column = jnp.where(meets, place % 24 + lane % 12 - (WLON - 1) - second, -2)
     cols_ref[...] = jnp.zeros_like(cols_ref)
     for th in range(24):
         cols_ref[th * 144 : (th + 1) * 144, 0:23] = jnp.swapaxes(
@@ -170,9 +171,11 @@
             tile = piece if tile is None else tile + piece
         tiles.append(tile)
     parts = jnp.concatenate(split3(jnp.concatenate(tiles, axis=1)), axis=0)
-    for p in range(WLON):
+    for p in range(0, WLON, 2):
         spread = nn(parts, (column == p).astype(F32).astype(BF16))
-        out_ref[pl.ds(p, 288, stride=12), :] = spread[:288] + spread[288:576] + spread[576:]
+        total = spread[:288] + spread[288:576] + spread[576:]
+        out_ref[pl.ds(p, 288, stride=12), :] = total[:, :128]
+        out_ref[pl.ds(p + 1, 288, stride=12), :] = total[:, 128:]
 
 
 def fine_bias_call(table):
@@ -187,7 +190,7 @@
     )(table)
 
 
-def coarse_bias_kernel(table_ref, onehot_ref, out_ref, cols_ref):
+def coarse_bias_kernel(table_ref, onehot_ref, tail_ref, out_ref, cols_ref):
     cols_ref[...] = jnp.zeros_like(cols_ref)
     par = parity()
     for h in range(12):
@@ -204,43 +207,46 @@
             tile = piece if tile is None else tile + piece
         tiles.append(tile)
     parts = jnp.concatenate(split3(jnp.concatenate(tiles, axis=1)), axis=0)
-    for p in range(WLON):
-        spread = nn(parts, onehot_ref[p])
+    for p in range(0, WLON, 2):
+        pair = jnp.concatenate([onehot_ref[p, :, :128], onehot_ref[p + 1, :, :128]], axis=1)
+        spread = nn(parts, pair)
         total = spread[:144] + spread[144:288] + spread[288:]
         out_ref[0, pl.ds(p, 144, stride=12), :] = total[:, :128]
-        out_ref[1, pl.ds(p, 144, stride=12), :] = total[:, 128:]
+        out_ref[0, pl.ds(p + 1, 144, stride=12), :] = total[:, 128:]
+    spread = nn(parts, tail_ref[...])
+    total = spread[:144] + spread[144:288] + spread[288:]
+    for p in range(WLON):
+        tile = total[:, p // 8 * 128 : p // 8 * 128 + 128]
+        if p % 8:
+            tile = pltpu.roll(tile, 128 - p % 8 * 16, 1)
+        out_ref[1, pl.ds(p, 144, stride=12), :] = tile
 
 
 def coarse_bias_call(table, onehot):
+    tail = np.zeros((onehot.shape[1], 256), onehot.dtype)
+    for p in range(WLON):
+        tail[:, p * 16 : p * 16 + 16] = onehot[p, :, 128:144]
     return pl.pallas_call(
         coarse_bias_kernel,
         out_shape=jax.ShapeDtypeStruct((2, 1728, 128), F32),
-        in_specs=vmem(2),
+        in_specs=vmem(3),
         scratch_shapes=[pltpu.VMEM((1728, 128), F32)],
         compiler_params=pltpu.CompilerParams(vmem_limit_bytes=10 << 20),
         cost_estimate=cost(2),
         name="coarse_bias_spread",
-    )(table, onehot)
-
-
-def split_kernel(
-    far_tok_ref, table_ref, left_ref, top_ref, corner_ref, near_ref, tok_ref, tok_sem, table_sem
-):
+    )(table, onehot, tail)
+
+
+def split_kernel(tok_ref, left_ref, top_ref, corner_ref):
     half = left_ref.shape[2]
-    tok_copy = pltpu.make_async_copy(far_tok_ref, tok_ref, tok_sem)
-    table_copy = pltpu.make_async_copy(table_ref, near_ref, table_sem)
-    tok_copy.start()
-    table_copy.start()
-    tok_copy.wait()
     left_ref[...] = tok_ref[:, :, :half]
     for z in range(2):
         rows = tok_ref[z].astype(F32)[:3]
         top_ref[z] = rows[:, half:].astype(BF16)
         corner_ref[z] = rows[:, :half].astype(BF16)
-    table_copy.wait()
-
-
-def split_call(tokens, table):
+
+
+def split_call(tokens):
     levels, rows, width = tokens.shape
     shape = jax.ShapeDtypeStruct
     return pl.pallas_call(
@@ -249,18 +255,12 @@
             shape((levels, rows, width // 2), BF16),
             shape((levels, 3, width // 2), BF16),
             shape((levels, 3, width // 2), BF16),
-            shape(table.shape, F32),
         ),
-        in_specs=[pl.BlockSpec(memory_space=pl.ANY)] * 2,
-        scratch_shapes=[
-            pltpu.VMEM(tokens.shape, BF16),
-            pltpu.SemaphoreType.DMA,
-            pltpu.SemaphoreType.DMA,
-        ],
+        in_specs=vmem(1),
         compiler_params=pltpu.CompilerParams(vmem_limit_bytes=4 << 20),
-        cost_estimate=cost(1),
+        cost_estimate=cost(8),
         name="left_half",
-    )(tokens, table)
+    )(tokens)
 
 
 def fine_kernel(windows, *refs):
@@ -408,22 +408,18 @@
 
 
 def half_places(par):
-    row = lax.broadcasted_iota(jnp.int32, (144, 24), 0)
+    row = lax.broadcasted_iota(jnp.int32, (144, 288), 0)
     z, a, c = row // 72, row // 12 % 6, row % 12
-    match = (z * 12 + par * 6 + a == lax.broadcasted_iota(jnp.int32, (144, 24), 1)).astype(F32)
-    places = []
-    for side in (par, 1 - par):
-        places.append(
-            [jnp.where(c == side * 6 + col, match, 0.0).astype(BF16) for col in range(6)]
-        )
-    return places
+    side = jnp.where(c // 6 == par, 0, 1)
+    place = (side * 6 + c % 6) * 24 + z * 12 + par * 6 + a
+    return (place == lax.broadcasted_iota(jnp.int32, (144, 288), 1)).astype(F32).astype(BF16)
 
 
 def coarse_kernel(
     both_ref, pboth_ref, even_ref, odd_ref, seed_ref, pseed_ref,
     wa_ref, wp_ref, g1_ref, we_ref, wr_ref, g2_ref, bias_ref,
     gboth_ref, gpboth_ref, geven_ref, godd_ref, out_ref, ds_ref,
-    a_ref, qs_ref, o_ref, slope_ref, band_ref,
+    a_ref, qs_ref, o_ref, slope_ref, band_ref, packed_ref,
 ):
     par = parity()
     pick = window_places(par)
@@ -434,11 +430,10 @@
         wide = source_ref[...].astype(F32)
         for z in range(2):
             band_ref[side, z * 12 : (z + 1) * 12, :] = wide[:, z, :]
-    seed = None
-    for side in range(2):
-        for col in range(6):
-            part = nn(half[side][col], band_ref[side, :, col * C2 : (col + 1) * C2].astype(BF16))
-            seed = part if seed is None else seed + part
+    bands = [
+        band_ref[side, :, col * C2 : (col + 1) * C2] for side in range(2) for col in range(6)
+    ]
+    seed = nn(half, jnp.concatenate(bands, axis=0).astype(BF16))
     ds_ref[1] = jnp.zeros_like(ds_ref[1])
     packed = nn(x, wa_ref[...]).astype(BF16)
     mask = head_mask(144, 4, 128)
@@ -468,7 +463,6 @@
     grad_middle = grad_middle.astype(F32)
     grad_att = norm_back(grad_middle * g1_ref[...][None, :], normed1, scale1).astype(BF16)
     grad_o = nt(grad_att, wp_ref[...]).astype(BF16)
-    grad_x = grad_middle
     for g in range(3):
         lanes = slice(g * 128, (g + 1) * 128)
         rows = slice(g * 576, (g + 1) * 576)
@@ -485,9 +479,9 @@
         grad_v = tn(weights, os).astype(BF16)
         grad_q = (heads_fold(nn(short, key), 4, mask) * SCALE).astype(BF16)
         grad_k = (tn(short, qs_ref[rows, :]) * SCALE).astype(BF16)
-        grad_x = grad_x + nt(grad_q, wa_ref[:, g * 128 : (g + 1) * 128])
-        grad_x = grad_x + nt(grad_k, wa_ref[:, C2 + g * 128 : C2 + (g + 1) * 128])
-        grad_x = grad_x + nt(grad_v, wa_ref[:, 2 * C2 + g * 128 : 2 * C2 + (g + 1) * 128])
+        for part, grad in enumerate((grad_q, grad_k, grad_v)):
+            packed_ref[:, part * C2 + g * 128 : part * C2 + (g + 1) * 128] = grad
+    grad_x = grad_middle + nt(packed_ref[...], wa_ref[...])
     parted = tn(pick, grad_x.astype(BF16)).astype(BF16)
     gboth_ref[...] = parted[:192]
     gpboth_ref[...] = parted[192:384]
@@ -498,12 +492,13 @@
 def coarse_rest_kernel(out_ref, ds_ref, ec_ref, okeep_ref, osend_ref, dt_ref, cells_ref):
     half = half_places(parity())
     out = out_ref[...]
-    for col in range(6):
-        lanes = slice(col * C2, (col + 1) * C2)
-        for side in range(2):
-            part = tn(half[side][col], out)
+    parted = tn(half, out)
+    for side in range(2):
+        for col in range(6):
+            lanes = slice(col * C2, (col + 1) * C2)
             for z in range(2):
-                cells_ref[side, :, z, lanes] = part[z * 12 : (z + 1) * 12]
+                place = (side * 6 + col) * 24 + z * 12
+                cells_ref[side, :, z, lanes] = parted[place : place + 12]
     okeep_ref[...] = cells_ref[0].astype(BF16)
     osend_ref[...] = cells_ref[1].astype(BF16)
     table = None
@@ -553,6 +548,7 @@
             pltpu.VMEM((144, C2), F32),
             pltpu.VMEM((144, 4 * C2), F32),
             pltpu.VMEM((2, 24, 6 * C2), F32),
+            pltpu.VMEM((144, 3 * C2), BF16),
         ],
         compiler_params=pltpu.CompilerParams(vmem_limit_bytes=20 << 20),
         cost_estimate=cost(7),
@@ -730,26 +726,30 @@
     )(keep, got, coarse)
 
 
-def sum_kernel(parts_ref, out_ref):
+def sum_kernel(parts_ref, _, out_ref):
     total = jnp.sum(parts_ref[...].astype(F32), axis=0, keepdims=True).astype(BF16)
     out_ref[...] = jnp.broadcast_to(total, out_ref.shape)
 
 
-def sum_call(parts):
+def sum_call(parts, after):
     return pl.pallas_call(
         sum_kernel,
         out_shape=jax.ShapeDtypeStruct(parts.shape, BF16),
-        in_specs=vmem(1),
+        in_specs=vmem(1) + [pl.BlockSpec(memory_space=pl.ANY)],
         compiler_params=pltpu.CompilerParams(vmem_limit_bytes=4 << 20),
         cost_estimate=cost(0.7),
         name="chip_sums",
-    )(parts)
+    )(parts, after)
 
 
 def table_kernel(
-    mine_ref, got_ref, okeep_ref, ogot_ref, out_ref, fine_ref, coarse_ref, cols_f, cols_c
+    mine_ref, got_ref, okeep_ref, ogot_ref, right_ref, band_ref,
+    out_ref, tokens_ref, fine_ref, coarse_ref, cols_f, cols_c,
 ):
     par = parity()
+    half = right_ref.shape[2]
+    tokens_ref[:, :, :half] = right_ref[...]
+    tokens_ref[:, :, half:] = band_ref[:, :, :half]
     out_ref[...] = (okeep_ref[...].astype(F32) + ogot_ref[...].astype(F32)).astype(BF16)
     level = lax.broadcasted_iota(jnp.int32, (144, 128), 0) % 12 < 6
     for s in range(2):
@@ -772,21 +772,22 @@
         coarse_ref[th % 12, :, th // 12, :] = jnp.swapaxes(cols_c[rows, 0:24], 0, 1)[:23]
 
 
-def table_call(mine, got, okeep, ogot):
+def table_call(mine, got, okeep, ogot, right, band):
     shape = jax.ShapeDtypeStruct
     return pl.pallas_call(
         table_kernel,
         out_shape=(
             shape((12, 2, 6 * C2), BF16),
+            shape((2, 24, WLON * C1), BF16),
             shape((6, 23, 4, 144), F32),
             shape((12, 23, 2, 144), F32),
         ),
-        in_specs=vmem(4),
+        in_specs=vmem(6),
         scratch_shapes=[pltpu.VMEM((3456, 128), F32)] * 2,
         compiler_params=pltpu.CompilerParams(vmem_limit_bytes=10 << 20),
         cost_estimate=cost(2),
         name="results",
-    )(mine, got, okeep, ogot)
+    )(mine, got, okeep, ogot, right, band)
 
 
 def shifted(value, axis, steps):
@@ -825,11 +826,11 @@
     pick = merge_onehot()
     seed = jnp.transpose(cotangent, (1, 0, 2))
     seeds = (seed, swapped(seed))
-    cols, top, corner, table = split_call(tokens, jnp.transpose(fine_bias, (1, 2, 0, 3)))
+    cols, top, corner = split_call(tokens)
     cols = shifted(cols, "lon", -1)
+    corner = diagonal(corner, -1)
     top = shifted(top, "lat", -1)
-    corner = diagonal(corner, -1)
-    bias_fine = fine_bias_call(table)
+    bias_fine = fine_bias_call(jnp.transpose(fine_bias, (1, 2, 0, 3)))
     bias_coarse = coarse_bias_call(jnp.transpose(coarse_bias, (1, 2, 0, 3)), ec)
 
     most, final = (0, 1, 2), (3,)
@@ -859,18 +860,16 @@
     own, edge, table_keep, table_send = fine_back_call(
         final, grads, saved_last, fine_weights, ef
     )
+    edge = shifted(edge, "lat", 1)
     partial = partial_call(table_keep, swapped(table_send), table_coarse).reshape(16, 48, 128)
     chips = [[2 * k + c for k in range(16)] for c in range(2)]
     partial = lax.all_to_all(partial, "lon", 0, 0, tiled=True, axis_index_groups=chips)
-    sums = lax.all_to_all(sum_call(partial), "lon", 0, 0, tiled=True, axis_index_groups=chips)
+    sums = lax.all_to_all(sum_call(partial, edge), "lon", 0, 0, tiled=True, axis_index_groups=chips)
     sums = sums.reshape(768, 128)
-    coarse_out, grad_fine, grad_coarse = table_call(
-        sums, swapped(sums), out_keep, swapped(out_send)
-    )
-    band = jnp.concatenate([shifted(edge, "lat", 1), own], axis=1)
-    half = band.shape[2] // 2
-    grad_tokens = jnp.concatenate(
-        [shifted(band[:, :, half:], "lon", 1), band[:, :, :half]], axis=2
+    band = jnp.concatenate([edge, own], axis=1)
+    right = shifted(band[:, :, band.shape[2] // 2 :], "lon", 1)
+    coarse_out, grad_tokens, grad_fine, grad_coarse = table_call(
+        sums, swapped(sums), out_keep, swapped(out_send), right, band
     )
     return (
         jnp.transpose(coarse_out, (1, 0, 2)),

time: 96.5 us -> 95.3 us (0.988)
  the two profiles are of different devices: /device:TPU:8 before, /device:TPU:1 now
where the time goes in v3:
time: 95.3 us; the launch traced here: 95 us
  starting transfers between devices  45.9 us (48%)
  Pallas kernels  30.1 us (32%)
  waiting for transfers between devices  16.7 us (18%)
  local copies, waits for them, and re-layouts  1.07 us (1%)
  between operations  1.07 us (1%)
    ppermute x10, starting transfers between devices, shifted(): lax.ppermute(value, axis, [(s, (s + steps) % count) for s in range(count)])  19.8 us
    ppermute x6, starting transfers between devices, swapped(): lax.ppermute(value, 'lon', [(s, s ^ 1) for s in range(lax.axis_size('lon'...  15.6 us
    ppermute x10, waiting for transfers between devices, shifted(): lax.ppermute(value, axis, [(s, (s + steps) % count) for s in range(count)])  10.1 us
    pallas_call x2, Pallas kernels, fine_back_call(): pl.pallas_call(functools.partial(fine_back_kernel, windows), out_shape=ou...  7.23 us
    pallas_call x1, Pallas kernels, coarse_call(): pl.pallas_call(coarse_kernel, out_shape=(shape((192, C2), BF16), shape((1...  6.76 us
    all_to_all x1, starting transfers between devices, shards(): lax.all_to_all(sum_call(partial, edge), 'lon', 0, 0, tiled=True, axis_ind...  6.69 us
    pallas_call x2, Pallas kernels, fine_call(): pl.pallas_call(functools.partial(fine_kernel, windows), out_shape=(shape(...  5.45 us
    all_to_all x1, waiting for transfers between devices, shards(): lax.all_to_all(sum_call(partial, edge), 'lon', 0, 0, tiled=True, axis_ind...  3.68 us
  transfers between devices with their start and end apart: 19, of which 8 were waited for; matrix products, arithmetic and copies ran while one was open for 0% of the time, Pallas kernels for 17%

profile of v3, /device:TPU:1, one launch (start us, length us, event | category | flops | bytes accessed | tf_op | source)
XLA Modules:
  0.0 95.0 jit_solution(5354887771596277932)
XLA Ops:
  0.6 3.3 %collective-permute-start.7 = (bf16[12,2,2304]{2,1,0:T(2,128)(2,1)}, bf16[12,2,2304]{2,1,0:T(2,128)(2,1)S(1)}, u32[]{:S(2)}, u32[]{:S(2)}) collective-permute-start(bf16[12,2,2304]{2,1,0:T(2,128)(2,1)} %bitcast.17), channel_id=1, source_target_pairs={{0,8},{8,0},{16,24},{24,16},{32,40},{40,32},{48,56},{56,48},{64,72... | collective-permute-start | bytes 331784 | tf_op jit(solution)/shard_map/ppermute | solution.py:809
  4.9 3.5 %collective-permute-start.1 = (bf16[2,3,1152]{2,1,0:T(4,128)(2,1)S(1)}, bf16[2,3,1152]{2,1,0:T(4,128)(2,1)S(1)}, u32[]{:S(2)}, u32[]{:S(2)}) collective-permute-start(bf16[2,3,1152]{2,1,0:T(4,128)(2,1)S(1)} %get-tuple-element.47), channel_id=1, source_target_pairs={{0,7},{1,0},{2,1},{3,2},{4,3},{5,4},{6,5},{7,6},{8,15},{9,8},{10,9... | collective-permute-start | bytes 41480 | tf_op jit(solution)/shard_map/ppermute | solution.py:795
  8.7 6.2 %collective-permute-start = (bf16[2,24,1152]{2,1,0:T(8,128)(2,1)S(1)}, bf16[2,24,1152]{2,1,0:T(8,128)(2,1)S(1)}, u32[]{:S(2)}, u32[]{:S(2)}) collective-permute-start(bf16[2,24,1152]{2,1,0:T(8,128)(2,1)S(1)} %get-tuple-element.45), channel_id=1, source_target_pairs={{0,248},{8,0},{16,8},{24,16},{32,24},{40,32},{48,40},{56,48},{64,5... | collective-permute-start | bytes 331784 | tf_op jit(solution)/shard_map/ppermute | solution.py:795
  14.9 1.6 %fine_bias_spread.1.refs_8_.refs_10_ = f32[3456,128]{1,0:T(8,128)S(1)} custom-call(f32[6,23,4,144]{3,2,1,0:T(4,128)S(1)} %bitcast.11), custom_call_target="tpu_custom_call" | custom-call | flops 2000000000 | bytes 2000000 | tf_op jit(solution)/shard_map/fine_bias_spread/pallas_call | solution.py:182
  16.6 2.0 %fine_forward_1.1 = (bf16[144,192]{1,0:T(8,128)(2,1)S(1)}, bf16[72,192]{1,0:T(8,128)(2,1)S(1)}, bf16[3,144,192]{2,1,0:T(8,128)(2,1)S(1)}, bf16[864,72]{1,0:T(8,1...) custom-call(bf16[2,24,2304]{2,1,0:T(8,128)(2,1)S(1)} %copy-done.11, ...), custom_call_target="tpu_custom_call" | custom-call | flops 1500000000 | bytes 1500000 | tf_op jit(solution)/shard_map/fine_forward_1/pallas_call | solution.py:342
  18.7 1.5 %collective-permute-start.3 = (bf16[72,192]{1,0:T(8,128)(2,1)S(1)}, bf16[72,192]{1,0:T(8,128)(2,1)S(1)}, u32[]{:S(2)}, u32[]{:S(2)}) collective-permute-start(bf16[72,192]{1,0:T(8,128)(2,1)S(1)} %get-tuple-element.50), channel_id=1, source_target_pairs={{0,1},{1,2},{2,3},{3,4},{4,5},{5,6},{6,7},{7,0},{8,9},{9,10},{10,1... | collective-permute-start | bytes 82952 | tf_op jit(solution)/shard_map/ppermute | solution.py:795
  20.2 3.5 %fine_forward_3.1 = (bf16[432,192]{1,0:T(8,128)(2,1)S(1)}, bf16[3,432,192]{2,1,0:T(8,128)(2,1)S(1)}, bf16[2592,72]{1,0:T(8,128)(2,1)S(1)}, f32[432,192]{1,0:T(8,...) custom-call(bf16[2,24,2304]{2,1,0:T(8,128)(2,1)S(1)} %copy-done.11, ...), custom_call_target="tpu_custom_call" | custom-call | flops 3500000000 | bytes 3500000 | tf_op jit(solution)/shard_map/fine_forward_3/pallas_call | solution.py:342
  23.6 1.5 %collective-permute-done.3.strip_ref = bf16[72,192]{1,0:T(8,128)(2,1)S(1)} collective-permute-done((bf16[72,192]{1,0:T(8,128)(2,1)S(1)}, bf16[72,192]{1,0:T(8,128)(2,1)S(1)}, u32[]{:S(2)}, u32[]{:S(2)}) %collective-permute-start.3) | collective-permute-done | bytes 27680 | tf_op jit(solution)/shard_map/ppermute | solution.py:795
  25.2 1.5 %merge_forward.1 = (bf16[192,384]{1,0:T(8,128)(2,1)S(1)}, bf16[96,384]{1,0:T(8,128)(2,1)S(1)}, bf16[768,192]{1,0:T(8,128)(2,1)S(1)}) custom-call(bf16[432,192]{1,0:T(8,128)(2,1)S(1)} %get-tuple-element.46.y_ref, bf16[144,192]{1,0:T(8,128)(2,1)S(1)} %get-tuple-element.49.last_ref, bf16[72,192]{1,0:T(8,128)(2,1)S(1)} %collective-permute-done.3.strip_ref, ...), custom_call_target="tpu_custom_call" | custom-call | flops 1500000000 | bytes 1500000 | tf_op jit(solution)/shard_map/merge_forward/pallas_call | solution.py:389
  26.8 1.7 %collective-permute-start.5 = (bf16[96,384]{1,0:T(8,128)(2,1)S(1)}, bf16[96,384]{1,0:T(8,128)(2,1)S(1)}, u32[]{:S(2)}, u32[]{:S(2)}) collective-permute-start(bf16[96,384]{1,0:T(8,128)(2,1)S(1)} %get-tuple-element.52), channel_id=1, source_target_pairs={{0,8},{8,16},{16,24},{24,32},{32,40},{40,48},{48,56},{56,64},{64,7... | collective-permute-start | bytes 221192 | tf_op jit(solution)/shard_map/ppermute | solution.py:795
  28.6 1.2 %collective-permute-start.4 = (bf16[192,384]{1,0:T(8,128)(2,1)S(1)}, bf16[192,384]{1,0:T(8,128)(2,1)S(1)}, u32[]{:S(2)}, u32[]{:S(2)}) collective-permute-start(bf16[192,384]{1,0:T(8,128)(2,1)S(1)} %get-tuple-element.51.both_ref), channel_id=1, source_target_pairs={{0,8},{8,0},{16,24},{24,16},{32,40},{40,32},{48,56},{56,48},{64,72... | collective-permute-start | bytes 442376 | tf_op jit(solution)/shard_map/ppermute | solution.py:809
  29.8 1.6 %coarse_bias_spread.1.bias_ref = f32[2,1728,128]{2,1,0:T(8,128)S(1)} custom-call(f32[12,23,2,144]{3,2,1,0:T(2,128)S(1)} %bitcast.12, bf16[12,384,256]{2,1,0:T(8,128)(2,1)S(1)} %copy-done.19, bf16[384,256]{1,0:T(8,128)(2,1)S(1)} %copy-done.23), custom_call_target="tpu_custom_call" | custom-call | flops 2000000000 | bytes 2000000 | tf_op jit(solution)/shard_map/coarse_bias_spread/pallas_call | solution.py:229
  31.5 2.1 %collective-permute-done.6.odd_ref = bf16[96,384]{1,0:T(8,128)(2,1)S(1)} collective-permute-done((bf16[96,384]{1,0:T(8,128)(2,1)S(1)}, bf16[96,384]{1,0:T(8,128)(2,1)S(1)}, u32[]{:S(2)}, u32[]{:S(2)}) %collective-permute-start.6) | collective-permute-done | bytes 73760 | tf_op jit(solution)/shard_map/ppermute | solution.py:795
  33.6 6.8 %coarse_both.1 = (bf16[192,384]{1,0:T(8,128)(2,1)S(1)}, bf16[192,384]{1,0:T(8,128)(2,1)S(1)}, bf16[96,384]{1,0:T(8,128)(2,1)S(1)}, bf16[96,384]{1,0:T(8,128)(2,1...) custom-call(bf16[192,384]{1,0:T(8,128)(2,1)S(1)} %get-tuple-element.51.both_ref, ...), custom_call_target="tpu_custom_call" | custom-call | flops 7000000000 | bytes 7000000 | tf_op jit(solution)/shard_map/coarse_both/pallas_call | solution.py:534
  40.4 2.9 %collective-permute-start.8 = (bf16[192,384]{1,0:T(8,128)(2,1)S(1)}, bf16[192,384]{1,0:T(8,128)(2,1)S(1)}, u32[]{:S(2)}, u32[]{:S(2)}) collective-permute-start(bf16[192,384]{1,0:T(8,128)(2,1)S(1)} %get-tuple-element.57), channel_id=1, source_target_pairs={{0,8},{8,0},{16,24},{24,16},{32,40},{40,32},{48,56},{56,48},{64,72... | collective-permute-start | bytes 442376 | tf_op jit(solution)/shard_map/ppermute | solution.py:809
  44.0 1.3 %coarse_rest.1 = (bf16[12,2,2304]{2,1,0:T(2,128)(2,1)S(1)}, bf16[12,2,2304]{2,1,0:T(2,128)(2,1)S(1)}, bf16[432,128]{1,0:T(8,128)(2,1)S(1)}) custom-call(bf16[144,384]{1,0:T(8,128)(2,1)S(1)} %get-tuple-element.53.out_ref, f32[2,1728,128]{2,1,0:T(8,128)S(1)} %get-tuple-element.54.ds_ref, bf16[12,384,256]{2,1,0:T(8,128)(2,1)S(1)} %copy-done.19), custom_call_target="tpu_custom_call" | custom-call | flops 1500000000 | bytes 1500000 | tf_op jit(solution)/shard_map/coarse_rest/pallas_call | solution.py:516
  45.3 2.0 %collective-permute-done.9.even_ref = bf16[96,384]{1,0:T(8,128)(2,1)S(1)} collective-permute-done((bf16[96,384]{1,0:T(8,128)(2,1)S(1)}, bf16[96,384]{1,0:T(8,128)(2,1)S(1)}, u32[]{:S(2)}, u32[]{:S(2)}) %collective-permute-start.9) | collective-permute-done | bytes 73760 | tf_op jit(solution)/shard_map/ppermute | solution.py:795
  47.3 1.1 %merge_backward.1 = (bf16[432,192]{1,0:T(8,128)(2,1)S(1)}, bf16[144,192]{1,0:T(8,128)(2,1)S(1)}, bf16[72,192]{1,0:T(8,128)(2,1)S(1)}) custom-call(bf16[432,128]{1,0:T(8,128)(2,1)S(1)} %get-tuple-element.55._.coarse_ref, bf16[192,384]{1,0:T(8,128)(2,1)S(1)} %get-tuple-element.56.g_ref, bf16[192,384]{1,0:T(8,128)(2,1)S(1)} %collective-permute-done.8.pg_ref, ...), custom_call_target="tpu_custom_call" | custom-call | flops 1000000000 | bytes 1000000 | tf_op jit(solution)/shard_map/merge_backward/pallas_call | solution.py:587
  48.5 2.5 %collective-permute-start.11 = (bf16[72,192]{1,0:T(8,128)(2,1)S(1)}, bf16[72,192]{1,0:T(8,128)(2,1)S(1)}, u32[]{:S(2)}, u32[]{:S(2)}) collective-permute-start(bf16[72,192]{1,0:T(8,128)(2,1)S(1)} %get-tuple-element.62), channel_id=1, source_target_pairs={{0,7},{1,0},{2,1},{3,2},{4,3},{5,4},{6,5},{7,6},{8,15},{9,8},{10,9... | collective-permute-start | bytes 82952 | tf_op jit(solution)/shard_map/ppermute | solution.py:795
  51.0 4.9 %fine_backward_3.1 = (bf16[2,18,2304]{2,1,0:T(8,128)(2,1)S(1)}, f32[216,256]{1,0:T(8,128)S(1)}) custom-call(bf16[432,192]{1,0:T(8,128)(2,1)S(1)} %get-tuple-element.63.refs_0_, bf16[3,432,192]{2,1,0:T(8,128)(2,1)S(1)} %get-tuple-element.64.refs_1_, bf16[2592,72]{1,0:T(8,128)(2,1)S(1)} %get-tuple-element.65.refs_2_, ...), custom_call_target="tpu_custom_call" | custom-call | flops 6000000000 | bytes 6000000 | tf_op jit(solution)/shard_map/fine_backward_3/pallas_call | solution.py:698
  55.9 2.3 %fine_backward_1.1 = (bf16[2,21,2304]{2,1,0:T(8,128)(2,1)S(1)}, bf16[2,3,2304]{2,1,0:T(4,128)(2,1)S(1)}, bf16[288,128]{1,0:T(8,128)(2,1)S(1)}, bf16[288,128]{1,0:T(8,128)(2,1)S(1)}) custom-call(bf16[144,192]{1,0:T(8,128)(2,1)S(1)} %get-tuple-element.61.refs_0_, bf16[72,192]{1,0:T(8,128)(2,1)S(1)} %collective-permute-done.11.refs_1_, ...), custom_call_target="tpu_custom_call" | custom-call | flops 2000000000 | bytes 2000000 | tf_op jit(solution)/shard_map/fine_backward_1/pallas_call | solution.py:698
  58.3 1.8 %collective-permute-start.12 = (bf16[288,128]{1,0:T(8,128)(2,1)S(1)}, bf16[288,128]{1,0:T(8,128)(2,1)S(1)}, u32[]{:S(2)}, u32[]{:S(2)}) collective-permute-start(bf16[288,128]{1,0:T(8,128)(2,1)S(1)} %get-tuple-element.77), channel_id=1, source_target_pairs={{0,8},{8,0},{16,24},{24,16},{32,40},{40,32},{48,56},{56,48},{64,72... | collective-permute-start | bytes 221192 | tf_op jit(solution)/shard_map/ppermute | solution.py:809
  61.7 3.6 %all-to-all-start = ((bf16[16,48,128]{2,1,0:T(8,128)(2,1)}), bf16[16,48,128]{2,1,0:T(8,128)(2,1)S(1)}, u32[]{:S(2)}, u32[]{:S(2)}) async-start(bf16[16,48,128]{2,1,0:T(8,128)(2,1)} %bitcast.4), calls=%async_computation | async-start | bytes 393216 | tf_op jit(solution)/shard_map/all_to_all | solution.py:866
  65.3 2.0 %collective-permute-start.13 = (bf16[2,3,2304]{2,1,0:T(4,128)(2,1)S(1)}, bf16[2,3,2304]{2,1,0:T(4,128)(2,1)S(1)}, u32[]{:S(2)}, u32[]{:S(2)}) collective-permute-start(bf16[2,3,2304]{2,1,0:T(4,128)(2,1)S(1)} %get-tuple-element.78), channel_id=1, source_target_pairs={{0,1},{1,2},{2,3},{3,4},{4,5},{5,6},{6,7},{7,0},{8,9},{9,10},{10,1... | collective-permute-start | bytes 82952 | tf_op jit(solution)/shard_map/ppermute | solution.py:795
  67.3 4.5 %collective-permute-done.13._ = bf16[2,3,2304]{2,1,0:T(4,128)(2,1)S(1)} collective-permute-done((bf16[2,3,2304]{2,1,0:T(4,128)(2,1)S(1)}, bf16[2,3,2304]{2,1,0:T(4,128)(2,1)S(1)}, u32[]{:S(2)}, u32[]{:S(2)}) %collective-permute-start.13) | collective-permute-done | bytes 27680 | tf_op jit(solution)/shard_map/ppermute | solution.py:795
  71.8 1.0 %all-to-all-done.parts_ref = bf16[16,48,128]{2,1,0:T(8,128)(2,1)S(1)} async-done(((bf16[16,48,128]{2,1,0:T(8,128)(2,1)}), bf16[16,48,128]{2,1,0:T(8,128)(2,1)S(1)}, u32[]{:S(2)}, u32[]{:S(2)}) %all-to-all-start) | async-done | bytes 196640 | tf_op jit(solution)/shard_map/all_to_all | solution.py:866
  73.5 6.7 %all-to-all-start.1 = ((bf16[16,48,128]{2,1,0:T(8,128)(2,1)}), bf16[16,48,128]{2,1,0:T(8,128)(2,1)S(1)}, u32[]{:S(2)}, u32[]{:S(2)}) async-start(bf16[16,48,128]{2,1,0:T(8,128)(2,1)} %chip_sums.1), calls=%async_computation.1 | async-start | bytes 393216 | tf_op jit(solution)/shard_map/all_to_all | solution.py:867
  80.2 2.2 %collective-permute-start.15 = (bf16[12,2,2304]{2,1,0:T(2,128)(2,1)S(1)}, bf16[12,2,2304]{2,1,0:T(2,128)(2,1)S(1)}, u32[]{:S(2)}, u32[]{:S(2)}) collective-permute-start(bf16[12,2,2304]{2,1,0:T(2,128)(2,1)S(1)} %get-tuple-element.80), channel_id=1, source_target_pairs={{0,8},{8,0},{16,24},{24,16},{32,40},{40,32},{48,56},{56,48},{64,72... | collective-permute-start | bytes 331784 | tf_op jit(solution)/shard_map/ppermute | solution.py:809
  82.5 1.5 %collective-permute-start.16 = (bf16[2,24,1152]{2,1,0:T(8,128)(2,1)S(1)}, bf16[2,24,1152]{2,1,0:T(8,128)(2,1)S(1)}, u32[]{:S(2)}, u32[]{:S(2)}) collective-permute-start(bf16[2,24,1152]{2,1,0:T(8,128)(2,1)S(1)} %fusion), channel_id=1, source_target_pairs={{0,8},{8,16},{16,24},{24,32},{32,40},{40,48},{48,56},{56,64},{64,7... | collective-permute-start | bytes 331784 | tf_op jit(solution)/shard_map/ppermute | solution.py:795
  84.0 3.7 %all-to-all-done.1 = bf16[16,48,128]{2,1,0:T(8,128)(2,1)S(1)} async-done(((bf16[16,48,128]{2,1,0:T(8,128)(2,1)}), bf16[16,48,128]{2,1,0:T(8,128)(2,1)S(1)}, u32[]{:S(2)}, u32[]{:S(2)}) %all-to-all-start.1) | async-done | bytes 196640 | tf_op jit(solution)/shard_map/all_to_all | solution.py:867
  87.7 4.2 %collective-permute-start.14 = (bf16[768,128]{1,0:T(8,128)(2,1)S(1)}, bf16[768,128]{1,0:T(8,128)(2,1)S(1)}, u32[]{:S(2)}, u32[]{:S(2)}) collective-permute-start(bf16[768,128]{1,0:T(8,128)(2,1)S(1)} %bitcast.9), channel_id=1, source_target_pairs={{0,8},{8,0},{16,24},{24,16},{32,40},{40,32},{48,56},{56,48},{64,72... | collective-permute-start | bytes 589832 | tf_op jit(solution)/shard_map/ppermute | solution.py:809
  92.9 2.1 %results.1 = (bf16[12,2,2304]{2,1,0:T(2,128)(2,1)}, bf16[2,24,2304]{2,1,0:T(8,128)(2,1)}, f32[6,23,4,144]{3,2,1,0:T(4,128)}, f32[12,23,2,144]{3,2,1,0:T(2,128)}) custom-call(bf16[768,128]{1,0:T(8,128)(2,1)S(1)} %bitcast.10, bf16[768,128]{1,0:T(8,128)(2,1)S(1)} %collective-permute-done.14.got_ref, bf16[12,2,2304]{2,1,0:T(2,128)(2,1)S(1)} %get-tuple-element.79.okeep_ref, ...), custom_call_target="tpu_custom_call" | custom-call | flops 2000000000 | bytes 2000000 | tf_op jit(solution)/shard_map/results/pallas_call | solution.py:777
  (72 shorter events, 5.7 us)
Async XLA Ops:
  0.6 14.2 %copy-start.4 = (f32[4,6,23,144]{3,0,2,1:T(4,128)S(1)}, f32[4,6,23,144]{3,0,2,1:T(4,128)}, u32[]{:S(2)}) copy-start(f32[4,6,23,144]{3,0,2,1:T(4,128)} %param.31) | copy-start | bytes 953860
  0.6 30.8 %collective-permute-start.7 = (bf16[12,2,2304]{2,1,0:T(2,128)(2,1)}, bf16[12,2,2304]{2,1,0:T(2,128)(2,1)S(1)}, u32[]{:S(2)}, u32[]{:S(2)}) collective-permute-start(bf16[12,2,2304]{2,1,0:T(2,128)(2,1)} %bitcast.17), channel_id=1, source_target_pairs={{0,8},{8,0},{16,24},{24,16},{32,40},{40,32},{48,56},{56,48},{64,72... | collective-permute-start | bytes 331784 | tf_op jit(solution)/shard_map/ppermute | solution.py:809
  4.9 11.6 %collective-permute-start.1 = (bf16[2,3,1152]{2,1,0:T(4,128)(2,1)S(1)}, bf16[2,3,1152]{2,1,0:T(4,128)(2,1)S(1)}, u32[]{:S(2)}, u32[]{:S(2)}) collective-permute-start(bf16[2,3,1152]{2,1,0:T(4,128)(2,1)S(1)} %get-tuple-element.47), channel_id=1, source_target_pairs={{0,7},{1,0},{2,1},{3,2},{4,3},{5,4},{6,5},{7,6},{8,15},{9,8},{10,9... | collective-permute-start | bytes 41480 | tf_op jit(solution)/shard_map/ppermute | solution.py:795
  8.4 8.2 %collective-permute-start.2 = (bf16[2,3,1152]{2,1,0:T(4,128)(2,1)S(1)}, bf16[2,3,1152]{2,1,0:T(4,128)(2,1)S(1)}, u32[]{:S(2)}, u32[]{:S(2)}) collective-permute-start(bf16[2,3,1152]{2,1,0:T(4,128)(2,1)S(1)} %get-tuple-element.48), channel_id=1, source_target_pairs={{0,255},{1,248},{2,249},{3,250},{4,251},{5,252},{6,253},{7,254},{8... | collective-permute-start | bytes 41480 | tf_op jit(solution)/shard_map/ppermute | solution.py:805
  8.7 7.9 %collective-permute-start = (bf16[2,24,1152]{2,1,0:T(8,128)(2,1)S(1)}, bf16[2,24,1152]{2,1,0:T(8,128)(2,1)S(1)}, u32[]{:S(2)}, u32[]{:S(2)}) collective-permute-start(bf16[2,24,1152]{2,1,0:T(8,128)(2,1)S(1)} %get-tuple-element.45), channel_id=1, source_target_pairs={{0,248},{8,0},{16,8},{24,16},{32,24},{40,32},{48,40},{56,48},{64,5... | collective-permute-start | bytes 331784 | tf_op jit(solution)/shard_map/ppermute | solution.py:795
  18.6 6.5 %copy-start.3 = (bf16[768,384]{1,0:T(8,128)(2,1)S(1)}, bf16[768,384]{1,0:T(8,128)(2,1)}, u32[]{:S(2)}) copy-start(bf16[768,384]{1,0:T(8,128)(2,1)} %w_ref.3) | copy-start | bytes 1769476
  18.7 6.5 %copy-start.14 = (f32[768]{0:T(1024)S(1)}, f32[768]{0:T(1024)}, u32[]{:S(2)}) copy-start(f32[768]{0:T(1024)} %gain_ref.3) | copy-start | bytes 9220
  18.7 6.5 %copy-start.20 = (bf16[768,648]{1,0:T(8,128)(2,1)S(1)}, bf16[768,648]{1,0:T(8,128)(2,1)}, u32[]{:S(2)}) copy-start(bf16[768,648]{1,0:T(8,128)(2,1)} %constant.14.clone.pick_ref) | copy-start | bytes 2985988
  18.7 6.5 %collective-permute-start.3 = (bf16[72,192]{1,0:T(8,128)(2,1)S(1)}, bf16[72,192]{1,0:T(8,128)(2,1)S(1)}, u32[]{:S(2)}, u32[]{:S(2)}) collective-permute-start(bf16[72,192]{1,0:T(8,128)(2,1)S(1)} %get-tuple-element.50), channel_id=1, source_target_pairs={{0,1},{1,2},{2,3},{3,4},{4,5},{5,6},{6,7},{7,0},{8,9},{9,10},{10,1... | collective-permute-start | bytes 82952 | tf_op jit(solution)/shard_map/ppermute | solution.py:795
  25.2 4.5 %copy-start.5 = (f32[2,12,23,144]{3,0,2,1:T(2,128)S(1)}, f32[2,12,23,144]{3,0,2,1:T(2,128)}, u32[]{:S(2)}) copy-start(f32[2,12,23,144]{3,0,2,1:T(2,128)} %param.40) | copy-start | bytes 953860
  25.2 4.5 %copy-start.19 = (bf16[12,384,256]{2,1,0:T(8,128)(2,1)S(1)}, bf16[12,384,256]{2,1,0:T(8,128)(2,1)}, u32[]{:S(2)}) copy-start(bf16[12,384,256]{2,1,0:T(8,128)(2,1)} %constant.12.clone.onehot_ref.ec_ref) | copy-start | bytes 7077892
  25.2 4.5 %copy-start.23 = (bf16[384,256]{1,0:T(8,128)(2,1)S(1)}, bf16[384,256]{1,0:T(8,128)(2,1)}, u32[]{:S(2)}) copy-start(bf16[384,256]{1,0:T(8,128)(2,1)} %constant.13.clone.tail_ref) | copy-start | bytes 589828
  26.7 6.8 %collective-permute-start.6 = (bf16[96,384]{1,0:T(8,128)(2,1)S(1)}, bf16[96,384]{1,0:T(8,128)(2,1)S(1)}, u32[]{:S(2)}, u32[]{:S(2)}) collective-permute-start(bf16[96,384]{1,0:T(8,128)(2,1)S(1)} %get-tuple-element.52), channel_id=1, source_target_pairs={{0,16},{8,24},{16,32},{24,40},{32,48},{40,56},{48,64},{56,72},{64,... | collective-permute-start | bytes 221192 | tf_op jit(solution)/shard_map/ppermute | solution.py:795
  26.8 6.7 %collective-permute-start.5 = (bf16[96,384]{1,0:T(8,128)(2,1)S(1)}, bf16[96,384]{1,0:T(8,128)(2,1)S(1)}, u32[]{:S(2)}, u32[]{:S(2)}) collective-permute-start(bf16[96,384]{1,0:T(8,128)(2,1)S(1)} %get-tuple-element.52), channel_id=1, source_target_pairs={{0,8},{8,16},{16,24},{24,32},{32,40},{40,48},{48,56},{56,64},{64,7... | collective-permute-start | bytes 221192 | tf_op jit(solution)/shard_map/ppermute | solution.py:795
  28.6 5.0 %collective-permute-start.4 = (bf16[192,384]{1,0:T(8,128)(2,1)S(1)}, bf16[192,384]{1,0:T(8,128)(2,1)S(1)}, u32[]{:S(2)}, u32[]{:S(2)}) collective-permute-start(bf16[192,384]{1,0:T(8,128)(2,1)S(1)} %get-tuple-element.51.both_ref), channel_id=1, source_target_pairs={{0,8},{8,0},{16,24},{24,16},{32,40},{40,32},{48,56},{56,48},{64,72... | collective-permute-start | bytes 442376 | tf_op jit(solution)/shard_map/ppermute | solution.py:809
  29.7 3.8 %copy-start = (bf16[384,1536]{1,0:T(8,128)(2,1)S(1)}, bf16[384,1536]{1,0:T(8,128)(2,1)}, u32[]{:S(2)}) copy-start(bf16[384,1536]{1,0:T(8,128)(2,1)} %we_ref.1) | copy-start | bytes 3538948
  29.7 3.8 %copy-start.1 = (bf16[1536,384]{1,0:T(8,128)(2,1)S(1)}, bf16[1536,384]{1,0:T(8,128)(2,1)}, u32[]{:S(2)}) copy-start(bf16[1536,384]{1,0:T(8,128)(2,1)} %wr_ref.1) | copy-start | bytes 3538948
  29.8 3.8 %copy-start.2 = (bf16[384,1152]{1,0:T(8,128)(2,1)S(1)}, bf16[384,1152]{1,0:T(8,128)(2,1)}, u32[]{:S(2)}) copy-start(bf16[384,1152]{1,0:T(8,128)(2,1)} %wa_ref.1) | copy-start | bytes 2654212
  29.8 3.8 %copy-start.6 = (bf16[384,384]{1,0:T(8,128)(2,1)S(1)}, bf16[384,384]{1,0:T(8,128)(2,1)}, u32[]{:S(2)}) copy-start(bf16[384,384]{1,0:T(8,128)(2,1)} %wp_ref.1) | copy-start | bytes 884740
  29.8 3.8 %copy-start.12 = (bf16[2,12,2304]{2,0,1:T(2,128)(2,1)S(1)}, bf16[2,12,2304]{2,0,1:T(2,128)(2,1)}, u32[]{:S(2)}) copy-start(bf16[2,12,2304]{2,0,1:T(2,128)(2,1)} %param.41) | copy-start | bytes 331780
  40.4 7.0 %collective-permute-start.8 = (bf16[192,384]{1,0:T(8,128)(2,1)S(1)}, bf16[192,384]{1,0:T(8,128)(2,1)S(1)}, u32[]{:S(2)}, u32[]{:S(2)}) collective-permute-start(bf16[192,384]{1,0:T(8,128)(2,1)S(1)} %get-tuple-element.57), channel_id=1, source_target_pairs={{0,8},{8,0},{16,24},{24,16},{32,40},{40,32},{48,56},{56,48},{64,72... | collective-permute-start | bytes 442376 | tf_op jit(solution)/shard_map/ppermute | solution.py:809
  43.2 4.1 %collective-permute-start.9 = (bf16[96,384]{1,0:T(8,128)(2,1)S(1)}, bf16[96,384]{1,0:T(8,128)(2,1)S(1)}, u32[]{:S(2)}, u32[]{:S(2)}) collective-permute-start(bf16[96,384]{1,0:T(8,128)(2,1)S(1)} %get-tuple-element.58), channel_id=1, source_target_pairs={{0,248},{8,0},{16,8},{24,16},{32,24},{40,32},{48,40},{56,48},{64,5... | collective-permute-start | bytes 221192 | tf_op jit(solution)/shard_map/ppermute | solution.py:795
  43.3 4.0 %collective-permute-start.10 = (bf16[96,384]{1,0:T(8,128)(2,1)S(1)}, bf16[96,384]{1,0:T(8,128)(2,1)S(1)}, u32[]{:S(2)}, u32[]{:S(2)}) collective-permute-start(bf16[96,384]{1,0:T(8,128)(2,1)S(1)} %get-tuple-element.59), channel_id=1, source_target_pairs={{0,240},{8,248},{16,0},{24,8},{32,16},{40,24},{48,32},{56,40},{64,... | collective-permute-start | bytes 221192 | tf_op jit(solution)/shard_map/ppermute | solution.py:795
  48.5 7.4 %collective-permute-start.11 = (bf16[72,192]{1,0:T(8,128)(2,1)S(1)}, bf16[72,192]{1,0:T(8,128)(2,1)S(1)}, u32[]{:S(2)}, u32[]{:S(2)}) collective-permute-start(bf16[72,192]{1,0:T(8,128)(2,1)S(1)} %get-tuple-element.62), channel_id=1, source_target_pairs={{0,7},{1,0},{2,1},{3,2},{4,3},{5,4},{6,5},{7,6},{8,15},{9,8},{10,9... | collective-permute-start | bytes 82952 | tf_op jit(solution)/shard_map/ppermute | solution.py:795
  51.0 4.9 %copy-start.24 = (bf16[144,72]{1,0:T(8,128)(2,1)S(1)}, bf16[144,72]{1,0:T(8,128)(2,1)}, u32[]{:S(2)}) copy-start(bf16[144,72]{1,0:T(8,128)(2,1)} %constant.17.clone.refs_2_) | copy-start | bytes 62212
  58.3 2.8 %collective-permute-start.12 = (bf16[288,128]{1,0:T(8,128)(2,1)S(1)}, bf16[288,128]{1,0:T(8,128)(2,1)S(1)}, u32[]{:S(2)}, u32[]{:S(2)}) collective-permute-start(bf16[288,128]{1,0:T(8,128)(2,1)S(1)} %get-tuple-element.77), channel_id=1, source_target_pairs={{0,8},{8,0},{16,24},{24,16},{32,40},{40,32},{48,56},{56,48},{64,72... | collective-permute-start | bytes 221192 | tf_op jit(solution)/shard_map/ppermute | solution.py:809
  61.7 11.1 %all-to-all-start = ((bf16[16,48,128]{2,1,0:T(8,128)(2,1)}), bf16[16,48,128]{2,1,0:T(8,128)(2,1)S(1)}, u32[]{:S(2)}, u32[]{:S(2)}) async-start(bf16[16,48,128]{2,1,0:T(8,128)(2,1)} %bitcast.4), calls=%async_computation | async-start | bytes 393216 | tf_op jit(solution)/shard_map/all_to_all | solution.py:866
  65.3 6.5 %collective-permute-start.13 = (bf16[2,3,2304]{2,1,0:T(4,128)(2,1)S(1)}, bf16[2,3,2304]{2,1,0:T(4,128)(2,1)S(1)}, u32[]{:S(2)}, u32[]{:S(2)}) collective-permute-start(bf16[2,3,2304]{2,1,0:T(4,128)(2,1)S(1)} %get-tuple-element.78), channel_id=1, source_target_pairs={{0,1},{1,2},{2,3},{3,4},{4,5},{5,6},{6,7},{7,0},{8,9},{9,10},{10,1... | collective-permute-start | bytes 82952 | tf_op jit(solution)/shard_map/ppermute | solution.py:795
  73.5 14.2 %all-to-all-start.1 = ((bf16[16,48,128]{2,1,0:T(8,128)(2,1)}), bf16[16,48,128]{2,1,0:T(8,128)(2,1)S(1)}, u32[]{:S(2)}, u32[]{:S(2)}) async-start(bf16[16,48,128]{2,1,0:T(8,128)(2,1)} %chip_sums.1), calls=%async_computation.1 | async-start | bytes 393216 | tf_op jit(solution)/shard_map/all_to_all | solution.py:867
  80.2 11.7 %collective-permute-start.15 = (bf16[12,2,2304]{2,1,0:T(2,128)(2,1)S(1)}, bf16[12,2,2304]{2,1,0:T(2,128)(2,1)S(1)}, u32[]{:S(2)}, u32[]{:S(2)}) collective-permute-start(bf16[12,2,2304]{2,1,0:T(2,128)(2,1)S(1)} %get-tuple-element.80), channel_id=1, source_target_pairs={{0,8},{8,0},{16,24},{24,16},{32,40},{40,32},{48,56},{56,48},{64,72... | collective-permute-start | bytes 331784 | tf_op jit(solution)/shard_map/ppermute | solution.py:809
  82.5 9.5 %collective-permute-start.16 = (bf16[2,24,1152]{2,1,0:T(8,128)(2,1)S(1)}, bf16[2,24,1152]{2,1,0:T(8,128)(2,1)S(1)}, u32[]{:S(2)}, u32[]{:S(2)}) collective-permute-start(bf16[2,24,1152]{2,1,0:T(8,128)(2,1)S(1)} %fusion), channel_id=1, source_target_pairs={{0,8},{8,16},{16,24},{24,32},{32,40},{40,48},{48,56},{56,64},{64,7... | collective-permute-start | bytes 331784 | tf_op jit(solution)/shard_map/ppermute | solution.py:795
  87.7 5.2 %collective-permute-start.14 = (bf16[768,128]{1,0:T(8,128)(2,1)S(1)}, bf16[768,128]{1,0:T(8,128)(2,1)S(1)}, u32[]{:S(2)}, u32[]{:S(2)}) collective-permute-start(bf16[768,128]{1,0:T(8,128)(2,1)S(1)} %bitcast.9), channel_id=1, source_target_pairs={{0,8},{8,0},{16,24},{24,16},{32,40},{40,32},{48,56},{56,48},{64,72... | collective-permute-start | bytes 589832 | tf_op jit(solution)/shard_map/ppermute | solution.py:809
  (12 other events, 27.7 us)

commit v4 on v3

--- a/solution.py
+++ b/solution.py
@@ -710,15 +710,18 @@
 
 
 def partial_kernel(keep_ref, got_ref, coarse_ref, out_ref):
-    out_ref[:288, :] = (keep_ref[...].astype(F32) + got_ref[...].astype(F32)).astype(BF16)
-    out_ref[288:720, :] = coarse_ref[...]
-    out_ref[720:, :] = jnp.zeros((48, 128), BF16)
+    fine = keep_ref[...].astype(F32) + got_ref[...].astype(F32)
+    coarse = coarse_ref[...].astype(F32)
+    out_ref[:144, :] = fine[:144].astype(BF16)
+    out_ref[144:288, :] = (pltpu.roll(fine[144:], 48, 1) + coarse[288:]).astype(BF16)
+    out_ref[288:576, :] = coarse[:288].astype(BF16)
+    out_ref[576:, :] = jnp.zeros((64, 128), BF16)
 
 
 def partial_call(keep, got, coarse):
     return pl.pallas_call(
         partial_kernel,
-        out_shape=jax.ShapeDtypeStruct((768, 128), BF16),
+        out_shape=jax.ShapeDtypeStruct((640, 128), BF16),
         in_specs=vmem(3),
         compiler_params=pltpu.CompilerParams(vmem_limit_bytes=4 << 20),
         cost_estimate=cost(0.5),
@@ -756,13 +759,15 @@
         source = jnp.where(par == s, mine_ref[...].astype(F32), got_ref[...].astype(F32))
         for jm in range(6):
             tile = source[jm // 5 * 144 : jm // 5 * 144 + 144]
-            if jm % 5:
-                tile = pltpu.roll(tile, 128 - jm % 5 * 24, 1)
+            lane = 48 if jm == 5 else jm * 24
+            if lane:
+                tile = pltpu.roll(tile, 128 - lane, 1)
             base = s * 1728
             cols_f[pl.ds(base + jm, 144, stride=12), :] = jnp.where(level, tile, 0.0)
             cols_f[pl.ds(base + 6 + jm, 144, stride=12), :] = jnp.where(level, 0.0, tile)
         for b in range(12):
-            tile = source[288 + b // 5 * 144 : 288 + b // 5 * 144 + 144]
+            place = (288, 432, 144)[b // 5]
+            tile = source[place : place + 144]
             if b % 5:
                 tile = pltpu.roll(tile, 128 - b % 5 * 24, 1)
             cols_c[pl.ds(s * 1728 + b, 144, stride=12), :] = tile
@@ -861,11 +866,11 @@
         final, grads, saved_last, fine_weights, ef
     )
     edge = shifted(edge, "lat", 1)
-    partial = partial_call(table_keep, swapped(table_send), table_coarse).reshape(16, 48, 128)
+    partial = partial_call(table_keep, swapped(table_send), table_coarse).reshape(16, 40, 128)
     chips = [[2 * k + c for k in range(16)] for c in range(2)]
     partial = lax.all_to_all(partial, "lon", 0, 0, tiled=True, axis_index_groups=chips)
     sums = lax.all_to_all(sum_call(partial, edge), "lon", 0, 0, tiled=True, axis_index_groups=chips)
-    sums = sums.reshape(768, 128)
+    sums = sums.reshape(640, 128)
     band = jnp.concatenate([edge, own], axis=1)
     right = shifted(band[:, :, band.shape[2] // 2 :], "lon", 1)
     coarse_out, grad_tokens, grad_fine, grad_coarse = table_call(

time: 95.3 us -> 94.8 us (level)
  no operation moved by 1% of the time
where the time goes in v4:
time: 94.8 us; the launch traced here: 94.5 us
  starting transfers between devices  45.5 us (48%)
  Pallas kernels  30.2 us (32%)
  waiting for transfers between devices  16.5 us (17%)
  local copies, waits for them, and re-layouts  1.07 us (1%)
  between operations  1.07 us (1%)
    ppermute x10, starting transfers between devices, shifted(): lax.ppermute(value, axis, [(s, (s + steps) % count) for s in range(count)])  19.8 us
    ppermute x6, starting transfers between devices, swapped(): lax.ppermute(value, 'lon', [(s, s ^ 1) for s in range(lax.axis_size('lon'...  15.4 us
    ppermute x10, waiting for transfers between devices, shifted(): lax.ppermute(value, axis, [(s, (s + steps) % count) for s in range(count)])  10.3 us
    pallas_call x2, Pallas kernels, fine_back_call(): pl.pallas_call(functools.partial(fine_back_kernel, windows), out_shape=ou...  7.23 us
    pallas_call x1, Pallas kernels, coarse_call(): pl.pallas_call(coarse_kernel, out_shape=(shape((192, C2), BF16), shape((1...  6.76 us
    all_to_all x1, starting transfers between devices, shards(): lax.all_to_all(sum_call(partial, edge), 'lon', 0, 0, tiled=True, axis_ind...  6.53 us
    pallas_call x2, Pallas kernels, fine_call(): pl.pallas_call(functools.partial(fine_kernel, windows), out_shape=(shape(...  5.45 us
    all_to_all x1, waiting for transfers between devices, shards(): lax.all_to_all(sum_call(partial, edge), 'lon', 0, 0, tiled=True, axis_ind...  3.59 us
  transfers between devices with their start and end apart: 19, of which 8 were waited for; matrix products, arithmetic and copies ran while one was open for 0% of the time, Pallas kernels for 17%

profile of v4, /device:TPU:1, one launch (start us, length us, event | category | flops | bytes accessed | tf_op | source)
XLA Modules:
  0.0 94.5 jit_solution(10341985938938179087)
XLA Ops:
  0.6 3.3 %collective-permute-start.7 = (bf16[12,2,2304]{2,1,0:T(2,128)(2,1)}, bf16[12,2,2304]{2,1,0:T(2,128)(2,1)S(1)}, u32[]{:S(2)}, u32[]{:S(2)}) collective-permute-start(bf16[12,2,2304]{2,1,0:T(2,128)(2,1)} %bitcast.17), channel_id=1, source_target_pairs={{0,8},{8,0},{16,24},{24,16},{32,40},{40,32},{48,56},{56,48},{64,72... | collective-permute-start | bytes 331784 | tf_op jit(solution)/shard_map/ppermute | solution.py:814
  4.0 0.9 copy-done.10
  4.9 3.5 %collective-permute-start.1 = (bf16[2,3,1152]{2,1,0:T(4,128)(2,1)S(1)}, bf16[2,3,1152]{2,1,0:T(4,128)(2,1)S(1)}, u32[]{:S(2)}, u32[]{:S(2)}) collective-permute-start(bf16[2,3,1152]{2,1,0:T(4,128)(2,1)S(1)} %get-tuple-element.47), channel_id=1, source_target_pairs={{0,7},{1,0},{2,1},{3,2},{4,3},{5,4},{6,5},{7,6},{8,15},{9,8},{10,9... | collective-permute-start | bytes 41480 | tf_op jit(solution)/shard_map/ppermute | solution.py:800
  8.7 6.2 %collective-permute-start = (bf16[2,24,1152]{2,1,0:T(8,128)(2,1)S(1)}, bf16[2,24,1152]{2,1,0:T(8,128)(2,1)S(1)}, u32[]{:S(2)}, u32[]{:S(2)}) collective-permute-start(bf16[2,24,1152]{2,1,0:T(8,128)(2,1)S(1)} %get-tuple-element.45), channel_id=1, source_target_pairs={{0,248},{8,0},{16,8},{24,16},{32,24},{40,32},{48,40},{56,48},{64,5... | collective-permute-start | bytes 331784 | tf_op jit(solution)/shard_map/ppermute | solution.py:800
  14.9 1.6 %fine_bias_spread.1.refs_8_.refs_10_ = f32[3456,128]{1,0:T(8,128)S(1)} custom-call(f32[6,23,4,144]{3,2,1,0:T(4,128)S(1)} %bitcast.11), custom_call_target="tpu_custom_call" | custom-call | flops 2000000000 | bytes 2000000 | tf_op jit(solution)/shard_map/fine_bias_spread/pallas_call | solution.py:182
  16.6 2.0 %fine_forward_1.1 = (bf16[144,192]{1,0:T(8,128)(2,1)S(1)}, bf16[72,192]{1,0:T(8,128)(2,1)S(1)}, bf16[3,144,192]{2,1,0:T(8,128)(2,1)S(1)}, bf16[864,72]{1,0:T(8,1...) custom-call(bf16[2,24,2304]{2,1,0:T(8,128)(2,1)S(1)} %copy-done.11, ...), custom_call_target="tpu_custom_call" | custom-call | flops 1500000000 | bytes 1500000 | tf_op jit(solution)/shard_map/fine_forward_1/pallas_call | solution.py:342
  18.7 1.5 %collective-permute-start.3 = (bf16[72,192]{1,0:T(8,128)(2,1)S(1)}, bf16[72,192]{1,0:T(8,128)(2,1)S(1)}, u32[]{:S(2)}, u32[]{:S(2)}) collective-permute-start(bf16[72,192]{1,0:T(8,128)(2,1)S(1)} %get-tuple-element.50), channel_id=1, source_target_pairs={{0,1},{1,2},{2,3},{3,4},{4,5},{5,6},{6,7},{7,0},{8,9},{9,10},{10,1... | collective-permute-start | bytes 82952 | tf_op jit(solution)/shard_map/ppermute | solution.py:800
  20.2 3.5 %fine_forward_3.1 = (bf16[432,192]{1,0:T(8,128)(2,1)S(1)}, bf16[3,432,192]{2,1,0:T(8,128)(2,1)S(1)}, bf16[2592,72]{1,0:T(8,128)(2,1)S(1)}, f32[432,192]{1,0:T(8,...) custom-call(bf16[2,24,2304]{2,1,0:T(8,128)(2,1)S(1)} %copy-done.11, ...), custom_call_target="tpu_custom_call" | custom-call | flops 3500000000 | bytes 3500000 | tf_op jit(solution)/shard_map/fine_forward_3/pallas_call | solution.py:342
  23.6 1.5 %collective-permute-done.3.strip_ref = bf16[72,192]{1,0:T(8,128)(2,1)S(1)} collective-permute-done((bf16[72,192]{1,0:T(8,128)(2,1)S(1)}, bf16[72,192]{1,0:T(8,128)(2,1)S(1)}, u32[]{:S(2)}, u32[]{:S(2)}) %collective-permute-start.3) | collective-permute-done | bytes 27680 | tf_op jit(solution)/shard_map/ppermute | solution.py:800
  25.2 1.5 %merge_forward.1 = (bf16[192,384]{1,0:T(8,128)(2,1)S(1)}, bf16[96,384]{1,0:T(8,128)(2,1)S(1)}, bf16[768,192]{1,0:T(8,128)(2,1)S(1)}) custom-call(bf16[432,192]{1,0:T(8,128)(2,1)S(1)} %get-tuple-element.46.y_ref, bf16[144,192]{1,0:T(8,128)(2,1)S(1)} %get-tuple-element.49.last_ref, bf16[72,192]{1,0:T(8,128)(2,1)S(1)} %collective-permute-done.3.strip_ref, ...), custom_call_target="tpu_custom_call" | custom-call | flops 1500000000 | bytes 1500000 | tf_op jit(solution)/shard_map/merge_forward/pallas_call | solution.py:389
  26.8 1.7 %collective-permute-start.5 = (bf16[96,384]{1,0:T(8,128)(2,1)S(1)}, bf16[96,384]{1,0:T(8,128)(2,1)S(1)}, u32[]{:S(2)}, u32[]{:S(2)}) collective-permute-start(bf16[96,384]{1,0:T(8,128)(2,1)S(1)} %get-tuple-element.52), channel_id=1, source_target_pairs={{0,8},{8,16},{16,24},{24,32},{32,40},{40,48},{48,56},{56,64},{64,7... | collective-permute-start | bytes 221192 | tf_op jit(solution)/shard_map/ppermute | solution.py:800
  28.6 1.2 %collective-permute-start.4 = (bf16[192,384]{1,0:T(8,128)(2,1)S(1)}, bf16[192,384]{1,0:T(8,128)(2,1)S(1)}, u32[]{:S(2)}, u32[]{:S(2)}) collective-permute-start(bf16[192,384]{1,0:T(8,128)(2,1)S(1)} %get-tuple-element.51.both_ref), channel_id=1, source_target_pairs={{0,8},{8,0},{16,24},{24,16},{32,40},{40,32},{48,56},{56,48},{64,72... | collective-permute-start | bytes 442376 | tf_op jit(solution)/shard_map/ppermute | solution.py:814
  29.8 1.6 %coarse_bias_spread.1.bias_ref = f32[2,1728,128]{2,1,0:T(8,128)S(1)} custom-call(f32[12,23,2,144]{3,2,1,0:T(2,128)S(1)} %bitcast.12, bf16[12,384,256]{2,1,0:T(8,128)(2,1)S(1)} %copy-done.19, bf16[384,256]{1,0:T(8,128)(2,1)S(1)} %copy-done.23), custom_call_target="tpu_custom_call" | custom-call | flops 2000000000 | bytes 2000000 | tf_op jit(solution)/shard_map/coarse_bias_spread/pallas_call | solution.py:229
  31.5 2.1 %collective-permute-done.6.odd_ref = bf16[96,384]{1,0:T(8,128)(2,1)S(1)} collective-permute-done((bf16[96,384]{1,0:T(8,128)(2,1)S(1)}, bf16[96,384]{1,0:T(8,128)(2,1)S(1)}, u32[]{:S(2)}, u32[]{:S(2)}) %collective-permute-start.6) | collective-permute-done | bytes 73760 | tf_op jit(solution)/shard_map/ppermute | solution.py:800
  33.6 6.8 %coarse_both.1 = (bf16[192,384]{1,0:T(8,128)(2,1)S(1)}, bf16[192,384]{1,0:T(8,128)(2,1)S(1)}, bf16[96,384]{1,0:T(8,128)(2,1)S(1)}, bf16[96,384]{1,0:T(8,128)(2,1...) custom-call(bf16[192,384]{1,0:T(8,128)(2,1)S(1)} %get-tuple-element.51.both_ref, ...), custom_call_target="tpu_custom_call" | custom-call | flops 7000000000 | bytes 7000000 | tf_op jit(solution)/shard_map/coarse_both/pallas_call | solution.py:534
  40.4 2.9 %collective-permute-start.8 = (bf16[192,384]{1,0:T(8,128)(2,1)S(1)}, bf16[192,384]{1,0:T(8,128)(2,1)S(1)}, u32[]{:S(2)}, u32[]{:S(2)}) collective-permute-start(bf16[192,384]{1,0:T(8,128)(2,1)S(1)} %get-tuple-element.57), channel_id=1, source_target_pairs={{0,8},{8,0},{16,24},{24,16},{32,40},{40,32},{48,56},{56,48},{64,72... | collective-permute-start | bytes 442376 | tf_op jit(solution)/shard_map/ppermute | solution.py:814
  44.0 1.3 %coarse_rest.1 = (bf16[12,2,2304]{2,1,0:T(2,128)(2,1)S(1)}, bf16[12,2,2304]{2,1,0:T(2,128)(2,1)S(1)}, bf16[432,128]{1,0:T(8,128)(2,1)S(1)}) custom-call(bf16[144,384]{1,0:T(8,128)(2,1)S(1)} %get-tuple-element.53.out_ref, f32[2,1728,128]{2,1,0:T(8,128)S(1)} %get-tuple-element.54.ds_ref, bf16[12,384,256]{2,1,0:T(8,128)(2,1)S(1)} %copy-done.19), custom_call_target="tpu_custom_call" | custom-call | flops 1500000000 | bytes 1500000 | tf_op jit(solution)/shard_map/coarse_rest/pallas_call | solution.py:516
  45.3 2.0 %collective-permute-done.9.even_ref = bf16[96,384]{1,0:T(8,128)(2,1)S(1)} collective-permute-done((bf16[96,384]{1,0:T(8,128)(2,1)S(1)}, bf16[96,384]{1,0:T(8,128)(2,1)S(1)}, u32[]{:S(2)}, u32[]{:S(2)}) %collective-permute-start.9) | collective-permute-done | bytes 73760 | tf_op jit(solution)/shard_map/ppermute | solution.py:800
  47.3 1.1 %merge_backward.1 = (bf16[432,192]{1,0:T(8,128)(2,1)S(1)}, bf16[144,192]{1,0:T(8,128)(2,1)S(1)}, bf16[72,192]{1,0:T(8,128)(2,1)S(1)}) custom-call(bf16[432,128]{1,0:T(8,128)(2,1)S(1)} %get-tuple-element.55._.coarse_ref, bf16[192,384]{1,0:T(8,128)(2,1)S(1)} %get-tuple-element.56.g_ref, bf16[192,384]{1,0:T(8,128)(2,1)S(1)} %collective-permute-done.8.pg_ref, ...), custom_call_target="tpu_custom_call" | custom-call | flops 1000000000 | bytes 1000000 | tf_op jit(solution)/shard_map/merge_backward/pallas_call | solution.py:587
  48.5 2.5 %collective-permute-start.11 = (bf16[72,192]{1,0:T(8,128)(2,1)S(1)}, bf16[72,192]{1,0:T(8,128)(2,1)S(1)}, u32[]{:S(2)}, u32[]{:S(2)}) collective-permute-start(bf16[72,192]{1,0:T(8,128)(2,1)S(1)} %get-tuple-element.62), channel_id=1, source_target_pairs={{0,7},{1,0},{2,1},{3,2},{4,3},{5,4},{6,5},{7,6},{8,15},{9,8},{10,9... | collective-permute-start | bytes 82952 | tf_op jit(solution)/shard_map/ppermute | solution.py:800
  51.0 4.9 %fine_backward_3.1 = (bf16[2,18,2304]{2,1,0:T(8,128)(2,1)S(1)}, f32[216,256]{1,0:T(8,128)S(1)}) custom-call(bf16[432,192]{1,0:T(8,128)(2,1)S(1)} %get-tuple-element.63.refs_0_, bf16[3,432,192]{2,1,0:T(8,128)(2,1)S(1)} %get-tuple-element.64.refs_1_, bf16[2592,72]{1,0:T(8,128)(2,1)S(1)} %get-tuple-element.65.refs_2_, ...), custom_call_target="tpu_custom_call" | custom-call | flops 6000000000 | bytes 6000000 | tf_op jit(solution)/shard_map/fine_backward_3/pallas_call | solution.py:698
  55.9 2.3 %fine_backward_1.1 = (bf16[2,21,2304]{2,1,0:T(8,128)(2,1)S(1)}, bf16[2,3,2304]{2,1,0:T(4,128)(2,1)S(1)}, bf16[288,128]{1,0:T(8,128)(2,1)S(1)}, bf16[288,128]{1,0:T(8,128)(2,1)S(1)}) custom-call(bf16[144,192]{1,0:T(8,128)(2,1)S(1)} %get-tuple-element.61.refs_0_, bf16[72,192]{1,0:T(8,128)(2,1)S(1)} %collective-permute-done.11.refs_1_, ...), custom_call_target="tpu_custom_call" | custom-call | flops 2000000000 | bytes 2000000 | tf_op jit(solution)/shard_map/fine_backward_1/pallas_call | solution.py:698
  58.3 1.8 %collective-permute-start.12 = (bf16[288,128]{1,0:T(8,128)(2,1)S(1)}, bf16[288,128]{1,0:T(8,128)(2,1)S(1)}, u32[]{:S(2)}, u32[]{:S(2)}) collective-permute-start(bf16[288,128]{1,0:T(8,128)(2,1)S(1)} %get-tuple-element.77), channel_id=1, source_target_pairs={{0,8},{8,0},{16,24},{24,16},{32,40},{40,32},{48,56},{56,48},{64,72... | collective-permute-start | bytes 221192 | tf_op jit(solution)/shard_map/ppermute | solution.py:814
  61.8 3.6 %all-to-all-start = ((bf16[16,40,128]{2,1,0:T(8,128)(2,1)}), bf16[16,40,128]{2,1,0:T(8,128)(2,1)S(1)}, u32[]{:S(2)}, u32[]{:S(2)}) async-start(bf16[16,40,128]{2,1,0:T(8,128)(2,1)} %bitcast.4), calls=%async_computation | async-start | bytes 327680 | tf_op jit(solution)/shard_map/all_to_all | solution.py:871
  65.3 2.0 %collective-permute-start.13 = (bf16[2,3,2304]{2,1,0:T(4,128)(2,1)S(1)}, bf16[2,3,2304]{2,1,0:T(4,128)(2,1)S(1)}, u32[]{:S(2)}, u32[]{:S(2)}) collective-permute-start(bf16[2,3,2304]{2,1,0:T(4,128)(2,1)S(1)} %get-tuple-element.78), channel_id=1, source_target_pairs={{0,1},{1,2},{2,3},{3,4},{4,5},{5,6},{6,7},{7,0},{8,9},{9,10},{10,1... | collective-permute-start | bytes 82952 | tf_op jit(solution)/shard_map/ppermute | solution.py:800
  67.4 4.7 %collective-permute-done.13._ = bf16[2,3,2304]{2,1,0:T(4,128)(2,1)S(1)} collective-permute-done((bf16[2,3,2304]{2,1,0:T(4,128)(2,1)S(1)}, bf16[2,3,2304]{2,1,0:T(4,128)(2,1)S(1)}, u32[]{:S(2)}, u32[]{:S(2)}) %collective-permute-start.13) | collective-permute-done | bytes 27680 | tf_op jit(solution)/shard_map/ppermute | solution.py:800
  73.5 6.5 %all-to-all-start.1 = ((bf16[16,40,128]{2,1,0:T(8,128)(2,1)}), bf16[16,40,128]{2,1,0:T(8,128)(2,1)S(1)}, u32[]{:S(2)}, u32[]{:S(2)}) async-start(bf16[16,40,128]{2,1,0:T(8,128)(2,1)} %chip_sums.1), calls=%async_computation.1 | async-start | bytes 327680 | tf_op jit(solution)/shard_map/all_to_all | solution.py:872
  80.0 2.4 %collective-permute-start.15 = (bf16[12,2,2304]{2,1,0:T(2,128)(2,1)S(1)}, bf16[12,2,2304]{2,1,0:T(2,128)(2,1)S(1)}, u32[]{:S(2)}, u32[]{:S(2)}) collective-permute-start(bf16[12,2,2304]{2,1,0:T(2,128)(2,1)S(1)} %get-tuple-element.80), channel_id=1, source_target_pairs={{0,8},{8,0},{16,24},{24,16},{32,40},{40,32},{48,56},{56,48},{64,72... | collective-permute-start | bytes 331784 | tf_op jit(solution)/shard_map/ppermute | solution.py:814
  82.5 1.5 %collective-permute-start.16 = (bf16[2,24,1152]{2,1,0:T(8,128)(2,1)S(1)}, bf16[2,24,1152]{2,1,0:T(8,128)(2,1)S(1)}, u32[]{:S(2)}, u32[]{:S(2)}) collective-permute-start(bf16[2,24,1152]{2,1,0:T(8,128)(2,1)S(1)} %fusion), channel_id=1, source_target_pairs={{0,8},{8,16},{16,24},{24,32},{32,40},{40,48},{48,56},{56,64},{64,7... | collective-permute-start | bytes 331784 | tf_op jit(solution)/shard_map/ppermute | solution.py:800
  84.0 3.6 %all-to-all-done.1 = bf16[16,40,128]{2,1,0:T(8,128)(2,1)S(1)} async-done(((bf16[16,40,128]{2,1,0:T(8,128)(2,1)}), bf16[16,40,128]{2,1,0:T(8,128)(2,1)S(1)}, u32[]{:S(2)}, u32[]{:S(2)}) %all-to-all-start.1) | async-done | bytes 163872 | tf_op jit(solution)/shard_map/all_to_all | solution.py:872
  87.6 3.7 %collective-permute-start.14 = (bf16[640,128]{1,0:T(8,128)(2,1)S(1)}, bf16[640,128]{1,0:T(8,128)(2,1)S(1)}, u32[]{:S(2)}, u32[]{:S(2)}) collective-permute-start(bf16[640,128]{1,0:T(8,128)(2,1)S(1)} %bitcast.9), channel_id=1, source_target_pairs={{0,8},{8,0},{16,24},{24,16},{32,40},{40,32},{48,56},{56,48},{64,72... | collective-permute-start | bytes 491528 | tf_op jit(solution)/shard_map/ppermute | solution.py:814
  92.4 2.1 %results.1 = (bf16[12,2,2304]{2,1,0:T(2,128)(2,1)}, bf16[2,24,2304]{2,1,0:T(8,128)(2,1)}, f32[6,23,4,144]{3,2,1,0:T(4,128)}, f32[12,23,2,144]{3,2,1,0:T(2,128)}) custom-call(bf16[640,128]{1,0:T(8,128)(2,1)S(1)} %bitcast.10, bf16[640,128]{1,0:T(8,128)(2,1)S(1)} %collective-permute-done.14.got_ref, bf16[12,2,2304]{2,1,0:T(2,128)(2,1)S(1)} %get-tuple-element.79.okeep_ref, ...), custom_call_target="tpu_custom_call" | custom-call | flops 2000000000 | bytes 2000000 | tf_op jit(solution)/shard_map/results/pallas_call | solution.py:782
  (72 shorter events, 5.5 us)
Async XLA Ops:
  0.6 14.2 %copy-start.4 = (f32[4,6,23,144]{3,0,2,1:T(4,128)S(1)}, f32[4,6,23,144]{3,0,2,1:T(4,128)}, u32[]{:S(2)}) copy-start(f32[4,6,23,144]{3,0,2,1:T(4,128)} %param.31) | copy-start | bytes 953860
  0.6 30.8 %collective-permute-start.7 = (bf16[12,2,2304]{2,1,0:T(2,128)(2,1)}, bf16[12,2,2304]{2,1,0:T(2,128)(2,1)S(1)}, u32[]{:S(2)}, u32[]{:S(2)}) collective-permute-start(bf16[12,2,2304]{2,1,0:T(2,128)(2,1)} %bitcast.17), channel_id=1, source_target_pairs={{0,8},{8,0},{16,24},{24,16},{32,40},{40,32},{48,56},{56,48},{64,72... | collective-permute-start | bytes 331784 | tf_op jit(solution)/shard_map/ppermute | solution.py:814
  4.9 11.6 %collective-permute-start.1 = (bf16[2,3,1152]{2,1,0:T(4,128)(2,1)S(1)}, bf16[2,3,1152]{2,1,0:T(4,128)(2,1)S(1)}, u32[]{:S(2)}, u32[]{:S(2)}) collective-permute-start(bf16[2,3,1152]{2,1,0:T(4,128)(2,1)S(1)} %get-tuple-element.47), channel_id=1, source_target_pairs={{0,7},{1,0},{2,1},{3,2},{4,3},{5,4},{6,5},{7,6},{8,15},{9,8},{10,9... | collective-permute-start | bytes 41480 | tf_op jit(solution)/shard_map/ppermute | solution.py:800
  8.4 8.2 %collective-permute-start.2 = (bf16[2,3,1152]{2,1,0:T(4,128)(2,1)S(1)}, bf16[2,3,1152]{2,1,0:T(4,128)(2,1)S(1)}, u32[]{:S(2)}, u32[]{:S(2)}) collective-permute-start(bf16[2,3,1152]{2,1,0:T(4,128)(2,1)S(1)} %get-tuple-element.48), channel_id=1, source_target_pairs={{0,255},{1,248},{2,249},{3,250},{4,251},{5,252},{6,253},{7,254},{8... | collective-permute-start | bytes 41480 | tf_op jit(solution)/shard_map/ppermute | solution.py:810
  8.7 7.9 %collective-permute-start = (bf16[2,24,1152]{2,1,0:T(8,128)(2,1)S(1)}, bf16[2,24,1152]{2,1,0:T(8,128)(2,1)S(1)}, u32[]{:S(2)}, u32[]{:S(2)}) collective-permute-start(bf16[2,24,1152]{2,1,0:T(8,128)(2,1)S(1)} %get-tuple-element.45), channel_id=1, source_target_pairs={{0,248},{8,0},{16,8},{24,16},{32,24},{40,32},{48,40},{56,48},{64,5... | collective-permute-start | bytes 331784 | tf_op jit(solution)/shard_map/ppermute | solution.py:800
  18.6 6.5 %copy-start.3 = (bf16[768,384]{1,0:T(8,128)(2,1)S(1)}, bf16[768,384]{1,0:T(8,128)(2,1)}, u32[]{:S(2)}) copy-start(bf16[768,384]{1,0:T(8,128)(2,1)} %w_ref.3) | copy-start | bytes 1769476
  18.7 6.5 %copy-start.14 = (f32[768]{0:T(1024)S(1)}, f32[768]{0:T(1024)}, u32[]{:S(2)}) copy-start(f32[768]{0:T(1024)} %gain_ref.3) | copy-start | bytes 9220
  18.7 6.5 %copy-start.20 = (bf16[768,648]{1,0:T(8,128)(2,1)S(1)}, bf16[768,648]{1,0:T(8,128)(2,1)}, u32[]{:S(2)}) copy-start(bf16[768,648]{1,0:T(8,128)(2,1)} %constant.14.clone.pick_ref) | copy-start | bytes 2985988
  18.7 6.5 %collective-permute-start.3 = (bf16[72,192]{1,0:T(8,128)(2,1)S(1)}, bf16[72,192]{1,0:T(8,128)(2,1)S(1)}, u32[]{:S(2)}, u32[]{:S(2)}) collective-permute-start(bf16[72,192]{1,0:T(8,128)(2,1)S(1)} %get-tuple-element.50), channel_id=1, source_target_pairs={{0,1},{1,2},{2,3},{3,4},{4,5},{5,6},{6,7},{7,0},{8,9},{9,10},{10,1... | collective-permute-start | bytes 82952 | tf_op jit(solution)/shard_map/ppermute | solution.py:800
  25.2 4.5 %copy-start.5 = (f32[2,12,23,144]{3,0,2,1:T(2,128)S(1)}, f32[2,12,23,144]{3,0,2,1:T(2,128)}, u32[]{:S(2)}) copy-start(f32[2,12,23,144]{3,0,2,1:T(2,128)} %param.40) | copy-start | bytes 953860
  25.2 4.5 %copy-start.19 = (bf16[12,384,256]{2,1,0:T(8,128)(2,1)S(1)}, bf16[12,384,256]{2,1,0:T(8,128)(2,1)}, u32[]{:S(2)}) copy-start(bf16[12,384,256]{2,1,0:T(8,128)(2,1)} %constant.12.clone.onehot_ref.ec_ref) | copy-start | bytes 7077892
  25.2 4.5 %copy-start.23 = (bf16[384,256]{1,0:T(8,128)(2,1)S(1)}, bf16[384,256]{1,0:T(8,128)(2,1)}, u32[]{:S(2)}) copy-start(bf16[384,256]{1,0:T(8,128)(2,1)} %constant.13.clone.tail_ref) | copy-start | bytes 589828
  26.7 6.8 %collective-permute-start.6 = (bf16[96,384]{1,0:T(8,128)(2,1)S(1)}, bf16[96,384]{1,0:T(8,128)(2,1)S(1)}, u32[]{:S(2)}, u32[]{:S(2)}) collective-permute-start(bf16[96,384]{1,0:T(8,128)(2,1)S(1)} %get-tuple-element.52), channel_id=1, source_target_pairs={{0,16},{8,24},{16,32},{24,40},{32,48},{40,56},{48,64},{56,72},{64,... | collective-permute-start | bytes 221192 | tf_op jit(solution)/shard_map/ppermute | solution.py:800
  26.8 6.7 %collective-permute-start.5 = (bf16[96,384]{1,0:T(8,128)(2,1)S(1)}, bf16[96,384]{1,0:T(8,128)(2,1)S(1)}, u32[]{:S(2)}, u32[]{:S(2)}) collective-permute-start(bf16[96,384]{1,0:T(8,128)(2,1)S(1)} %get-tuple-element.52), channel_id=1, source_target_pairs={{0,8},{8,16},{16,24},{24,32},{32,40},{40,48},{48,56},{56,64},{64,7... | collective-permute-start | bytes 221192 | tf_op jit(solution)/shard_map/ppermute | solution.py:800
  28.6 5.0 %collective-permute-start.4 = (bf16[192,384]{1,0:T(8,128)(2,1)S(1)}, bf16[192,384]{1,0:T(8,128)(2,1)S(1)}, u32[]{:S(2)}, u32[]{:S(2)}) collective-permute-start(bf16[192,384]{1,0:T(8,128)(2,1)S(1)} %get-tuple-element.51.both_ref), channel_id=1, source_target_pairs={{0,8},{8,0},{16,24},{24,16},{32,40},{40,32},{48,56},{56,48},{64,72... | collective-permute-start | bytes 442376 | tf_op jit(solution)/shard_map/ppermute | solution.py:814
  29.7 3.8 %copy-start = (bf16[384,1536]{1,0:T(8,128)(2,1)S(1)}, bf16[384,1536]{1,0:T(8,128)(2,1)}, u32[]{:S(2)}) copy-start(bf16[384,1536]{1,0:T(8,128)(2,1)} %we_ref.1) | copy-start | bytes 3538948
  29.7 3.8 %copy-start.1 = (bf16[1536,384]{1,0:T(8,128)(2,1)S(1)}, bf16[1536,384]{1,0:T(8,128)(2,1)}, u32[]{:S(2)}) copy-start(bf16[1536,384]{1,0:T(8,128)(2,1)} %wr_ref.1) | copy-start | bytes 3538948
  29.8 3.8 %copy-start.2 = (bf16[384,1152]{1,0:T(8,128)(2,1)S(1)}, bf16[384,1152]{1,0:T(8,128)(2,1)}, u32[]{:S(2)}) copy-start(bf16[384,1152]{1,0:T(8,128)(2,1)} %wa_ref.1) | copy-start | bytes 2654212
  29.8 3.8 %copy-start.6 = (bf16[384,384]{1,0:T(8,128)(2,1)S(1)}, bf16[384,384]{1,0:T(8,128)(2,1)}, u32[]{:S(2)}) copy-start(bf16[384,384]{1,0:T(8,128)(2,1)} %wp_ref.1) | copy-start | bytes 884740
  29.8 3.8 %copy-start.12 = (bf16[2,12,2304]{2,0,1:T(2,128)(2,1)S(1)}, bf16[2,12,2304]{2,0,1:T(2,128)(2,1)}, u32[]{:S(2)}) copy-start(bf16[2,12,2304]{2,0,1:T(2,128)(2,1)} %param.41) | copy-start | bytes 331780
  40.4 7.0 %collective-permute-start.8 = (bf16[192,384]{1,0:T(8,128)(2,1)S(1)}, bf16[192,384]{1,0:T(8,128)(2,1)S(1)}, u32[]{:S(2)}, u32[]{:S(2)}) collective-permute-start(bf16[192,384]{1,0:T(8,128)(2,1)S(1)} %get-tuple-element.57), channel_id=1, source_target_pairs={{0,8},{8,0},{16,24},{24,16},{32,40},{40,32},{48,56},{56,48},{64,72... | collective-permute-start | bytes 442376 | tf_op jit(solution)/shard_map/ppermute | solution.py:814
  43.2 4.1 %collective-permute-start.9 = (bf16[96,384]{1,0:T(8,128)(2,1)S(1)}, bf16[96,384]{1,0:T(8,128)(2,1)S(1)}, u32[]{:S(2)}, u32[]{:S(2)}) collective-permute-start(bf16[96,384]{1,0:T(8,128)(2,1)S(1)} %get-tuple-element.58), channel_id=1, source_target_pairs={{0,248},{8,0},{16,8},{24,16},{32,24},{40,32},{48,40},{56,48},{64,5... | collective-permute-start | bytes 221192 | tf_op jit(solution)/shard_map/ppermute | solution.py:800
  43.3 4.0 %collective-permute-start.10 = (bf16[96,384]{1,0:T(8,128)(2,1)S(1)}, bf16[96,384]{1,0:T(8,128)(2,1)S(1)}, u32[]{:S(2)}, u32[]{:S(2)}) collective-permute-start(bf16[96,384]{1,0:T(8,128)(2,1)S(1)} %get-tuple-element.59), channel_id=1, source_target_pairs={{0,240},{8,248},{16,0},{24,8},{32,16},{40,24},{48,32},{56,40},{64,... | collective-permute-start | bytes 221192 | tf_op jit(solution)/shard_map/ppermute | solution.py:800
  48.5 7.4 %collective-permute-start.11 = (bf16[72,192]{1,0:T(8,128)(2,1)S(1)}, bf16[72,192]{1,0:T(8,128)(2,1)S(1)}, u32[]{:S(2)}, u32[]{:S(2)}) collective-permute-start(bf16[72,192]{1,0:T(8,128)(2,1)S(1)} %get-tuple-element.62), channel_id=1, source_target_pairs={{0,7},{1,0},{2,1},{3,2},{4,3},{5,4},{6,5},{7,6},{8,15},{9,8},{10,9... | collective-permute-start | bytes 82952 | tf_op jit(solution)/shard_map/ppermute | solution.py:800
  51.0 4.9 %copy-start.24 = (bf16[144,72]{1,0:T(8,128)(2,1)S(1)}, bf16[144,72]{1,0:T(8,128)(2,1)}, u32[]{:S(2)}) copy-start(bf16[144,72]{1,0:T(8,128)(2,1)} %constant.17.clone.refs_2_) | copy-start | bytes 62212
  58.3 2.8 %collective-permute-start.12 = (bf16[288,128]{1,0:T(8,128)(2,1)S(1)}, bf16[288,128]{1,0:T(8,128)(2,1)S(1)}, u32[]{:S(2)}, u32[]{:S(2)}) collective-permute-start(bf16[288,128]{1,0:T(8,128)(2,1)S(1)} %get-tuple-element.77), channel_id=1, source_target_pairs={{0,8},{8,0},{16,24},{24,16},{32,40},{40,32},{48,56},{56,48},{64,72... | collective-permute-start | bytes 221192 | tf_op jit(solution)/shard_map/ppermute | solution.py:814
  61.8 11.0 %all-to-all-start = ((bf16[16,40,128]{2,1,0:T(8,128)(2,1)}), bf16[16,40,128]{2,1,0:T(8,128)(2,1)S(1)}, u32[]{:S(2)}, u32[]{:S(2)}) async-start(bf16[16,40,128]{2,1,0:T(8,128)(2,1)} %bitcast.4), calls=%async_computation | async-start | bytes 327680 | tf_op jit(solution)/shard_map/all_to_all | solution.py:871
  65.3 6.7 %collective-permute-start.13 = (bf16[2,3,2304]{2,1,0:T(4,128)(2,1)S(1)}, bf16[2,3,2304]{2,1,0:T(4,128)(2,1)S(1)}, u32[]{:S(2)}, u32[]{:S(2)}) collective-permute-start(bf16[2,3,2304]{2,1,0:T(4,128)(2,1)S(1)} %get-tuple-element.78), channel_id=1, source_target_pairs={{0,1},{1,2},{2,3},{3,4},{4,5},{5,6},{6,7},{7,0},{8,9},{9,10},{10,1... | collective-permute-start | bytes 82952 | tf_op jit(solution)/shard_map/ppermute | solution.py:800
  73.5 14.1 %all-to-all-start.1 = ((bf16[16,40,128]{2,1,0:T(8,128)(2,1)}), bf16[16,40,128]{2,1,0:T(8,128)(2,1)S(1)}, u32[]{:S(2)}, u32[]{:S(2)}) async-start(bf16[16,40,128]{2,1,0:T(8,128)(2,1)} %chip_sums.1), calls=%async_computation.1 | async-start | bytes 327680 | tf_op jit(solution)/shard_map/all_to_all | solution.py:872
  80.0 11.4 %collective-permute-start.15 = (bf16[12,2,2304]{2,1,0:T(2,128)(2,1)S(1)}, bf16[12,2,2304]{2,1,0:T(2,128)(2,1)S(1)}, u32[]{:S(2)}, u32[]{:S(2)}) collective-permute-start(bf16[12,2,2304]{2,1,0:T(2,128)(2,1)S(1)} %get-tuple-element.80), channel_id=1, source_target_pairs={{0,8},{8,0},{16,24},{24,16},{32,40},{40,32},{48,56},{56,48},{64,72... | collective-permute-start | bytes 331784 | tf_op jit(solution)/shard_map/ppermute | solution.py:814
  82.5 9.0 %collective-permute-start.16 = (bf16[2,24,1152]{2,1,0:T(8,128)(2,1)S(1)}, bf16[2,24,1152]{2,1,0:T(8,128)(2,1)S(1)}, u32[]{:S(2)}, u32[]{:S(2)}) collective-permute-start(bf16[2,24,1152]{2,1,0:T(8,128)(2,1)S(1)} %fusion), channel_id=1, source_target_pairs={{0,8},{8,16},{16,24},{24,32},{32,40},{40,48},{48,56},{56,64},{64,7... | collective-permute-start | bytes 331784 | tf_op jit(solution)/shard_map/ppermute | solution.py:800
  87.6 4.8 %collective-permute-start.14 = (bf16[640,128]{1,0:T(8,128)(2,1)S(1)}, bf16[640,128]{1,0:T(8,128)(2,1)S(1)}, u32[]{:S(2)}, u32[]{:S(2)}) collective-permute-start(bf16[640,128]{1,0:T(8,128)(2,1)S(1)} %bitcast.9), channel_id=1, source_target_pairs={{0,8},{8,0},{16,24},{24,16},{32,40},{40,32},{48,56},{56,48},{64,72... | collective-permute-start | bytes 491528 | tf_op jit(solution)/shard_map/ppermute | solution.py:814
  (12 other events, 27.7 us)

commit v5 on v4

--- a/solution.py
+++ b/solution.py
@@ -365,7 +365,7 @@
     )(*cells, wa, wp, g1, we, wr, g2, bias)
 
 
-def merge_kernel(y_ref, last_ref, strip_ref, pick_ref, gain_ref, w_ref, both_ref, right_ref, f_ref):
+def merge_kernel(y_ref, last_ref, strip_ref, pick_ref, gain_ref, w_ref, both_ref, upper_ref, lower_ref, f_ref):
     gain = gain_ref[...][None, :]
     cells = jnp.concatenate([y_ref[...], last_ref[...], strip_ref[...]], axis=0)
     f = nn(pick_ref[...], cells)
@@ -381,14 +381,20 @@
         part = nn(normed, w_ref[k * 192 : (k + 1) * 192, :])
         result = part if result is None else result + part
     both_ref[...] = result.astype(BF16)
-    right_ref[...] = result[96:].astype(BF16)
+    upper_ref[...] = result[96:144].astype(BF16)
+    lower_ref[...] = result[144:].astype(BF16)
 
 
 def merge_call(y, last, strip, pick, gain, weight):
     shape = jax.ShapeDtypeStruct
     return pl.pallas_call(
         merge_kernel,
-        out_shape=(shape((192, C2), BF16), shape((96, C2), BF16), shape((768, C1), BF16)),
+        out_shape=(
+            shape((192, C2), BF16),
+            shape((48, C2), BF16),
+            shape((48, C2), BF16),
+            shape((768, C1), BF16),
+        ),
         in_specs=vmem(6),
         compiler_params=pltpu.CompilerParams(vmem_limit_bytes=8 << 20),
         cost_estimate=cost(1.5),
@@ -397,14 +403,14 @@
 
 
 def window_places(par):
-    row = lax.broadcasted_iota(jnp.int32, (144, 576), 0)
+    row = lax.broadcasted_iota(jnp.int32, (144, 480), 0)
     z, a, c = row // 72, row // 12 % 6, row % 12
     group = c // 3
-    even = jnp.where(group == 0, 4, jnp.where(group == 1, 0, jnp.where(group == 2, 1, 2)))
-    odd = jnp.where(group == 0, 5, jnp.where(group == 1, 2, jnp.where(group == 2, 3, 0)))
+    even = jnp.where(group == 0, 8, jnp.where(group == 1, 0, jnp.where(group == 2, 2, 4)))
+    odd = jnp.where(group == 0, 9, jnp.where(group == 1, 5, jnp.where(group == 2, 7, 1)))
     source = jnp.where(par == 0, even, odd)
-    place = source * 96 + par * 48 + z * 18 + a * 3 + c % 3
-    return (place == lax.broadcasted_iota(jnp.int32, (144, 576), 1)).astype(F32).astype(BF16)
+    place = source * 48 + z * 18 + a * 3 + c % 3
+    return (place == lax.broadcasted_iota(jnp.int32, (144, 480), 1)).astype(F32).astype(BF16)
 
 
 def half_places(par):
@@ -485,8 +491,8 @@
     parted = tn(pick, grad_x.astype(BF16)).astype(BF16)
     gboth_ref[...] = parted[:192]
     gpboth_ref[...] = parted[192:384]
-    geven_ref[...] = parted[384:480]
-    godd_ref[...] = parted[480:]
+    geven_ref[...] = parted[384:432]
+    godd_ref[...] = parted[432:]
 
 
 def coarse_rest_kernel(out_ref, ds_ref, ec_ref, okeep_ref, osend_ref, dt_ref, cells_ref):
@@ -536,8 +542,8 @@
         out_shape=(
             shape((192, C2), BF16),
             shape((192, C2), BF16),
-            shape((96, C2), BF16),
-            shape((96, C2), BF16),
+            shape((48, C2), BF16),
+            shape((48, C2), BF16),
             shape((144, C2), BF16),
             shape((2, 1728, 128), F32),
         ),
@@ -565,8 +571,9 @@
     scale = lax.rsqrt(square * (1.0 / 768) + EPSILON)
     gain = gain_ref[...][None, :]
     both = g_ref[...].astype(F32) + pg_ref[...].astype(F32)
-    right = both[96:] + even_ref[...].astype(F32) + odd_ref[...].astype(F32)
-    g = jnp.concatenate([both[:96], right], axis=0).astype(BF16)
+    upper = both[96:144] + even_ref[...].astype(F32)
+    lower = both[144:] + odd_ref[...].astype(F32)
+    g = jnp.concatenate([both[:96], upper, lower], axis=0).astype(BF16)
     normed = [c * scale for c in centred]
     grads = []
     for k in range(4):
@@ -844,8 +851,8 @@
     )
     strip = shifted(strip, "lat", 1)
     y_most, *saved_most = fine_call(most, (tokens, cols), fine_weights, bias_fine)
-    both, right, quads = merge_call(y_most, y_last, strip, pick, merge_gain, merge_weight)
-    cells = (both, swapped(both), shifted(right, "lon", 1), shifted(right, "lon", 2))
+    both, upper, lower, quads = merge_call(y_most, y_last, strip, pick, merge_gain, merge_weight)
+    cells = (both, swapped(both), shifted(upper, "lon", 1), shifted(lower, "lon", 2))
     grad_both, grad_pboth, grad_even, grad_odd, out, grad_scores = coarse_call(
         cells, seeds, coarse_weights, bias_coarse
     )

time: 94.8 us -> 93.6 us (0.987)
  starting transfers between devices: 45.5 us -> 43.5 us
  waiting for transfers between devices: 16.5 us -> 17.5 us
    ppermute x10, starting transfers between devices: 19.8 us -> 18.4 us  [shifted(): lax.ppermute(value, axis, [(s, (s + steps) % count) for s in range(count)])]
  transfers between devices with their start and end apart: 19 -> 19, of which waited for: 8 -> 8; matrix products, arithmetic and copies ran while one was open for 0% -> 0% of each run, Pallas kernels for 17% -> 18%
where the time goes in v5:
time: 93.6 us; the launch traced here: 93.3 us
  starting transfers between devices  43.5 us (46%)
  Pallas kernels  30.1 us (32%)
  waiting for transfers between devices  17.5 us (19%)
  local copies, waits for them, and re-layouts  1.07 us (1%)
  between operations  1.07 us (1%)
    ppermute x10, starting transfers between devices, shifted(): lax.ppermute(value, axis, [(s, (s + steps) % count) for s in range(count)])  18.4 us
    ppermute x6, starting transfers between devices, swapped(): lax.ppermute(value, 'lon', [(s, s ^ 1) for s in range(lax.axis_size('lon'...  14.8 us
    ppermute x10, waiting for transfers between devices, shifted(): lax.ppermute(value, axis, [(s, (s + steps) % count) for s in range(count)])  11.1 us
    pallas_call x2, Pallas kernels, fine_back_call(): pl.pallas_call(functools.partial(fine_back_kernel, windows), out_shape=ou...  7.22 us
    pallas_call x1, Pallas kernels, coarse_call(): pl.pallas_call(coarse_kernel, out_shape=(shape((192, C2), BF16), shape((1...  6.69 us
    all_to_all x1, starting transfers between devices, shards(): lax.all_to_all(sum_call(partial, edge), 'lon', 0, 0, tiled=True, axis_ind...  6.43 us
    pallas_call x2, Pallas kernels, fine_call(): pl.pallas_call(functools.partial(fine_kernel, windows), out_shape=(shape(...  5.46 us
    all_to_all x1, waiting for transfers between devices, shards(): lax.all_to_all(sum_call(partial, edge), 'lon', 0, 0, tiled=True, axis_ind...  3.72 us
  transfers between devices with their start and end apart: 19, of which 8 were waited for; matrix products, arithmetic and copies ran while one was open for 0% of the time, Pallas kernels for 18%

profile of v5, /device:TPU:1, one launch (start us, length us, event | category | flops | bytes accessed | tf_op | source)
XLA Modules:
  0.0 93.3 jit_solution(12012694254870798380)
XLA Ops:
  0.6 3.3 %collective-permute-start.7 = (bf16[12,2,2304]{2,1,0:T(2,128)(2,1)}, bf16[12,2,2304]{2,1,0:T(2,128)(2,1)S(1)}, u32[]{:S(2)}, u32[]{:S(2)}) collective-permute-start(bf16[12,2,2304]{2,1,0:T(2,128)(2,1)} %bitcast.17), channel_id=1, source_target_pairs={{0,8},{8,0},{16,24},{24,16},{32,40},{40,32},{48,56},{56,48},{64,72... | collective-permute-start | bytes 331784 | tf_op jit(solution)/shard_map/ppermute | solution.py:821
  4.0 0.9 %copy-done.10 = bf16[2,24,2304]{2,1,0:T(8,128)(2,1)S(1)} copy-done((bf16[2,24,2304]{2,1,0:T(8,128)(2,1)S(1)}, bf16[2,24,2304]{2,1,0:T(8,128)(2,1)}, u32[]{:S(2)}) %copy-start.10) | copy-done | bytes 221208
  4.9 3.5 %collective-permute-start.1 = (bf16[2,3,1152]{2,1,0:T(4,128)(2,1)S(1)}, bf16[2,3,1152]{2,1,0:T(4,128)(2,1)S(1)}, u32[]{:S(2)}, u32[]{:S(2)}) collective-permute-start(bf16[2,3,1152]{2,1,0:T(4,128)(2,1)S(1)} %get-tuple-element.48), channel_id=1, source_target_pairs={{0,7},{1,0},{2,1},{3,2},{4,3},{5,4},{6,5},{7,6},{8,15},{9,8},{10,9... | collective-permute-start | bytes 41480 | tf_op jit(solution)/shard_map/ppermute | solution.py:807
  8.7 6.2 %collective-permute-start = (bf16[2,24,1152]{2,1,0:T(8,128)(2,1)S(1)}, bf16[2,24,1152]{2,1,0:T(8,128)(2,1)S(1)}, u32[]{:S(2)}, u32[]{:S(2)}) collective-permute-start(bf16[2,24,1152]{2,1,0:T(8,128)(2,1)S(1)} %get-tuple-element.46), channel_id=1, source_target_pairs={{0,248},{8,0},{16,8},{24,16},{32,24},{40,32},{48,40},{56,48},{64,5... | collective-permute-start | bytes 331784 | tf_op jit(solution)/shard_map/ppermute | solution.py:807
  14.9 1.6 %fine_bias_spread.1.refs_8_.refs_10_ = f32[3456,128]{1,0:T(8,128)S(1)} custom-call(f32[6,23,4,144]{3,2,1,0:T(4,128)S(1)} %bitcast.11), custom_call_target="tpu_custom_call" | custom-call | flops 2000000000 | bytes 2000000 | tf_op jit(solution)/shard_map/fine_bias_spread/pallas_call | solution.py:182
  16.6 2.0 %fine_forward_1.1 = (bf16[144,192]{1,0:T(8,128)(2,1)S(1)}, bf16[72,192]{1,0:T(8,128)(2,1)S(1)}, bf16[3,144,192]{2,1,0:T(8,128)(2,1)S(1)}, bf16[864,72]{1,0:T(8,1...) custom-call(bf16[2,24,2304]{2,1,0:T(8,128)(2,1)S(1)} %copy-done.11, ...), custom_call_target="tpu_custom_call" | custom-call | flops 1500000000 | bytes 1500000 | tf_op jit(solution)/shard_map/fine_forward_1/pallas_call | solution.py:342
  18.7 1.5 %collective-permute-start.3 = (bf16[72,192]{1,0:T(8,128)(2,1)S(1)}, bf16[72,192]{1,0:T(8,128)(2,1)S(1)}, u32[]{:S(2)}, u32[]{:S(2)}) collective-permute-start(bf16[72,192]{1,0:T(8,128)(2,1)S(1)} %get-tuple-element.51), channel_id=1, source_target_pairs={{0,1},{1,2},{2,3},{3,4},{4,5},{5,6},{6,7},{7,0},{8,9},{9,10},{10,1... | collective-permute-start | bytes 82952 | tf_op jit(solution)/shard_map/ppermute | solution.py:807
  20.2 3.5 %fine_forward_3.1 = (bf16[432,192]{1,0:T(8,128)(2,1)S(1)}, bf16[3,432,192]{2,1,0:T(8,128)(2,1)S(1)}, bf16[2592,72]{1,0:T(8,128)(2,1)S(1)}, f32[432,192]{1,0:T(8,...) custom-call(bf16[2,24,2304]{2,1,0:T(8,128)(2,1)S(1)} %copy-done.11, ...), custom_call_target="tpu_custom_call" | custom-call | flops 3500000000 | bytes 3500000 | tf_op jit(solution)/shard_map/fine_forward_3/pallas_call | solution.py:342
  23.6 1.5 %collective-permute-done.3.strip_ref = bf16[72,192]{1,0:T(8,128)(2,1)S(1)} collective-permute-done((bf16[72,192]{1,0:T(8,128)(2,1)S(1)}, bf16[72,192]{1,0:T(8,128)(2,1)S(1)}, u32[]{:S(2)}, u32[]{:S(2)}) %collective-permute-start.3) | collective-permute-done | bytes 27680 | tf_op jit(solution)/shard_map/ppermute | solution.py:807
  25.2 1.5 %merge_forward.1 = (bf16[192,384]{1,0:T(8,128)(2,1)S(1)}, bf16[48,384]{1,0:T(8,128)(2,1)S(1)}, bf16[48,384]{1,0:T(8,128)(2,1)S(1)}, bf16[768,192]{1,0:T(8,128)(2,1)S(1)}) custom-call(bf16[432,192]{1,0:T(8,128)(2,1)S(1)} %get-tuple-element.47.y_ref, bf16[144,192]{1,0:T(8,128)(2,1)S(1)} %get-tuple-element.50.last_ref, ...), custom_call_target="tpu_custom_call" | custom-call | flops 1500000000 | bytes 1500000 | tf_op jit(solution)/shard_map/merge_forward/pallas_call | solution.py:390
  26.8 1.4 %collective-permute-start.6 = (bf16[48,384]{1,0:T(8,128)(2,1)S(1)}, bf16[48,384]{1,0:T(8,128)(2,1)S(1)}, u32[]{:S(2)}, u32[]{:S(2)}) collective-permute-start(bf16[48,384]{1,0:T(8,128)(2,1)S(1)} %get-tuple-element.54), channel_id=1, source_target_pairs={{0,16},{8,24},{16,32},{24,40},{32,48},{40,56},{48,64},{56,72},{64,... | collective-permute-start | bytes 110600 | tf_op jit(solution)/shard_map/ppermute | solution.py:807
  28.3 1.4 %collective-permute-start.4 = (bf16[192,384]{1,0:T(8,128)(2,1)S(1)}, bf16[192,384]{1,0:T(8,128)(2,1)S(1)}, u32[]{:S(2)}, u32[]{:S(2)}) collective-permute-start(bf16[192,384]{1,0:T(8,128)(2,1)S(1)} %get-tuple-element.52.both_ref), channel_id=1, source_target_pairs={{0,8},{8,0},{16,24},{24,16},{32,40},{40,32},{48,56},{56,48},{64,72... | collective-permute-start | bytes 442376 | tf_op jit(solution)/shard_map/ppermute | solution.py:821
  29.8 1.6 %coarse_bias_spread.1.bias_ref = f32[2,1728,128]{2,1,0:T(8,128)S(1)} custom-call(f32[12,23,2,144]{3,2,1,0:T(2,128)S(1)} %bitcast.12, bf16[12,384,256]{2,1,0:T(8,128)(2,1)S(1)} %copy-done.19, bf16[384,256]{1,0:T(8,128)(2,1)S(1)} %copy-done.23), custom_call_target="tpu_custom_call" | custom-call | flops 2000000000 | bytes 2000000 | tf_op jit(solution)/shard_map/coarse_bias_spread/pallas_call | solution.py:229
  31.5 3.1 %collective-permute-done.6.odd_ref = bf16[48,384]{1,0:T(8,128)(2,1)S(1)} collective-permute-done((bf16[48,384]{1,0:T(8,128)(2,1)S(1)}, bf16[48,384]{1,0:T(8,128)(2,1)S(1)}, u32[]{:S(2)}, u32[]{:S(2)}) %collective-permute-start.6) | collective-permute-done | bytes 36896 | tf_op jit(solution)/shard_map/ppermute | solution.py:807
  34.6 6.7 %coarse_both.1 = (bf16[192,384]{1,0:T(8,128)(2,1)S(1)}, bf16[192,384]{1,0:T(8,128)(2,1)S(1)}, bf16[48,384]{1,0:T(8,128)(2,1)S(1)}, bf16[48,384]{1,0:T(8,128)(2,1...) custom-call(bf16[192,384]{1,0:T(8,128)(2,1)S(1)} %get-tuple-element.52.both_ref, ...), custom_call_target="tpu_custom_call" | custom-call | flops 7000000000 | bytes 7000000 | tf_op jit(solution)/shard_map/coarse_both/pallas_call | solution.py:540
  41.3 1.2 %collective-permute-start.8 = (bf16[192,384]{1,0:T(8,128)(2,1)S(1)}, bf16[192,384]{1,0:T(8,128)(2,1)S(1)}, u32[]{:S(2)}, u32[]{:S(2)}) collective-permute-start(bf16[192,384]{1,0:T(8,128)(2,1)S(1)} %get-tuple-element.59), channel_id=1, source_target_pairs={{0,8},{8,0},{16,24},{24,16},{32,40},{40,32},{48,56},{56,48},{64,72... | collective-permute-start | bytes 442376 | tf_op jit(solution)/shard_map/ppermute | solution.py:821
  43.5 1.3 %coarse_rest.1 = (bf16[12,2,2304]{2,1,0:T(2,128)(2,1)S(1)}, bf16[12,2,2304]{2,1,0:T(2,128)(2,1)S(1)}, bf16[432,128]{1,0:T(8,128)(2,1)S(1)}) custom-call(bf16[144,384]{1,0:T(8,128)(2,1)S(1)} %get-tuple-element.55.out_ref, f32[2,1728,128]{2,1,0:T(8,128)S(1)} %get-tuple-element.56.ds_ref, bf16[12,384,256]{2,1,0:T(8,128)(2,1)S(1)} %copy-done.19), custom_call_target="tpu_custom_call" | custom-call | flops 1500000000 | bytes 1500000 | tf_op jit(solution)/shard_map/coarse_rest/pallas_call | solution.py:522
  44.8 1.1 %collective-permute-done.9.even_ref = bf16[48,384]{1,0:T(8,128)(2,1)S(1)} collective-permute-done((bf16[48,384]{1,0:T(8,128)(2,1)S(1)}, bf16[48,384]{1,0:T(8,128)(2,1)S(1)}, u32[]{:S(2)}, u32[]{:S(2)}) %collective-permute-start.9) | collective-permute-done | bytes 36896 | tf_op jit(solution)/shard_map/ppermute | solution.py:807
  45.9 1.1 %merge_backward.1 = (bf16[432,192]{1,0:T(8,128)(2,1)S(1)}, bf16[144,192]{1,0:T(8,128)(2,1)S(1)}, bf16[72,192]{1,0:T(8,128)(2,1)S(1)}) custom-call(bf16[432,128]{1,0:T(8,128)(2,1)S(1)} %get-tuple-element.57._.coarse_ref, bf16[192,384]{1,0:T(8,128)(2,1)S(1)} %get-tuple-element.58.g_ref, bf16[192,384]{1,0:T(8,128)(2,1)S(1)} %collective-permute-done.8.pg_ref, ...), custom_call_target="tpu_custom_call" | custom-call | flops 1000000000 | bytes 1000000 | tf_op jit(solution)/shard_map/merge_backward/pallas_call | solution.py:594
  47.1 2.0 %collective-permute-start.11 = (bf16[72,192]{1,0:T(8,128)(2,1)S(1)}, bf16[72,192]{1,0:T(8,128)(2,1)S(1)}, u32[]{:S(2)}, u32[]{:S(2)}) collective-permute-start(bf16[72,192]{1,0:T(8,128)(2,1)S(1)} %get-tuple-element.64), channel_id=1, source_target_pairs={{0,7},{1,0},{2,1},{3,2},{4,3},{5,4},{6,5},{7,6},{8,15},{9,8},{10,9... | collective-permute-start | bytes 82952 | tf_op jit(solution)/shard_map/ppermute | solution.py:807
  49.0 4.9 %fine_backward_3.1 = (bf16[2,18,2304]{2,1,0:T(8,128)(2,1)S(1)}, f32[216,256]{1,0:T(8,128)S(1)}) custom-call(bf16[432,192]{1,0:T(8,128)(2,1)S(1)} %get-tuple-element.65.refs_0_, bf16[3,432,192]{2,1,0:T(8,128)(2,1)S(1)} %get-tuple-element.66.refs_1_, bf16[2592,72]{1,0:T(8,128)(2,1)S(1)} %get-tuple-element.67.refs_2_, ...), custom_call_target="tpu_custom_call" | custom-call | flops 6000000000 | bytes 6000000 | tf_op jit(solution)/shard_map/fine_backward_3/pallas_call | solution.py:705
  53.9 2.3 %fine_backward_1.1 = (bf16[2,21,2304]{2,1,0:T(8,128)(2,1)S(1)}, bf16[2,3,2304]{2,1,0:T(4,128)(2,1)S(1)}, bf16[288,128]{1,0:T(8,128)(2,1)S(1)}, bf16[288,128]{1,0:T(8,128)(2,1)S(1)}) custom-call(bf16[144,192]{1,0:T(8,128)(2,1)S(1)} %get-tuple-element.63.refs_0_, bf16[72,192]{1,0:T(8,128)(2,1)S(1)} %collective-permute-done.11.refs_1_, ...), custom_call_target="tpu_custom_call" | custom-call | flops 2000000000 | bytes 2000000 | tf_op jit(solution)/shard_map/fine_backward_1/pallas_call | solution.py:705
  56.3 3.0 %collective-permute-start.12 = (bf16[288,128]{1,0:T(8,128)(2,1)S(1)}, bf16[288,128]{1,0:T(8,128)(2,1)S(1)}, u32[]{:S(2)}, u32[]{:S(2)}) collective-permute-start(bf16[288,128]{1,0:T(8,128)(2,1)S(1)} %get-tuple-element.79), channel_id=1, source_target_pairs={{0,8},{8,0},{16,24},{24,16},{32,40},{40,32},{48,56},{56,48},{64,72... | collective-permute-start | bytes 221192 | tf_op jit(solution)/shard_map/ppermute | solution.py:821
  60.9 3.5 %all-to-all-start = ((bf16[16,40,128]{2,1,0:T(8,128)(2,1)}), bf16[16,40,128]{2,1,0:T(8,128)(2,1)S(1)}, u32[]{:S(2)}, u32[]{:S(2)}) async-start(bf16[16,40,128]{2,1,0:T(8,128)(2,1)} %bitcast.4), calls=%async_computation | async-start | bytes 327680 | tf_op jit(solution)/shard_map/all_to_all | solution.py:878
  64.4 1.3 %collective-permute-start.13 = (bf16[2,3,2304]{2,1,0:T(4,128)(2,1)S(1)}, bf16[2,3,2304]{2,1,0:T(4,128)(2,1)S(1)}, u32[]{:S(2)}, u32[]{:S(2)}) collective-permute-start(bf16[2,3,2304]{2,1,0:T(4,128)(2,1)S(1)} %get-tuple-element.80), channel_id=1, source_target_pairs={{0,1},{1,2},{2,3},{3,4},{4,5},{5,6},{6,7},{7,0},{8,9},{9,10},{10,1... | collective-permute-start | bytes 82952 | tf_op jit(solution)/shard_map/ppermute | solution.py:807
  65.8 5.4 %collective-permute-done.13._ = bf16[2,3,2304]{2,1,0:T(4,128)(2,1)S(1)} collective-permute-done((bf16[2,3,2304]{2,1,0:T(4,128)(2,1)S(1)}, bf16[2,3,2304]{2,1,0:T(4,128)(2,1)S(1)}, u32[]{:S(2)}, u32[]{:S(2)}) %collective-permute-start.13) | collective-permute-done | bytes 27680 | tf_op jit(solution)/shard_map/ppermute | solution.py:807
  72.6 6.4 %all-to-all-start.1 = ((bf16[16,40,128]{2,1,0:T(8,128)(2,1)}), bf16[16,40,128]{2,1,0:T(8,128)(2,1)S(1)}, u32[]{:S(2)}, u32[]{:S(2)}) async-start(bf16[16,40,128]{2,1,0:T(8,128)(2,1)} %chip_sums.1), calls=%async_computation.1 | async-start | bytes 327680 | tf_op jit(solution)/shard_map/all_to_all | solution.py:879
  79.1 2.1 %collective-permute-start.15 = (bf16[12,2,2304]{2,1,0:T(2,128)(2,1)S(1)}, bf16[12,2,2304]{2,1,0:T(2,128)(2,1)S(1)}, u32[]{:S(2)}, u32[]{:S(2)}) collective-permute-start(bf16[12,2,2304]{2,1,0:T(2,128)(2,1)S(1)} %get-tuple-element.82), channel_id=1, source_target_pairs={{0,8},{8,0},{16,24},{24,16},{32,40},{40,32},{48,56},{56,48},{64,72... | collective-permute-start | bytes 331784 | tf_op jit(solution)/shard_map/ppermute | solution.py:821
  81.3 1.5 %collective-permute-start.16 = (bf16[2,24,1152]{2,1,0:T(8,128)(2,1)S(1)}, bf16[2,24,1152]{2,1,0:T(8,128)(2,1)S(1)}, u32[]{:S(2)}, u32[]{:S(2)}) collective-permute-start(bf16[2,24,1152]{2,1,0:T(8,128)(2,1)S(1)} %fusion), channel_id=1, source_target_pairs={{0,8},{8,16},{16,24},{24,32},{32,40},{40,48},{48,56},{56,64},{64,7... | collective-permute-start | bytes 331784 | tf_op jit(solution)/shard_map/ppermute | solution.py:807
  82.8 3.7 %all-to-all-done.1 = bf16[16,40,128]{2,1,0:T(8,128)(2,1)S(1)} async-done(((bf16[16,40,128]{2,1,0:T(8,128)(2,1)}), bf16[16,40,128]{2,1,0:T(8,128)(2,1)S(1)}, u32[]{:S(2)}, u32[]{:S(2)}) %all-to-all-start.1) | async-done | bytes 163872 | tf_op jit(solution)/shard_map/all_to_all | solution.py:879
  86.5 3.7 %collective-permute-start.14 = (bf16[640,128]{1,0:T(8,128)(2,1)S(1)}, bf16[640,128]{1,0:T(8,128)(2,1)S(1)}, u32[]{:S(2)}, u32[]{:S(2)}) collective-permute-start(bf16[640,128]{1,0:T(8,128)(2,1)S(1)} %bitcast.9), channel_id=1, source_target_pairs={{0,8},{8,0},{16,24},{24,16},{32,40},{40,32},{48,56},{56,48},{64,72... | collective-permute-start | bytes 491528 | tf_op jit(solution)/shard_map/ppermute | solution.py:821
  91.2 2.1 %results.1 = (bf16[12,2,2304]{2,1,0:T(2,128)(2,1)}, bf16[2,24,2304]{2,1,0:T(8,128)(2,1)}, f32[6,23,4,144]{3,2,1,0:T(4,128)}, f32[12,23,2,144]{3,2,1,0:T(2,128)}) custom-call(bf16[640,128]{1,0:T(8,128)(2,1)S(1)} %bitcast.10, bf16[640,128]{1,0:T(8,128)(2,1)S(1)} %collective-permute-done.14.got_ref, bf16[12,2,2304]{2,1,0:T(2,128)(2,1)S(1)} %get-tuple-element.81.okeep_ref, ...), custom_call_target="tpu_custom_call" | custom-call | flops 2000000000 | bytes 2000000 | tf_op jit(solution)/shard_map/results/pallas_call | solution.py:789
  (72 shorter events, 5.7 us)
Async XLA Ops:
  0.6 14.2 %copy-start.4 = (f32[4,6,23,144]{3,0,2,1:T(4,128)S(1)}, f32[4,6,23,144]{3,0,2,1:T(4,128)}, u32[]{:S(2)}) copy-start(f32[4,6,23,144]{3,0,2,1:T(4,128)} %param.31) | copy-start | bytes 953860
  0.6 30.8 %collective-permute-start.7 = (bf16[12,2,2304]{2,1,0:T(2,128)(2,1)}, bf16[12,2,2304]{2,1,0:T(2,128)(2,1)S(1)}, u32[]{:S(2)}, u32[]{:S(2)}) collective-permute-start(bf16[12,2,2304]{2,1,0:T(2,128)(2,1)} %bitcast.17), channel_id=1, source_target_pairs={{0,8},{8,0},{16,24},{24,16},{32,40},{40,32},{48,56},{56,48},{64,72... | collective-permute-start | bytes 331784 | tf_op jit(solution)/shard_map/ppermute | solution.py:821
  4.9 11.6 %collective-permute-start.1 = (bf16[2,3,1152]{2,1,0:T(4,128)(2,1)S(1)}, bf16[2,3,1152]{2,1,0:T(4,128)(2,1)S(1)}, u32[]{:S(2)}, u32[]{:S(2)}) collective-permute-start(bf16[2,3,1152]{2,1,0:T(4,128)(2,1)S(1)} %get-tuple-element.48), channel_id=1, source_target_pairs={{0,7},{1,0},{2,1},{3,2},{4,3},{5,4},{6,5},{7,6},{8,15},{9,8},{10,9... | collective-permute-start | bytes 41480 | tf_op jit(solution)/shard_map/ppermute | solution.py:807
  8.4 8.2 %collective-permute-start.2 = (bf16[2,3,1152]{2,1,0:T(4,128)(2,1)S(1)}, bf16[2,3,1152]{2,1,0:T(4,128)(2,1)S(1)}, u32[]{:S(2)}, u32[]{:S(2)}) collective-permute-start(bf16[2,3,1152]{2,1,0:T(4,128)(2,1)S(1)} %get-tuple-element.49), channel_id=1, source_target_pairs={{0,255},{1,248},{2,249},{3,250},{4,251},{5,252},{6,253},{7,254},{8... | collective-permute-start | bytes 41480 | tf_op jit(solution)/shard_map/ppermute | solution.py:817
  8.7 7.9 %collective-permute-start = (bf16[2,24,1152]{2,1,0:T(8,128)(2,1)S(1)}, bf16[2,24,1152]{2,1,0:T(8,128)(2,1)S(1)}, u32[]{:S(2)}, u32[]{:S(2)}) collective-permute-start(bf16[2,24,1152]{2,1,0:T(8,128)(2,1)S(1)} %get-tuple-element.46), channel_id=1, source_target_pairs={{0,248},{8,0},{16,8},{24,16},{32,24},{40,32},{48,40},{56,48},{64,5... | collective-permute-start | bytes 331784 | tf_op jit(solution)/shard_map/ppermute | solution.py:807
  18.6 6.5 %copy-start.3 = (bf16[768,384]{1,0:T(8,128)(2,1)S(1)}, bf16[768,384]{1,0:T(8,128)(2,1)}, u32[]{:S(2)}) copy-start(bf16[768,384]{1,0:T(8,128)(2,1)} %w_ref.3) | copy-start | bytes 1769476
  18.7 6.5 %copy-start.14 = (f32[768]{0:T(1024)S(1)}, f32[768]{0:T(1024)}, u32[]{:S(2)}) copy-start(f32[768]{0:T(1024)} %gain_ref.3) | copy-start | bytes 9220
  18.7 6.5 %copy-start.20 = (bf16[768,648]{1,0:T(8,128)(2,1)S(1)}, bf16[768,648]{1,0:T(8,128)(2,1)}, u32[]{:S(2)}) copy-start(bf16[768,648]{1,0:T(8,128)(2,1)} %constant.14.clone.pick_ref) | copy-start | bytes 2985988
  18.7 6.5 %collective-permute-start.3 = (bf16[72,192]{1,0:T(8,128)(2,1)S(1)}, bf16[72,192]{1,0:T(8,128)(2,1)S(1)}, u32[]{:S(2)}, u32[]{:S(2)}) collective-permute-start(bf16[72,192]{1,0:T(8,128)(2,1)S(1)} %get-tuple-element.51), channel_id=1, source_target_pairs={{0,1},{1,2},{2,3},{3,4},{4,5},{5,6},{6,7},{7,0},{8,9},{9,10},{10,1... | collective-permute-start | bytes 82952 | tf_op jit(solution)/shard_map/ppermute | solution.py:807
  25.2 4.5 %copy-start.5 = (f32[2,12,23,144]{3,0,2,1:T(2,128)S(1)}, f32[2,12,23,144]{3,0,2,1:T(2,128)}, u32[]{:S(2)}) copy-start(f32[2,12,23,144]{3,0,2,1:T(2,128)} %param.40) | copy-start | bytes 953860
  26.7 4.7 %collective-permute-start.5 = (bf16[48,384]{1,0:T(8,128)(2,1)S(1)}, bf16[48,384]{1,0:T(8,128)(2,1)S(1)}, u32[]{:S(2)}, u32[]{:S(2)}) collective-permute-start(bf16[48,384]{1,0:T(8,128)(2,1)S(1)} %get-tuple-element.53), channel_id=1, source_target_pairs={{0,8},{8,16},{16,24},{24,32},{32,40},{40,48},{48,56},{56,64},{64,7... | collective-permute-start | bytes 110600 | tf_op jit(solution)/shard_map/ppermute | solution.py:807
  26.8 7.7 %collective-permute-start.6 = (bf16[48,384]{1,0:T(8,128)(2,1)S(1)}, bf16[48,384]{1,0:T(8,128)(2,1)S(1)}, u32[]{:S(2)}, u32[]{:S(2)}) collective-permute-start(bf16[48,384]{1,0:T(8,128)(2,1)S(1)} %get-tuple-element.54), channel_id=1, source_target_pairs={{0,16},{8,24},{16,32},{24,40},{32,48},{40,56},{48,64},{56,72},{64,... | collective-permute-start | bytes 110600 | tf_op jit(solution)/shard_map/ppermute | solution.py:807
  28.3 6.3 %collective-permute-start.4 = (bf16[192,384]{1,0:T(8,128)(2,1)S(1)}, bf16[192,384]{1,0:T(8,128)(2,1)S(1)}, u32[]{:S(2)}, u32[]{:S(2)}) collective-permute-start(bf16[192,384]{1,0:T(8,128)(2,1)S(1)} %get-tuple-element.52.both_ref), channel_id=1, source_target_pairs={{0,8},{8,0},{16,24},{24,16},{32,40},{40,32},{48,56},{56,48},{64,72... | collective-permute-start | bytes 442376 | tf_op jit(solution)/shard_map/ppermute | solution.py:821
  29.7 4.8 %copy-start = (bf16[384,1536]{1,0:T(8,128)(2,1)S(1)}, bf16[384,1536]{1,0:T(8,128)(2,1)}, u32[]{:S(2)}) copy-start(bf16[384,1536]{1,0:T(8,128)(2,1)} %we_ref.1) | copy-start | bytes 3538948
  29.7 4.8 %copy-start.1 = (bf16[1536,384]{1,0:T(8,128)(2,1)S(1)}, bf16[1536,384]{1,0:T(8,128)(2,1)}, u32[]{:S(2)}) copy-start(bf16[1536,384]{1,0:T(8,128)(2,1)} %wr_ref.1) | copy-start | bytes 3538948
  29.8 4.8 %copy-start.2 = (bf16[384,1152]{1,0:T(8,128)(2,1)S(1)}, bf16[384,1152]{1,0:T(8,128)(2,1)}, u32[]{:S(2)}) copy-start(bf16[384,1152]{1,0:T(8,128)(2,1)} %wa_ref.1) | copy-start | bytes 2654212
  29.8 4.8 %copy-start.6 = (bf16[384,384]{1,0:T(8,128)(2,1)S(1)}, bf16[384,384]{1,0:T(8,128)(2,1)}, u32[]{:S(2)}) copy-start(bf16[384,384]{1,0:T(8,128)(2,1)} %wp_ref.1) | copy-start | bytes 884740
  29.8 4.8 %copy-start.12 = (bf16[2,12,2304]{2,0,1:T(2,128)(2,1)S(1)}, bf16[2,12,2304]{2,0,1:T(2,128)(2,1)}, u32[]{:S(2)}) copy-start(bf16[2,12,2304]{2,0,1:T(2,128)(2,1)} %param.41) | copy-start | bytes 331780
  29.8 4.8 %copy-start.15 = (f32[384]{0:T(512)S(1)}, f32[384]{0:T(512)}, u32[]{:S(2)}) copy-start(f32[384]{0:T(512)} %g1_ref.1) | copy-start | bytes 4612
  29.8 4.8 %copy-start.16 = (f32[384]{0:T(512)S(1)}, f32[384]{0:T(512)}, u32[]{:S(2)}) copy-start(f32[384]{0:T(512)} %g2_ref.1) | copy-start | bytes 4612
  41.3 4.6 %collective-permute-start.8 = (bf16[192,384]{1,0:T(8,128)(2,1)S(1)}, bf16[192,384]{1,0:T(8,128)(2,1)S(1)}, u32[]{:S(2)}, u32[]{:S(2)}) collective-permute-start(bf16[192,384]{1,0:T(8,128)(2,1)S(1)} %get-tuple-element.59), channel_id=1, source_target_pairs={{0,8},{8,0},{16,24},{24,16},{32,40},{40,32},{48,56},{56,48},{64,72... | collective-permute-start | bytes 442376 | tf_op jit(solution)/shard_map/ppermute | solution.py:821
  42.5 3.4 %collective-permute-start.9 = (bf16[48,384]{1,0:T(8,128)(2,1)S(1)}, bf16[48,384]{1,0:T(8,128)(2,1)S(1)}, u32[]{:S(2)}, u32[]{:S(2)}) collective-permute-start(bf16[48,384]{1,0:T(8,128)(2,1)S(1)} %get-tuple-element.60), channel_id=1, source_target_pairs={{0,248},{8,0},{16,8},{24,16},{32,24},{40,32},{48,40},{56,48},{64,5... | collective-permute-start | bytes 110600 | tf_op jit(solution)/shard_map/ppermute | solution.py:807
  42.6 3.3 %collective-permute-start.10 = (bf16[48,384]{1,0:T(8,128)(2,1)S(1)}, bf16[48,384]{1,0:T(8,128)(2,1)S(1)}, u32[]{:S(2)}, u32[]{:S(2)}) collective-permute-start(bf16[48,384]{1,0:T(8,128)(2,1)S(1)} %get-tuple-element.61), channel_id=1, source_target_pairs={{0,240},{8,248},{16,0},{24,8},{32,16},{40,24},{48,32},{56,40},{64,... | collective-permute-start | bytes 110600 | tf_op jit(solution)/shard_map/ppermute | solution.py:807
  47.1 6.9 %collective-permute-start.11 = (bf16[72,192]{1,0:T(8,128)(2,1)S(1)}, bf16[72,192]{1,0:T(8,128)(2,1)S(1)}, u32[]{:S(2)}, u32[]{:S(2)}) collective-permute-start(bf16[72,192]{1,0:T(8,128)(2,1)S(1)} %get-tuple-element.64), channel_id=1, source_target_pairs={{0,7},{1,0},{2,1},{3,2},{4,3},{5,4},{6,5},{7,6},{8,15},{9,8},{10,9... | collective-permute-start | bytes 82952 | tf_op jit(solution)/shard_map/ppermute | solution.py:807
  49.0 4.9 %copy-start.24 = (bf16[144,72]{1,0:T(8,128)(2,1)S(1)}, bf16[144,72]{1,0:T(8,128)(2,1)}, u32[]{:S(2)}) copy-start(bf16[144,72]{1,0:T(8,128)(2,1)} %constant.17.clone.refs_2_) | copy-start | bytes 62212
  56.3 3.9 %collective-permute-start.12 = (bf16[288,128]{1,0:T(8,128)(2,1)S(1)}, bf16[288,128]{1,0:T(8,128)(2,1)S(1)}, u32[]{:S(2)}, u32[]{:S(2)}) collective-permute-start(bf16[288,128]{1,0:T(8,128)(2,1)S(1)} %get-tuple-element.79), channel_id=1, source_target_pairs={{0,8},{8,0},{16,24},{24,16},{32,40},{40,32},{48,56},{56,48},{64,72... | collective-permute-start | bytes 221192 | tf_op jit(solution)/shard_map/ppermute | solution.py:821
  60.9 11.0 %all-to-all-start = ((bf16[16,40,128]{2,1,0:T(8,128)(2,1)}), bf16[16,40,128]{2,1,0:T(8,128)(2,1)S(1)}, u32[]{:S(2)}, u32[]{:S(2)}) async-start(bf16[16,40,128]{2,1,0:T(8,128)(2,1)} %bitcast.4), calls=%async_computation | async-start | bytes 327680 | tf_op jit(solution)/shard_map/all_to_all | solution.py:878
  64.4 6.7 %collective-permute-start.13 = (bf16[2,3,2304]{2,1,0:T(4,128)(2,1)S(1)}, bf16[2,3,2304]{2,1,0:T(4,128)(2,1)S(1)}, u32[]{:S(2)}, u32[]{:S(2)}) collective-permute-start(bf16[2,3,2304]{2,1,0:T(4,128)(2,1)S(1)} %get-tuple-element.80), channel_id=1, source_target_pairs={{0,1},{1,2},{2,3},{3,4},{4,5},{5,6},{6,7},{7,0},{8,9},{9,10},{10,1... | collective-permute-start | bytes 82952 | tf_op jit(solution)/shard_map/ppermute | solution.py:807
  72.6 13.9 %all-to-all-start.1 = ((bf16[16,40,128]{2,1,0:T(8,128)(2,1)}), bf16[16,40,128]{2,1,0:T(8,128)(2,1)S(1)}, u32[]{:S(2)}, u32[]{:S(2)}) async-start(bf16[16,40,128]{2,1,0:T(8,128)(2,1)} %chip_sums.1), calls=%async_computation.1 | async-start | bytes 327680 | tf_op jit(solution)/shard_map/all_to_all | solution.py:879
  79.1 11.2 %collective-permute-start.15 = (bf16[12,2,2304]{2,1,0:T(2,128)(2,1)S(1)}, bf16[12,2,2304]{2,1,0:T(2,128)(2,1)S(1)}, u32[]{:S(2)}, u32[]{:S(2)}) collective-permute-start(bf16[12,2,2304]{2,1,0:T(2,128)(2,1)S(1)} %get-tuple-element.82), channel_id=1, source_target_pairs={{0,8},{8,0},{16,24},{24,16},{32,40},{40,32},{48,56},{56,48},{64,72... | collective-permute-start | bytes 331784 | tf_op jit(solution)/shard_map/ppermute | solution.py:821
  81.3 9.0 %collective-permute-start.16 = (bf16[2,24,1152]{2,1,0:T(8,128)(2,1)S(1)}, bf16[2,24,1152]{2,1,0:T(8,128)(2,1)S(1)}, u32[]{:S(2)}, u32[]{:S(2)}) collective-permute-start(bf16[2,24,1152]{2,1,0:T(8,128)(2,1)S(1)} %fusion), channel_id=1, source_target_pairs={{0,8},{8,16},{16,24},{24,32},{32,40},{40,48},{48,56},{56,64},{64,7... | collective-permute-start | bytes 331784 | tf_op jit(solution)/shard_map/ppermute | solution.py:807
  86.5 4.7 %collective-permute-start.14 = (bf16[640,128]{1,0:T(8,128)(2,1)S(1)}, bf16[640,128]{1,0:T(8,128)(2,1)S(1)}, u32[]{:S(2)}, u32[]{:S(2)}) collective-permute-start(bf16[640,128]{1,0:T(8,128)(2,1)S(1)} %bitcast.9), channel_id=1, source_target_pairs={{0,8},{8,0},{16,24},{24,16},{32,40},{40,32},{48,56},{56,48},{64,72... | collective-permute-start | bytes 491528 | tf_op jit(solution)/shard_map/ppermute | solution.py:821
  (12 other events, 27.7 us)
